TPU v7x, 256 devices: a whole 4x4x8 slice. The times are simulated.
256 devices in a mesh: frame: 16 (over z_lo, x, core), cam: 16 (over z_hi, y).
Axes of the slice: x: 4, y: 4, z: 8 (z_hi: 4, z_lo: 2; z = z_hi * 2 + z_lo), core: 2. Of those that a mesh axis runs over, the one named last changes fastest.
Arguments:
- view_maps: bfloat16 [32, 176, 2, 32, 256], P('frame', 'cam'), may hold values from -6 to 6
- conv_weight: bfloat16 [9, 256, 256], replicated, may hold values from -0.125 to 0.125
- join_weight: bfloat16 [16384, 256], P('cam'), may hold values from -0.1875 to 0.1875
- valid_cams: int32 [32, 176], P('frame'), may hold values from 0 to 1, as said below
- latent_grad: bfloat16 [32, 256], P('frame'), may hold values from -6 to 6
Outputs:
- latent: float32 [32, 256], P('frame')
- conv_grad: float32 [9, 256, 256], replicated
- join_grad: float32 [16384, 256], P(('cam', 'frame'))
Inputs may be any that keep to these rules, and one draw needn't show every extreme that they name: `valid_cams`: every frame has at least one usable camera; the last 6 cameras are padding and never usable.
All inputs are finite; a program needn't handle non-finite values.
Results may differ from a plain program's by a relative error of at most 0.007.
Values may be sent and summed in bfloat16 or wider, within the bound.
No kernel may reach another device: no remote copies, remote signals or barrier semaphores. Data moves between devices by JAX's collectives and lax.ppermute only.
A program may use at most 64 MiB of HBM per device.

v0:
```python
import jax
import jax.numpy as jnp
from jax import lax
from jax.sharding import PartitionSpec as P


def make_shifts(maps, rows_n, cols_n, chans):
    padded = jnp.pad(maps, ((0, 0), (0, 0), (1, 1), (1, 1), (0, 0)))
    return [
        padded[:, :, dy : dy + rows_n, dx : dx + cols_n, :].reshape(-1, chans)
        for dy in range(3)
        for dx in range(3)
    ]


def on_device(view_maps, conv_weight, join_weight, valid_cams, latent_grad):
    frames_here, cams_here, rows_n, cols_n, chans = view_maps.shape
    feat_len = rows_n * cols_n * chans
    shifted = make_shifts(view_maps, rows_n, cols_n, chans)
    preact = jnp.zeros((frames_here * cams_here * rows_n * cols_n, chans), jnp.float32)
    for k in range(9):
        preact = preact + jnp.dot(shifted[k], conv_weight[k], preferred_element_type=jnp.float32)
    sigma = jax.nn.sigmoid(preact)
    features = (preact * sigma).astype(jnp.bfloat16)
    features = features.reshape(frames_here, cams_here, feat_len)
    slopes = (sigma * (1.0 + preact * (1.0 - sigma))).reshape(frames_here, cams_here, feat_len)
    cam_count = jnp.sum(valid_cams.astype(jnp.float32), axis=1)
    local_valid = lax.dynamic_slice_in_dim(
        valid_cams, lax.axis_index("cam") * cams_here, cams_here, 1
    )
    mask_f = local_valid.astype(jnp.float32)
    mask_b = local_valid.astype(jnp.bfloat16)
    pooled = lax.psum_scatter(
        jnp.einsum("fc,fcp->pf", mask_b, features, preferred_element_type=jnp.float32),
        "cam",
        scatter_dimension=0,
        tiled=True,
    )
    joined = (pooled.T / cam_count[:, None]).astype(jnp.bfloat16)
    partial_latent = jnp.dot(joined, join_weight, preferred_element_type=jnp.float32)
    latent = lax.psum(partial_latent, "cam")
    joined_grad = jnp.einsum(
        "fl,sl->fs", latent_grad, join_weight, preferred_element_type=jnp.float32
    ).astype(jnp.bfloat16)
    weighting = mask_f / cam_count[:, None]
    scaled = (
        lax.all_gather(joined_grad, "cam", axis=1, tiled=True).astype(jnp.float32)[:, None, :]
        * weighting[:, :, None]
        * slopes
    )
    pre_grad = scaled.astype(jnp.bfloat16)
    pre_grad = pre_grad.reshape(-1, chans)
    taps = jnp.stack(
        [
            lax.dot_general(
                shifted[k], pre_grad, (((0,), (0,)), ((), ())), preferred_element_type=jnp.float32
            )
            for k in range(9)
        ]
    )
    join_grad = lax.psum_scatter(
        lax.dot_general(
            joined, latent_grad, (((0,), (0,)), ((), ())), preferred_element_type=jnp.float32
        ),
        "frame",
        scatter_dimension=0,
        tiled=True,
    )
    conv_grad = lax.psum(taps, ("frame", "cam"))
    return (latent, conv_grad, join_grad)


def solution(mesh):
    in_specs = (
        P("frame", "cam", None, None, None),
        P(),
        P("cam", None),
        P("frame", None),
        P("frame", None),
    )
    out_specs = (P("frame", None), P(), P(("cam", "frame"), None))
    return jax.shard_map(
        on_device, mesh=mesh, in_specs=in_specs, out_specs=out_specs, check_vma=False
    )
```

profile of v0, /device:TPU:1, one launch (start us, length us, event | category | flops | bytes accessed | tf_op | source)
XLA Modules:
  0.0 382.2 jit_solution(3491703459873663761)
XLA Ops:
  8.1 0.8 convert_reduce_fusion
  10.4 0.9 convolution_convert_fusion
  11.3 40.6 %all_gather.3 = bf16[2,16384]{1,0:T(2,128)(2,1)S(1)} all-gather(bf16[2,1024]{1,0:T(2,128)(2,1)S(1)} %convolution_convert_fusion), channel_id=1, replica_groups=mesh['frame'=16,'cam'=16] {'cam'}, dimensions={1}, use_global_device_ids=true | all-gather | bytes 69632 | tf_op jit(solution)/shard_map/all_gather | solution.py:47
  52.2 1.4 mul.38
  53.7 2.1 pad_slice_fusion
  59.4 1.0 copy-done.16
  60.4 1.7 multiply_convert_fusion
  62.9 5.0 %copy.14 = f32[16384,2]{1,0:T(8,128)} copy(f32[16384,2]{0,1:T(2,128)S(1)} %bitcast.134) | data formatting | bytes 262144
  68.0 1.0 copy-done.15
  69.2 1.1 fusion.8
  70.3 1.1 fusion.7
  71.5 1.1 fusion.6
  72.6 1.1 fusion.5
  73.7 1.1 fusion.4
  74.8 1.1 fusion.3
  75.9 1.1 fusion.2
  77.0 1.1 fusion.1
  78.2 1.1 fusion
  79.3 115.0 %reduce-scatter.7.cloned.1.call-done = f32[1024,2]{1,0:T(8,128)} async-done(((f32[16384,2]{1,0:T(8,128)}), f32[1024,2]{1,0:T(8,128)}) %reduce-scatter.7.cloned.1.call-update) | async-done | bytes 8208
  194.4 1.2 copy.15
  195.6 1.4 fusion.31
  197.3 34.4 %psum.14 = f32[2,256]{1,0:T(2,128)} all-reduce(f32[2,256]{1,0:T(2,128)S(1)} %fusion.32), channel_id=1, replica_groups=mesh['frame'=16,'cam'=16] {'cam'}, use_global_device_ids=true, to_apply=%region_2.3 | all-reduce | flops 512 | bytes 4096 | tf_op jit(solution)/shard_map/psum | solution.py:41
  231.7 139.9 %all-reduce.3.cloned.1.call-done = f32[9,256,256]{2,1,0:T(8,128)} async-done(((f32[9,256,256]{2,1,0:T(8,128)}), f32[9,256,256]{2,1,0:T(8,128)}) %all-reduce.3.cloned.1.call-update) | async-done | bytes 2359312 | tf_op jit(solution)/shard_map/psum | solution.py:69
  371.6 3.2 copy.29
  (65 shorter events, 6.7 us)
Async XLA Ops:
  8.0 2.4 copy-start
  8.0 186.4 %reduce-scatter.7.cloned.1.call-start = ((), (), s32[]{:S(2)}) async-start(), calls=%async_computation.4 | async-start | bytes 8912896
  52.2 1.4 copy-start.1
  53.7 2.2 copy-start.17
  55.7 1.3 copy-start.12
  55.8 1.4 copy-start.10
  55.8 1.7 copy-start.8
  55.8 2.5 copy-start.6
  55.8 2.8 copy-start.4
  55.8 3.2 copy-start.2
  55.8 3.6 copy-start.18
  59.0 1.4 copy-start.16
  67.9 1.1 copy-start.15
  67.9 1.3 copy-start.20
  67.9 303.6 %all-reduce.3.cloned.1.call-start = ((), (), s32[]{:S(2)}) async-start(), calls=%async_computation.2 | async-start | bytes 4718592 | tf_op jit(solution)/shard_map/psum | solution.py:69
  68.0 2.4 copy-start.13
  69.2 2.2 copy-start.11
  70.3 2.2 copy-start.9
  72.6 2.2 copy-start.7
  73.7 2.3 copy-start.5
  74.8 2.2 copy-start.3
  75.9 2.2 copy-start.19
  79.3 116.3 %copy-start.21 = (bf16[2,256]{1,0:T(2,128)(2,1)S(1)}, bf16[2,256]{1,0:T(2,128)(2,1)}, u32[]{:S(2)}) copy-start(bf16[2,256]{1,0:T(2,128)(2,1)} %param.9) | copy-start | bytes 3076
  79.3 292.3 %reduce-scatter.5.cloned.1.call-start = ((), (), s32[]{:S(2)}) async-start(), calls=%async_computation.3 | async-start | bytes 1114112 | tf_op jit(solution)/shard_map/reduce_scatter | solution.py:61
  (1 other events, 1.0 us)
Sparse Core Ops, SparseCore 0:
  68.1 126.2 reduce-scatter.6
  197.5 59.9 reduce-scatter.4
Sparse Core Ops, SparseCore 1:
  79.4 292.1 all-reduce.2
where the time goes:
time: 383 us; the launch traced here: 382 us
  waiting for transfers between devices  255 us (67%)
  blocking collectives  75 us (20%)
  matrix products  17.3 us (5%)
  local copies, waits for them, and re-layouts  16.4 us (4%)
  between operations  15.7 us (4%)
    psum x1, waiting for transfers between devices, on_device(): conv_grad = lax.psum(taps, ('frame', 'cam'))  140 us
    unnamed x4, waiting for transfers between devices  115 us
    all_gather x1, blocking collectives, on_device(): lax.all_gather(joined_grad, 'cam', axis=1, tiled=True).astype(jnp.float32)  40.6 us
    psum x1, blocking collectives, on_device(): latent = lax.psum(partial_latent, 'cam')  34.4 us
    unnamed x47, local copies, waits for them, and re-layouts  12.3 us
    dot_general x9, matrix products, on_device(): lax.dot_general(shifted[k], pre_grad, (((0,), (0,)), ((), ())), preferred...  10 us
  transfers between devices with their start and end apart: 3, of which 2 were waited for; matrix products, arithmetic and copies ran while one was open for 3% of the time, Pallas kernels for 0%

commit v1 on v0

v1 whole, which is shorter than its diff:
```python
import functools

import jax
import jax.numpy as jnp
from jax import lax
from jax.experimental import pallas as pl
from jax.experimental.pallas import tpu as pltpu
from jax.sharding import Mesh, PartitionSpec as P

BF = jnp.bfloat16
F32 = jnp.float32
CHIPS = ("zh", "y", "zl", "x")
SWAP = [(0, 1), (1, 0)]
N_CHIPS = 128
KDIM = 768

VM = pl.BlockSpec(memory_space=pltpu.VMEM)
SM = pl.BlockSpec(memory_space=pltpu.SMEM)


def params():
    return pltpu.CompilerParams(vmem_limit_bytes=48 * 1024 * 1024)


def dot(a, b):
    return jnp.dot(a, b, preferred_element_type=F32)


def joined_grad_kernel(grad_ref, join_ref, out_ref, rows):
    grad = grad_ref[...]
    for pos in range(4):
        part = lax.dot_general(
            grad, join_ref[256 * pos : 256 * pos + 256, :], (((1,), (1,)), ((), ())), preferred_element_type=F32
        )
        rows[pos : pos + 1, :] = part[0:1]
        rows[pos + 4 : pos + 5, :] = part[1:2]
    block = rows[...].astype(BF)
    out_ref[...] = jnp.broadcast_to(block[None], out_ref.shape)


def edge_masks(rows):
    column = lax.broadcasted_iota(jnp.int32, (rows, 256), 0) % 32
    return column != 0, column != 31


def forward_kernel(core_ref, weight_ref, maps_ref, conv_ref, pooled_ref, slope_ref, turned_ref):
    n = 11 * 32
    not_first, not_last = edge_masks(n)

    def frame(f, carry):
        at = f * 11
        top = maps_ref[pl.ds(at, 11), 0:32, :].reshape(n, 256)
        low = maps_ref[pl.ds(at, 11), 32:64, :].reshape(n, 256)
        for r in range(2):
            taps = [
                dot(top, conv_ref[(1 - r) * 3 + dx]) + dot(low, conv_ref[(2 - r) * 3 + dx])
                for dx in range(3)
            ]
            pre = taps[1]
            pre = pre + jnp.where(not_first, pltpu.roll(taps[0], 1, 0), 0.0)
            pre = pre + jnp.where(not_last, pltpu.roll(taps[2], n - 1, 0), 0.0)
            sigma = jax.nn.sigmoid(pre)
            feature = pre * sigma
            slope = sigma * (1.0 + pre * (1.0 - sigma))
            pooled = jnp.zeros((32, 256), F32)
            for c in range(11):
                weight = weight_ref[f, c]
                rows = slice(32 * c, 32 * c + 32)
                pooled = pooled + feature[rows] * weight
                slope_ref[at + c, 32 * r : 32 * r + 32, :] = slope[rows] * weight
            pooled_ref[f, 32 * r : 32 * r + 32, :] = pooled
        return carry

    lax.fori_loop(0, 2, frame, 0)

    core = core_ref[0]
    m = 22 * 32
    keep_first, keep_last = edge_masks(m)
    for r in range(2):
        rows = maps_ref[:, 32 * r : 32 * r + 32, :].reshape(m, 256).astype(F32)
        for dx in range(3):
            if dx == 0:
                shifted = jnp.where(keep_first, pltpu.roll(rows, 1, 0), 0.0)
            elif dx == 1:
                shifted = rows
            else:
                shifted = jnp.where(keep_last, pltpu.roll(rows, m - 1, 0), 0.0)
            shifted = jnp.concatenate([shifted, jnp.zeros((KDIM - m, 256), F32)], 0)
            turned = shifted.T.astype(BF)
            for half in range(2):
                slot = core if half == 0 else 1 - core
                start = pl.multiple_of(slot * 384 + dx * 128, 128)
                turned_ref[r, pl.ds(start, 128), :] = turned[128 * half : 128 * half + 128]


def backward_kernel(grad_ref, slope_ref, turned_ref, mine_ref, send_ref, grads, acc):
    for k in range(16):
        block = grad_ref[k].astype(F32)
        for f in range(2):
            grads[f, 4 * k : 4 * k + 4, :] = block[4 * f : 4 * f + 4]
    pre = []
    for r in range(2):
        parts = []
        for f in range(2):
            rows = grads[f, 32 * r : 32 * r + 32, :]
            slope = slope_ref[11 * f : 11 * f + 11, 32 * r : 32 * r + 32, :]
            parts.append((slope * rows[None]).reshape(352, 256).astype(BF))
        parts.append(jnp.zeros((KDIM - 704, 256), BF))
        pre.append(jnp.concatenate(parts, 0))

    def put(dy, value):
        for slot, ref in enumerate((mine_ref, send_ref)):
            for dx in range(3):
                for h in range(2):
                    s = (dy * 3 + dx) * 2 + h
                    ref[128 * s : 128 * s + 128, :] = value[
                        slot * 384 + dx * 128 : slot * 384 + dx * 128 + 128, 128 * h : 128 * h + 128
                    ].astype(ref.dtype)

    put(0, dot(turned_ref[0], pre[1]))
    put(1, dot(turned_ref[0], pre[0]) + dot(turned_ref[1], pre[1]))
    put(2, dot(turned_ref[1], pre[0]))


def pack_kernel(mine_ref, got_ref, pooled_ref, grad_ref, out_ref, tail):
    total = mine_ref[...] + got_ref[...].astype(F32)
    out_ref[:, 0:16, :] = total[0:2048].reshape(128, 16, 128).astype(BF)
    grad = grad_ref[...].astype(F32)
    for h in range(2):
        lanes = slice(128 * h, 128 * h + 128)
        tail[pl.ds(h, 128, stride=8), :] = total[2048 + 128 * h : 2176 + 128 * h]
        for j in range(2):
            tail[pl.ds(2 + j + 8 * h, 64, stride=16), :] = pooled_ref[j, :, lanes]
            tail[pl.ds(4 + 2 * j + h, 128, stride=8), :] = jnp.broadcast_to(grad[j : j + 1, lanes], (128, 128))
    out_ref[:, 16:24, :] = tail[...].reshape(128, 8, 128).astype(BF)


def reduce_kernel(got_ref, join_ref, out_ref, rest_ref, few):
    conv_a = jnp.sum(got_ref[:, 0:16, :].astype(F32), axis=0)
    tail = got_ref[:, 16:24, :].astype(F32)
    by_chip = jnp.sum(tail.reshape(16, 8, 8, 128), axis=0)
    few[...] = by_chip.reshape(64, 128)
    conv_b = jnp.sum(by_chip, axis=0)
    joined = [few[pl.ds(2 + j, 8, stride=8), :].astype(BF) for j in range(2)]
    few[...] = tail[0:8].reshape(64, 128)
    for j in range(2):
        rest_ref[j, :, 0:128] = joined[j]
        for h in range(2):
            rest_ref[j, :, 128 + 128 * h : 256 + 128 * h] = few[pl.ds(4 + 2 * j + h, 8, stride=8), :].astype(BF)
    few[...] = jnp.broadcast_to(conv_b[None], (8, 8, 128)).reshape(64, 128)
    for j in range(2):
        latent = dot(joined[j], join_ref[...])
        for h in range(2):
            few[pl.ds(2 + 2 * j + h, 8, stride=8), :] = latent[:, 128 * h : 128 * h + 128]
    out_ref[:, 0:16, :] = jnp.broadcast_to(conv_a.astype(BF)[None], (128, 16, 128))
    end = few[...].reshape(8, 8, 128).astype(BF)
    for k in range(16):
        out_ref[8 * k : 8 * k + 8, 16:24, :] = end


def spread_kernel(core_ref, own_ref, other_ref, conv_ref, latent_ref, tail):
    core = core_ref[0]
    for ref, half in ((own_ref, core), (other_ref, 1 - core)):
        start = pl.multiple_of(half * 128, 128)
        for s in range(16):
            slab = ref[8 * s : 8 * s + 8, 0:16, :].astype(F32).reshape(128, 128)
            lanes = slice(128 * (s % 2), 128 * (s % 2) + 128)
            conv_ref[s // 2, pl.ds(start, 128), lanes] = slab
        end = ref[:, 16:24, :].astype(F32)
        tail[...] = end.reshape(1024, 128)
        for h in range(2):
            conv_ref[8, pl.ds(start, 128), 128 * h : 128 * h + 128] = tail[pl.ds(h, 128, stride=8), :]
        if ref is own_ref:
            total = jnp.sum(end, axis=0)
            for j in range(2):
                for h in range(2):
                    row = 2 + 2 * j + h
                    latent_ref[j : j + 1, 128 * h : 128 * h + 128] = total[row : row + 1]


def shape(*dims, dtype=F32):
    return jax.ShapeDtypeStruct(dims, dtype)


def cost(flops, bytes_accessed):
    return pl.CostEstimate(flops=flops, bytes_accessed=bytes_accessed, transcendentals=0)


def on_device(view_maps, conv_weight, join_weight, valid_cams, latent_grad):
    core = lax.axis_index("c").astype(jnp.int32)
    cam = lax.axis_index(("zh", "y"))
    line = lax.axis_index(("zl", "x"))

    with jax.named_scope("joined_grad"):
        sent = pl.pallas_call(
            joined_grad_kernel,
            out_shape=shape(16, 8, 256, dtype=BF),
            in_specs=[VM, VM],
            out_specs=VM,
            scratch_shapes=[pltpu.VMEM((8, 256), F32)],
            compiler_params=params(),
            cost_estimate=cost(1 << 20, 600_000),
            name="joined_grad",
        )(latent_grad, join_weight)
        joined_grad = lax.all_to_all(sent, ("zh", "y"), 0, 0)

    with jax.named_scope("weights"):
        count = jnp.sum(valid_cams.astype(F32), axis=1)
        usable = lax.dynamic_slice_in_dim(valid_cams, cam * 11, 11, 1).astype(F32)
        weight = usable / count[:, None]
        join_rows = lax.dynamic_slice_in_dim(join_weight, line * 128, 128, 0)
        core_at = core.reshape(1)

    with jax.named_scope("forward"):
        pooled, slope, turned = pl.pallas_call(
            forward_kernel,
            out_shape=[shape(2, 64, 256), shape(22, 64, 256), shape(2, 768, KDIM, dtype=BF)],
            in_specs=[SM, SM, VM, VM],
            out_specs=[VM, VM, VM],
            compiler_params=params(),
            cost_estimate=cost(1_200_000_000, 6_000_000),
            name="forward",
        )(core_at, weight, view_maps.reshape(22, 64, 256), conv_weight)

    with jax.named_scope("backward"):
        mine, send = pl.pallas_call(
            backward_kernel,
            out_shape=[shape(2304, 128), shape(2304, 128, dtype=BF)],
            in_specs=[VM, VM, VM],
            out_specs=[VM, VM],
            scratch_shapes=[pltpu.VMEM((2, 64, 256), F32), pltpu.VMEM((8, 128), F32)],
            compiler_params=params(),
            cost_estimate=cost(1_200_000_000, 6_000_000),
            name="backward",
        )(joined_grad, slope, turned)

    with jax.named_scope("conv_scatter"):
        got = lax.ppermute(send, "c", SWAP)
        packed = pl.pallas_call(
            pack_kernel,
            out_shape=shape(N_CHIPS, 24, 128, dtype=BF),
            in_specs=[VM, VM, VM, VM],
            out_specs=VM,
            scratch_shapes=[pltpu.VMEM((1024, 128), F32)],
            compiler_params=params(),
            cost_estimate=cost(1_000_000, 3_000_000),
            name="pack",
        )(mine, got, pooled, latent_grad)
        blocks = lax.all_to_all(packed, CHIPS, 0, 0)

    with jax.named_scope("reduce"):
        summed, rest = pl.pallas_call(
            reduce_kernel,
            out_shape=[shape(N_CHIPS, 24, 128, dtype=BF), shape(2, 8, 384, dtype=BF)],
            in_specs=[VM, VM],
            out_specs=[VM, VM],
            scratch_shapes=[pltpu.VMEM((64, 128), F32)],
            compiler_params=params(),
            cost_estimate=cost(1_000_000, 3_000_000),
            name="reduce",
        )(blocks, join_rows)

    with jax.named_scope("conv_gather"):
        own = lax.all_to_all(summed, CHIPS, 0, 0)
        other = lax.ppermute(own, "c", SWAP)
        conv_grad, latent = pl.pallas_call(
            spread_kernel,
            out_shape=[shape(9, 256, 256), shape(2, 256)],
            in_specs=[SM, VM, VM],
            out_specs=[VM, VM],
            scratch_shapes=[pltpu.VMEM((1024, 128), F32)],
            compiler_params=params(),
            cost_estimate=cost(1_000_000, 4_000_000),
            name="spread",
        )(core_at, own, other)

    with jax.named_scope("join_grad"):
        rest_other = lax.ppermute(rest, "c", SWAP)
        both = jnp.concatenate([rest, rest_other], 0).reshape(32, 384)
        rows = lax.dynamic_slice_in_dim(both, core * 64, 64, 1)
        join_grad = lax.dot_general(rows, both[:, 128:], (((0,), (0,)), ((), ())), preferred_element_type=F32)
    return (latent, conv_grad, join_grad)


def solution(mesh):
    fine = Mesh(mesh.devices.reshape(2, 4, 2, 4, 4), ("zl", "x", "c", "zh", "y"))
    frame, cam = ("zl", "x", "c"), ("zh", "y")
    in_specs = (
        P(frame, cam, None, None, None),
        P(),
        P(cam, None),
        P(frame, None),
        P(frame, None),
    )
    out_specs = (P(frame, None), P(), P(cam + frame, None))
    return jax.shard_map(on_device, mesh=fine, in_specs=in_specs, out_specs=out_specs, check_vma=False)
```

time: 383 us -> 106 us (0.28)
  waiting for transfers between devices: 255 us -> 26.8 us
  blocking collectives: 75 us -> 30.4 us
  starting transfers between devices: 0.12 us -> 29.1 us
  matrix products: 17.3 us -> 0.88 us
  between operations: 15.7 us -> 0.71 us
  local copies, waits for them, and re-layouts: 16.4 us -> 7.41 us
  Pallas kernels: 0 us -> 8.57 us
    psum x1 -> x0, waiting for transfers between devices: 140 us -> none  [on_device(): conv_grad = lax.psum(taps, ('frame', 'cam'))]
    unnamed x4 -> x0, waiting for transfers between devices: 115 us -> none
    all_gather x1 -> x0, blocking collectives: 40.6 us -> none  [on_device(): lax.all_gather(joined_grad, 'cam', axis=1, tiled=True).astype(jnp.float32)]
    psum x1 -> x0, blocking collectives: 34.4 us -> none  [on_device(): latent = lax.psum(partial_latent, 'cam')]
    all_to_all x0 -> x1, blocking collectives: none -> 30.4 us  [on_device(): own = lax.all_to_all(summed, CHIPS, 0, 0)]
    all_to_all x0 -> x2, starting transfers between devices: none -> 23.7 us  [the longest x1 11.9 us: on_device(): blocks = lax.all_to_all(packed, CHIPS, 0, 0)]
    all_to_all x0 -> x2, waiting for transfers between devices: none -> 23.3 us  [the longest x1 22.4 us: on_device(): blocks = lax.all_to_all(packed, CHIPS, 0, 0)]
    dot_general x22 -> x1, matrix products: 17.3 us -> 0.88 us  [on_device(): lax.dot_general(rows, both[:, 128:], (((0,), (0,)), ((), ())), preferred_...]
  transfers between devices with their start and end apart: 3 -> 5, of which waited for: 2 -> 4; matrix products, arithmetic and copies ran while one was open for 3% -> 3% of each run, Pallas kernels for 0% -> 3%
where the time goes in v1:
time: 106 us; the launch traced here: 105 us
  blocking collectives  30.4 us (29%)
  starting transfers between devices  29.1 us (27%)
  waiting for transfers between devices  26.8 us (25%)
  Pallas kernels  8.57 us (8%)
  local copies, waits for them, and re-layouts  7.41 us (7%)
  other arithmetic  1.56 us (1%)
    all_to_all x1, blocking collectives, on_device(): own = lax.all_to_all(summed, CHIPS, 0, 0)  30.4 us
    all_to_all x1, waiting for transfers between devices, on_device(): blocks = lax.all_to_all(packed, CHIPS, 0, 0)  22.4 us
    all_to_all x1, starting transfers between devices, on_device(): blocks = lax.all_to_all(packed, CHIPS, 0, 0)  11.9 us
    all_to_all x1, starting transfers between devices, on_device(): joined_grad = lax.all_to_all(sent, ('zh', 'y'), 0, 0)  11.7 us
    unnamed x14, local copies, waits for them, and re-layouts  6.56 us
    ppermute x1, starting transfers between devices, on_device(): other = lax.ppermute(own, 'c', SWAP)  3.24 us
    pallas_call x1, Pallas kernels, on_device(): pl.pallas_call(forward_kernel, out_shape=[shape(2, 64, 256), shape(22, 64...  3.06 us
    ppermute x1, starting transfers between devices, on_device(): got = lax.ppermute(send, 'c', SWAP)  2.18 us
  transfers between devices with their start and end apart: 5, of which 4 were waited for; matrix products, arithmetic and copies ran while one was open for 3% of the time, Pallas kernels for 3%

profile of v1, /device:TPU:1, one launch (start us, length us, event | category | flops | bytes accessed | tf_op | source)
XLA Modules:
  0.0 105.5 jit_solution(431426629937388949)
XLA Ops:
  0.6 1.0 copy-done
  1.7 0.7 copy-done.1
  2.4 0.9 joined_grad.1
  3.2 11.7 %all-to-all-start = ((bf16[16,8,256]{2,1,0:T(8,128)(2,1)}), bf16[16,8,256]{2,1,0:T(8,128)(2,1)S(1)}, u32[]{:S(2)}, u32[]{:S(2)}) async-start(bf16[16,8,256]{2,1,0:T(8,128)(2,1)} %joined_grad.1), calls=%async_computation | async-start | bytes 131072 | tf_op jit(solution)/shard_map/joined_grad/all_to_all | solution.py:205
  15.0 0.8 convert_reduce_fusion
  15.8 0.8 convert_divide_fusion.weight_ref
  16.6 1.3 %copy-done.3 = bf16[9,256,256]{2,1,0:T(8,128)(2,1)S(1)} copy-done((bf16[9,256,256]{2,1,0:T(8,128)(2,1)S(1)}, bf16[9,256,256]{2,1,0:T(8,128)(2,1)}, u32[]{:S(2)}) %copy-start.3) | copy-done | bytes 1179672
  17.8 1.1 %copy-done.4 = bf16[2,11,2,32,256]{4,3,2,1,0:T(8,128)(2,1)S(1)} copy-done((bf16[2,11,2,32,256]{4,3,2,1,0:T(8,128)(2,1)S(1)}, bf16[2,11,2,32,256]{4,3,2,1,0:T(8,128)(2,1)}, u32[]{:S(2)}) %copy-start.4) | copy-done | bytes 720920
  19.0 3.1 %forward.1 = (f32[2,64,256]{2,1,0:T(8,128)S(1)}, f32[22,64,256]{2,1,0:T(8,128)S(1)}, bf16[2,768,768]{2,1,0:T(8,128)(2,1)S(1)}) custom-call(s32[1]{0:T(128)} %bitcast.core_ref, f32[2,11]{1,0:T(2,128)S(1)} %convert_divide_fusion.weight_ref, bf16[22,64,256]{2,1,0:T(8,128)(2,1)S(1)} %bitcast.4, bf16[9,256,256]{2,1,0:T(8,128)(2,1)S(1)} %copy-done.3), custom_call_target="tpu_custom_call" | custom-call | flops 1200000000 | bytes 6000000 | tf_op jit(solution)/shard_map/forward/forward/pallas_call | solution.py:215
  22.0 1.1 %copy-done.5 = f32[22,64,256]{2,1,0:T(8,128)} copy-done((f32[22,64,256]{2,1,0:T(8,128)}, f32[22,64,256]{2,1,0:T(8,128)S(1)}, u32[]{:S(2)}) %copy-start.5) | copy-done | bytes 1441816
  23.1 0.8 all-to-all-done.grad_ref
  24.0 1.4 %copy-done.6 = f32[22,64,256]{2,1,0:T(8,128)S(1)} copy-done((f32[22,64,256]{2,1,0:T(8,128)S(1)}, f32[22,64,256]{2,1,0:T(8,128)}, u32[]{:S(2)}) %copy-start.6) | copy-done | bytes 1441816
  25.3 1.4 %backward.1 = (f32[2304,128]{1,0:T(8,128)S(1)}, bf16[2304,128]{1,0:T(8,128)(2,1)S(1)}) custom-call(bf16[16,8,256]{2,1,0:T(8,128)(2,1)S(1)} %all-to-all-done.grad_ref, f32[22,64,256]{2,1,0:T(8,128)S(1)} %copy-done.6, bf16[2,768,768]{2,1,0:T(8,128)(2,1)S(1)} %get-tuple-element.13.turned_ref), custom_call_target="tpu_custom_call" | custom-call | flops 1200000000 | bytes 6000000 | tf_op jit(solution)/shard_map/backward/backward/pallas_call | solution.py:226
  26.7 2.2 %collective-permute-start = (bf16[2304,128]{1,0:T(8,128)(2,1)S(1)}, bf16[2304,128]{1,0:T(8,128)(2,1)S(1)}, u32[]{:S(2)}, u32[]{:S(2)}) collective-permute-start(bf16[2304,128]{1,0:T(8,128)(2,1)S(1)} %get-tuple-element.15), channel_id=1, source_target_pairs={{0,16},{16,0},{1,17},{17,1},{2,18},{18,2},{3,19},{19,3},{4,20},{20... | collective-permute-start | bytes 1769480 | tf_op jit(solution)/shard_map/conv_scatter/ppermute | solution.py:238
  28.9 1.6 %collective-permute-done.got_ref = bf16[2304,128]{1,0:T(8,128)(2,1)S(1)} collective-permute-done((bf16[2304,128]{1,0:T(8,128)(2,1)S(1)}, bf16[2304,128]{1,0:T(8,128)(2,1)S(1)}, u32[]{:S(2)}, u32[]{:S(2)}) %collective-permute-start) | collective-permute-done | bytes 589856 | tf_op jit(solution)/shard_map/conv_scatter/ppermute | solution.py:238
  30.5 1.3 %pack.1 = bf16[128,24,128]{2,1,0:T(8,128)(2,1)} custom-call(f32[2304,128]{1,0:T(8,128)S(1)} %get-tuple-element.14.mine_ref, bf16[2304,128]{1,0:T(8,128)(2,1)S(1)} %collective-permute-done.got_ref, f32[2,64,256]{2,1,0:T(8,128)S(1)} %get-tuple-element.16.pooled_ref, bf16[2,256]{1,0:T(2,128)(2,1)S(1)} %copy-done.2), custom_call_target="tpu_custom_call" | custom-call | flops 1000000 | bytes 3000000 | tf_op jit(solution)/shard_map/conv_scatter/pack/pallas_call | solution.py:239
  31.8 11.9 %all-to-all-start.1 = ((bf16[128,24,128]{2,1,0:T(8,128)(2,1)}), bf16[128,24,128]{2,1,0:T(8,128)(2,1)S(1)}, u32[]{:S(2)}, u32[]{:S(2)}) async-start(bf16[128,24,128]{2,1,0:T(8,128)(2,1)} %pack.1), calls=%async_computation.1 | async-start | bytes 1572864 | tf_op jit(solution)/shard_map/conv_scatter/all_to_all | solution.py:249
  43.8 0.8 constant_dynamic-slice_fusion.join_ref
  44.6 22.4 %all-to-all-done.1.got_ref = bf16[128,24,128]{2,1,0:T(8,128)(2,1)S(1)} async-done(((bf16[128,24,128]{2,1,0:T(8,128)(2,1)}), bf16[128,24,128]{2,1,0:T(8,128)(2,1)S(1)}, u32[]{:S(2)}, u32[]{:S(2)}) %all-to-all-start.1) | async-done | bytes 786464 | tf_op jit(solution)/shard_map/conv_scatter/all_to_all | solution.py:249
  67.3 30.4 %all_to_all.15.own_ref = bf16[128,24,128]{2,1,0:T(8,128)(2,1)S(1)} all-to-all(bf16[128,24,128]{2,1,0:T(8,128)(2,1)S(1)} %get-tuple-element.17), channel_id=1, replica_groups=mesh['zl'=2,'x'=4,'c'=2,'zh'=4,'y'=4] {'zh','y','zl','x'}, dimensions={0} | all-to-all | bytes 1572864 | tf_op jit(solution)/shard_map/conv_gather/all_to_all | solution.py:264
  97.7 3.2 %collective-permute-start.1 = (bf16[128,24,128]{2,1,0:T(8,128)(2,1)S(1)}, bf16[128,24,128]{2,1,0:T(8,128)(2,1)S(1)}, u32[]{:S(2)}, u32[]{:S(2)}) collective-permute-start(bf16[128,24,128]{2,1,0:T(8,128)(2,1)S(1)} %all_to_all.15.own_ref), channel_id=1, source_target_pairs={{0,16},{16,0},{1,17},{17,1},{2,18},{18,2},{3,19},{19,3},{4,20},{20... | collective-permute-start | bytes 2359304 | tf_op jit(solution)/shard_map/conv_gather/ppermute | solution.py:265
  101.0 1.9 %collective-permute-done.2 = bf16[2,8,384]{2,1,0:T(8,128)(2,1)S(1)} collective-permute-done((bf16[2,8,384]{2,1,0:T(8,128)(2,1)S(1)}, bf16[2,8,384]{2,1,0:T(8,128)(2,1)S(1)}, u32[]{:S(2)}, u32[]{:S(2)}) %collective-permute-start.2) | collective-permute-done | bytes 12320 | tf_op jit(solution)/shard_map/join_grad/ppermute | solution.py:278
  102.9 0.9 fusion
  103.8 1.7 %spread.1 = (f32[9,256,256]{2,1,0:T(8,128)}, f32[2,256]{1,0:T(2,128)}) custom-call(s32[1]{0:T(128)} %bitcast.core_ref, bf16[128,24,128]{2,1,0:T(8,128)(2,1)S(1)} %all_to_all.15.own_ref, bf16[128,24,128]{2,1,0:T(8,128)(2,1)S(1)} %collective-permute-done.1.other_ref), custom_call_target="tpu_custom_call" | custom-call | flops 1000000 | bytes 4000000 | tf_op jit(solution)/shard_map/conv_gather/spread/pallas_call | solution.py:266
  (12 shorter events, 0.3 us)
Async XLA Ops:
  0.6 1.0 copy-start
  1.7 0.7 copy-start.1
  3.2 20.7 %all-to-all-start = ((bf16[16,8,256]{2,1,0:T(8,128)(2,1)}), bf16[16,8,256]{2,1,0:T(8,128)(2,1)S(1)}, u32[]{:S(2)}, u32[]{:S(2)}) async-start(bf16[16,8,256]{2,1,0:T(8,128)(2,1)} %joined_grad.1), calls=%async_computation | async-start | bytes 131072 | tf_op jit(solution)/shard_map/joined_grad/all_to_all | solution.py:205
  16.6 1.3 %copy-start.3 = (bf16[9,256,256]{2,1,0:T(8,128)(2,1)S(1)}, bf16[9,256,256]{2,1,0:T(8,128)(2,1)}, u32[]{:S(2)}) copy-start(bf16[9,256,256]{2,1,0:T(8,128)(2,1)} %conv_ref.1) | copy-start | bytes 3538948
  17.8 1.1 %copy-start.4 = (bf16[2,11,2,32,256]{4,3,2,1,0:T(8,128)(2,1)S(1)}, bf16[2,11,2,32,256]{4,3,2,1,0:T(8,128)(2,1)}, u32[]{:S(2)}) copy-start(bf16[2,11,2,32,256]{4,3,2,1,0:T(8,128)(2,1)} %param.5) | copy-start | bytes 2162692
  22.0 1.1 %copy-start.5 = (f32[22,64,256]{2,1,0:T(8,128)}, f32[22,64,256]{2,1,0:T(8,128)S(1)}, u32[]{:S(2)}) copy-start(f32[22,64,256]{2,1,0:T(8,128)S(1)} %get-tuple-element.12.slope_ref) | copy-start | bytes 4325380
  24.0 1.4 %copy-start.6 = (f32[22,64,256]{2,1,0:T(8,128)S(1)}, f32[22,64,256]{2,1,0:T(8,128)}, u32[]{:S(2)}) copy-start(f32[22,64,256]{2,1,0:T(8,128)} %copy-done.5) | copy-start | bytes 4325380
  25.3 5.2 %copy-start.2 = (bf16[2,256]{1,0:T(2,128)(2,1)S(1)}, bf16[2,256]{1,0:T(2,128)(2,1)}, u32[]{:S(2)}) copy-start(bf16[2,256]{1,0:T(2,128)(2,1)} %grad_ref.3) | copy-start | bytes 3076
  26.7 3.8 %collective-permute-start = (bf16[2304,128]{1,0:T(8,128)(2,1)S(1)}, bf16[2304,128]{1,0:T(8,128)(2,1)S(1)}, u32[]{:S(2)}, u32[]{:S(2)}) collective-permute-start(bf16[2304,128]{1,0:T(8,128)(2,1)S(1)} %get-tuple-element.15), channel_id=1, source_target_pairs={{0,16},{16,0},{1,17},{17,1},{2,18},{18,2},{3,19},{19,3},{4,20},{20... | collective-permute-start | bytes 1769480 | tf_op jit(solution)/shard_map/conv_scatter/ppermute | solution.py:238
  31.8 35.3 %all-to-all-start.1 = ((bf16[128,24,128]{2,1,0:T(8,128)(2,1)}), bf16[128,24,128]{2,1,0:T(8,128)(2,1)S(1)}, u32[]{:S(2)}, u32[]{:S(2)}) async-start(bf16[128,24,128]{2,1,0:T(8,128)(2,1)} %pack.1), calls=%async_computation.1 | async-start | bytes 1572864 | tf_op jit(solution)/shard_map/conv_scatter/all_to_all | solution.py:249
  97.7 6.1 %collective-permute-start.1 = (bf16[128,24,128]{2,1,0:T(8,128)(2,1)S(1)}, bf16[128,24,128]{2,1,0:T(8,128)(2,1)S(1)}, u32[]{:S(2)}, u32[]{:S(2)}) collective-permute-start(bf16[128,24,128]{2,1,0:T(8,128)(2,1)S(1)} %all_to_all.15.own_ref), channel_id=1, source_target_pairs={{0,16},{16,0},{1,17},{17,1},{2,18},{18,2},{3,19},{19,3},{4,20},{20... | collective-permute-start | bytes 2359304 | tf_op jit(solution)/shard_map/conv_gather/ppermute | solution.py:265
  101.0 1.9 %collective-permute-start.2 = (bf16[2,8,384]{2,1,0:T(8,128)(2,1)S(1)}, bf16[2,8,384]{2,1,0:T(8,128)(2,1)S(1)}, u32[]{:S(2)}, u32[]{:S(2)}) collective-permute-start(bf16[2,8,384]{2,1,0:T(8,128)(2,1)S(1)} %get-tuple-element.20), channel_id=1, source_target_pairs={{0,16},{16,0},{1,17},{17,1},{2,18},{18,2},{3,19},{19,3},{4,20},{20... | collective-permute-start | bytes 36872 | tf_op jit(solution)/shard_map/join_grad/ppermute | solution.py:278

commit v2 on v1

v2 whole, which is shorter than its diff:
```python
import functools

import jax
import jax.numpy as jnp
from jax import lax
from jax.experimental import pallas as pl
from jax.experimental.pallas import tpu as pltpu
from jax.sharding import Mesh, PartitionSpec as P

BF = jnp.bfloat16
F32 = jnp.float32
SWAP = [(0, 1), (1, 0)]
KDIM = 768

VM = pl.BlockSpec(memory_space=pltpu.VMEM)
SM = pl.BlockSpec(memory_space=pltpu.SMEM)
HBM = pl.BlockSpec(memory_space=pltpu.HBM)


def params():
    return pltpu.CompilerParams(vmem_limit_bytes=48 * 1024 * 1024)


def dot(a, b):
    return jnp.dot(a, b, preferred_element_type=F32)


def edge_masks(rows):
    column = lax.broadcasted_iota(jnp.int32, (rows, 256), 0) % 32
    return column != 0, column != 31


def forward_kernel(
    place_ref, valid_hbm, grad_hbm, join_hbm, maps_hbm, conv_hbm,
    out_ref, slope_ref, turned_ref,
    valid_ref, grad_ref, join_ref, maps_ref, conv_ref, rows_ref, sems,
):
    loads = [
        pltpu.make_async_copy(source, target, sems.at[i])
        for i, (source, target) in enumerate(
            (
                (valid_hbm, valid_ref),
                (grad_hbm, grad_ref),
                (join_hbm, join_ref),
                (maps_hbm, maps_ref),
                (conv_hbm, conv_ref),
            )
        )
    ]
    for load in loads:
        load.start()
    core, cam = place_ref[0], place_ref[1]
    loads[0].wait()
    valid = valid_ref[...].astype(F32)
    count = jnp.sum(valid, axis=1, keepdims=True)
    lane = lax.broadcasted_iota(jnp.int32, (2, 176), 1)
    weight = [jnp.sum(jnp.where(lane == cam * 11 + c, valid, 0.0), axis=1, keepdims=True) / count for c in range(11)]
    n = 11 * 32
    not_first, not_last = edge_masks(n)

    loads[1].wait()
    loads[2].wait()
    grad = grad_ref[...]
    for pos in range(4):
        part = lax.dot_general(
            grad, join_ref[256 * pos : 256 * pos + 256, :], (((1,), (1,)), ((), ())), preferred_element_type=F32
        )
        for j in range(2):
            rows_ref[4 * j + pos : 4 * j + pos + 1, :] = part[j : j + 1]
    out_ref[:, 0:8, :] = jnp.broadcast_to(rows_ref[0:8, :].astype(BF)[None], (16, 8, 256))

    loads[3].wait()
    loads[4].wait()
    for f in range(2):
        at = f * 11
        top = maps_ref[at : at + 11, 0:32, :].reshape(n, 256)
        low = maps_ref[at : at + 11, 32:64, :].reshape(n, 256)
        for r in range(2):
            taps = [
                dot(top, conv_ref[(1 - r) * 3 + dx]) + dot(low, conv_ref[(2 - r) * 3 + dx])
                for dx in range(3)
            ]
            pre = taps[1]
            pre = pre + jnp.where(not_first, pltpu.roll(taps[0], 1, 0), 0.0)
            pre = pre + jnp.where(not_last, pltpu.roll(taps[2], n - 1, 0), 0.0)
            sigma = jax.nn.sigmoid(pre)
            feature = pre * sigma
            slope = sigma * (1.0 + pre * (1.0 - sigma))
            pooled = jnp.zeros((32, 256), F32)
            for c in range(11):
                scale = weight[c][f : f + 1]
                rows = slice(32 * c, 32 * c + 32)
                pooled = pooled + feature[rows] * scale
                slope_ref[at + c, 32 * r : 32 * r + 32, :] = slope[rows] * scale
            for k in range(8):
                start = 8 * (8 * r + k) + 4 * f
                rows_ref[start : start + 4, :] = pooled[4 * k : 4 * k + 4]
    out_ref[:, 8:16, :] = rows_ref[...].reshape(16, 8, 256).astype(BF)

    m = 22 * 32
    keep_first, keep_last = edge_masks(m)
    for r in range(2):
        rows = maps_ref[:, 32 * r : 32 * r + 32, :].reshape(m, 256).astype(F32)
        for dx in range(3):
            if dx == 0:
                shifted = jnp.where(keep_first, pltpu.roll(rows, 1, 0), 0.0)
            elif dx == 1:
                shifted = rows
            else:
                shifted = jnp.where(keep_last, pltpu.roll(rows, m - 1, 0), 0.0)
            shifted = jnp.concatenate([shifted, jnp.zeros((KDIM - m, 256), F32)], 0)
            turned = shifted.T.astype(BF)
            for half in range(2):
                slot = core if half == 0 else 1 - core
                start = pl.multiple_of(slot * 384 + dx * 128, 128)
                turned_ref[r, pl.ds(start, 128), :] = turned[128 * half : 128 * half + 128]


def backward_kernel(grad_ref, slope_ref, turned_ref, mine_ref, send_ref, grads):
    for k in range(16):
        block = grad_ref[k, 0:8, :].astype(F32)
        for f in range(2):
            grads[f, 4 * k : 4 * k + 4, :] = block[4 * f : 4 * f + 4]
    pre = []
    for r in range(2):
        parts = []
        for f in range(2):
            rows = grads[f, 32 * r : 32 * r + 32, :]
            slope = slope_ref[11 * f : 11 * f + 11, 32 * r : 32 * r + 32, :]
            parts.append((slope * rows[None]).reshape(352, 256).astype(BF))
        parts.append(jnp.zeros((KDIM - 704, 256), BF))
        pre.append(jnp.concatenate(parts, 0))

    def put(dy, value):
        for slot, ref in enumerate((mine_ref, send_ref)):
            for dx in range(3):
                for h in range(2):
                    s = (dy * 3 + dx) * 2 + h
                    ref[128 * s : 128 * s + 128, :] = value[
                        slot * 384 + dx * 128 : slot * 384 + dx * 128 + 128, 128 * h : 128 * h + 128
                    ].astype(ref.dtype)

    put(0, dot(turned_ref[0], pre[1]))
    put(1, dot(turned_ref[0], pre[0]) + dot(turned_ref[1], pre[1]))
    put(2, dot(turned_ref[1], pre[0]))


def join_kernel(got_ref, join_ref, joined_ref, latent_ref):
    pooled = jnp.sum(got_ref[:, 8:16, :].astype(F32), axis=0)
    joined = pooled.astype(BF)
    joined_ref[...] = joined.astype(F32)
    parts = [dot(joined, join_ref[256 * pos : 256 * pos + 256, :]) for pos in range(4)]
    for j in range(2):
        latent_ref[j : j + 1, :] = sum(parts[pos][4 * j + pos : 4 * j + pos + 1] for pos in range(4))


def pack_kernel(place_ref, mine_ref, got_ref, joined_ref, latent_ref, grad_ref, out_ref, tail):
    total = (mine_ref[...] + got_ref[...].astype(F32)).astype(BF)
    out_ref[:, 0:144, :] = total.reshape(16, 144, 128)
    grad = grad_ref[...].astype(F32)
    tail[...] = jnp.zeros((16, 128), F32)
    for j in range(2):
        for h in range(2):
            tail[5 + 2 * j + h : 6 + 2 * j + h, :] = grad[j : j + 1, 128 * h : 128 * h + 128]
    for x in range(4):
        own = jnp.where(place_ref[2] == x, 1.0, 0.0)
        for j in range(2):
            for z in range(2):
                t = 4 * z + x
                row = 4 * j + t // 2
                lanes = slice(128 * (t % 2), 128 * (t % 2) + 128)
                tail[1 + 2 * j + z : 2 + 2 * j + z, :] = joined_ref[row : row + 1, lanes]
        for y in range(4):
            tail[0:1, :] = latent_ref[y // 2 : y // 2 + 1, 128 * (y % 2) : 128 * (y % 2) + 128] * own
            out_ref[4 * x + y, 144:160, :] = tail[...].astype(BF)


def middle_kernel(place_ref, got_ref, out_ref, ends):
    own_y = place_ref[3]
    conv = jnp.sum(got_ref[:, 0:144, :].astype(F32), axis=0)
    end = jnp.sum(got_ref[:, 144:160, :].astype(F32), axis=0)
    ends[...] = jnp.zeros((2, 32, 128), F32)
    for x in range(4):
        block = got_ref[4 * x + own_y, 144:160, :].astype(F32)
        for z in range(2):
            for j in range(2):
                ends[z, 1 + 2 * x + j : 2 + 2 * x + j, :] = block[1 + 2 * j + z : 2 + 2 * j + z]
            ends[z, 9 + 4 * x : 13 + 4 * x, :] = block[5:9]
    for z in range(2):
        ends[z, 0:1, :] = end[0:1]
    conv = conv.astype(BF)
    for z in range(8):
        out_ref[z, 0:144, :] = conv
        out_ref[z, 144:176, :] = ends[z % 2].astype(BF)


def finish_kernel(place_ref, got_ref, out_ref, rest_ref, rows_ref):
    own_high, own_low = place_ref[4], place_ref[5]
    conv = jnp.sum(got_ref[:, 0:144, :].astype(F32), axis=0).astype(BF)
    latent = jnp.zeros((8, 128), F32)
    for z in range(4):
        latent = latent + got_ref[2 * z + own_low, 144:176, :].astype(F32)[0:8]
    latent = latent.astype(BF)
    for k in range(16):
        out_ref[k, 0:144, :] = conv
        out_ref[k, 144:152, :] = latent
    for z in range(2):
        block = got_ref[2 * own_high + z, 144:176, :].astype(F32)
        rows_ref[8 * z : 8 * z + 8, 0:128] = block[1:9]
        for x in range(4):
            for j in range(2):
                for h in range(2):
                    row = 9 + 4 * x + 2 * j + h
                    at = 8 * z + 2 * x + j
                    rows_ref[at : at + 1, 128 + 128 * h : 256 + 128 * h] = block[row : row + 1]
    rest_ref[...] = rows_ref[...].astype(BF)


def spread_kernel(place_ref, own_ref, other_ref, conv_ref, latent_ref):
    core, own_x = place_ref[0], place_ref[2]
    for ref, half in ((own_ref, core), (other_ref, 1 - core)):
        for g in range(144):
            s, i = g // 8, 16 * (g % 8)
            start = pl.multiple_of(half * 128 + i, 16)
            lanes = slice(128 * (s % 2), 128 * (s % 2) + 128)
            offset = 16 * (g % 9)
            conv_ref[s // 2, pl.ds(start, 16), lanes] = ref[g // 9, offset : offset + 16, :].astype(F32)
    for y in range(4):
        row = own_ref[4 * own_x + y, 144:152, :].astype(F32)[0:1]
        latent_ref[y // 2 : y // 2 + 1, 128 * (y % 2) : 128 * (y % 2) + 128] = row


def shape(*dims, dtype=F32):
    return jax.ShapeDtypeStruct(dims, dtype)


def call(kernel, name, out_shape, in_specs, scratch=(), flops=1_000_000, moved=3_000_000):
    return pl.pallas_call(
        kernel,
        out_shape=out_shape,
        in_specs=in_specs,
        out_specs=[VM] * len(out_shape),
        scratch_shapes=scratch,
        compiler_params=params(),
        cost_estimate=pl.CostEstimate(flops=flops, bytes_accessed=moved, transcendentals=0),
        name=name,
    )


def on_device(view_maps, conv_weight, join_weight, valid_cams, latent_grad):
    names = ("c", ("zh", "y"), "x", "y", "zh", "zl")
    place = jnp.stack([lax.axis_index(name).astype(jnp.int32) for name in names])

    with jax.named_scope("forward"):
        shares, slope, turned = call(
            forward_kernel,
            "forward",
            [shape(16, 16, 256, dtype=BF), shape(22, 64, 256), shape(2, 768, KDIM, dtype=BF)],
            [SM, HBM, HBM, HBM, HBM, HBM],
            [
                pltpu.VMEM((2, 176), jnp.int32),
                pltpu.VMEM((2, 256), BF),
                pltpu.VMEM((1024, 256), BF),
                pltpu.VMEM((22, 64, 256), BF),
                pltpu.VMEM((9, 256, 256), BF),
                pltpu.VMEM((128, 256), F32),
                pltpu.SemaphoreType.DMA((5,)),
            ],
            flops=1_200_000_000,
        )(place, valid_cams, latent_grad, join_weight, view_maps.reshape(22, 64, 256), conv_weight)
        cam_shares = lax.all_to_all(shares, ("zh", "y"), 0, 0)

    with jax.named_scope("backward"):
        mine, send = call(
            backward_kernel,
            "backward",
            [shape(2304, 128), shape(2304, 128, dtype=BF)],
            [VM, VM, VM],
            [pltpu.VMEM((2, 64, 256), F32)],
            flops=1_200_000_000,
        )(cam_shares, slope, turned)
        got = lax.ppermute(send, "c", SWAP)

    with jax.named_scope("join"):
        joined, latent_part = call(join_kernel, "join", [shape(8, 256), shape(2, 256)], [VM, VM])(
            cam_shares, join_weight
        )

    with jax.named_scope("conv_scatter"):
        (packed,) = call(
            pack_kernel,
            "pack",
            [shape(16, 160, 128, dtype=BF)],
            [SM, VM, VM, VM, VM, VM],
            [pltpu.VMEM((16, 128), F32)],
        )(place, mine, got, joined, latent_part, latent_grad)
        blocks = lax.all_to_all(packed, ("x", "y"), 0, 0)

    with jax.named_scope("conv_middle"):
        (middle,) = call(
            middle_kernel, "middle", [shape(8, 176, 128, dtype=BF)], [SM, VM], [pltpu.VMEM((2, 32, 128), F32)]
        )(place, blocks)
        lines = lax.all_to_all(middle, ("zh", "zl"), 0, 0)

    with jax.named_scope("conv_gather"):
        summed, rest = call(
            finish_kernel,
            "finish",
            [shape(16, 152, 128, dtype=BF), shape(16, 384, dtype=BF)],
            [SM, VM],
            [pltpu.VMEM((16, 384), F32)],
        )(place, lines)
        own = lax.all_to_all(summed, ("x", "y"), 0, 0)
        other = lax.ppermute(own, "c", SWAP)
        conv_grad, latent = call(spread_kernel, "spread", [shape(9, 256, 256), shape(2, 256)], [SM, VM, VM])(
            place, own, other
        )

    with jax.named_scope("join_grad"):
        rest_other = lax.ppermute(rest, "c", SWAP)
        both = jnp.concatenate([rest, rest_other], 0)
        rows = lax.dynamic_slice_in_dim(both, place[0] * 64, 64, 1)
        join_grad = lax.dot_general(rows, both[:, 128:], (((0,), (0,)), ((), ())), preferred_element_type=F32)
    return (latent, conv_grad, join_grad)


def solution(mesh):
    fine = Mesh(mesh.devices.reshape(2, 4, 2, 4, 4), ("zl", "x", "c", "zh", "y"))
    frame, cam = ("zl", "x", "c"), ("zh", "y")
    in_specs = (
        P(frame, cam, None, None, None),
        P(),
        P(cam, None),
        P(frame, None),
        P(frame, None),
    )
    out_specs = (P(frame, None), P(), P(cam + frame, None))
    return jax.shard_map(on_device, mesh=fine, in_specs=in_specs, out_specs=out_specs, check_vma=False)
```

time: 106 us -> 93.7 us (0.88)
  blocking collectives: 30.4 us -> 65.1 us
  waiting for transfers between devices: 26.8 us -> 3.14 us
  starting transfers between devices: 29.1 us -> 6.26 us
  Pallas kernels: 8.57 us -> 10.7 us
  other arithmetic: 1.56 us -> 0 us
    all_to_all x1 -> x4, blocking collectives: 30.4 us -> 65.1 us  [the longest x1 20.8 us: on_device(): cam_shares = lax.all_to_all(shares, ('zh', 'y'), 0, 0)]
    all_to_all x2 -> x0, starting transfers between devices: 23.7 us -> none  [the longest x1 11.9 us: on_device(): blocks = lax.all_to_all(packed, CHIPS, 0, 0)]
    all_to_all x2 -> x0, waiting for transfers between devices: 23.3 us -> none  [the longest x1 22.4 us: on_device(): blocks = lax.all_to_all(packed, CHIPS, 0, 0)]
    pallas_call x6 -> x7, Pallas kernels: 8.57 us -> 10.7 us  [the longest x1 4.89 us: on_device(): call(forward_kernel, 'forward', [shape(16, 16, 256, dtype=BF), shape(22,...]
    unnamed x14 -> x17, local copies, waits for them, and re-layouts: 6.56 us -> 6.46 us
  transfers between devices with their start and end apart: 5 -> 3, of which waited for: 4 -> 2; matrix products, arithmetic and copies ran while one was open for 3% -> 1% of each run, Pallas kernels for 3% -> 0%
where the time goes in v2:
time: 93.7 us; the launch traced here: 93.3 us
  blocking collectives  65.1 us (69%)
  Pallas kernels  10.7 us (11%)
  local copies, waits for them, and re-layouts  6.55 us (7%)
  starting transfers between devices  6.26 us (7%)
  waiting for transfers between devices  3.14 us (3%)
    all_to_all x1, blocking collectives, on_device(): cam_shares = lax.all_to_all(shares, ('zh', 'y'), 0, 0)  20.8 us
    all_to_all x1, blocking collectives, on_device(): blocks = lax.all_to_all(packed, ('x', 'y'), 0, 0)  16.9 us
    all_to_all x1, blocking collectives, on_device(): lines = lax.all_to_all(middle, ('zh', 'zl'), 0, 0)  14.2 us
    all_to_all x1, blocking collectives, on_device(): own = lax.all_to_all(summed, ('x', 'y'), 0, 0)  13.2 us
    unnamed x17, local copies, waits for them, and re-layouts  6.46 us
    pallas_call x1, Pallas kernels, on_device(): call(forward_kernel, 'forward', [shape(16, 16, 256, dtype=BF), shape(22,...  4.89 us
    ppermute x1, starting transfers between devices, on_device(): other = lax.ppermute(own, 'c', SWAP)  4.07 us
    ppermute x1, starting transfers between devices, on_device(): got = lax.ppermute(send, 'c', SWAP)  2.18 us
  transfers between devices with their start and end apart: 3, of which 2 were waited for; matrix products, arithmetic and copies ran while one was open for 1% of the time, Pallas kernels for 0%

profile of v2, /device:TPU:1, one launch (start us, length us, event | category | flops | bytes accessed | tf_op | source)
XLA Modules:
  0.0 93.3 jit_solution(17314974209728718199)
XLA Ops:
  0.6 0.1 stack.27.place_ref
  0.7 1.0 %copy-done = bf16[1024,256]{1,0:T(8,128)(2,1)S(1)} copy-done((bf16[1024,256]{1,0:T(8,128)(2,1)S(1)}, bf16[1024,256]{1,0:T(8,128)(2,1)}, u32[]{:S(2)}) %copy-start) | copy-done | bytes 524312
  1.8 0.7 copy-done.2
  2.5 1.3 %copy-done.4 = bf16[9,256,256]{2,1,0:T(8,128)(2,1)S(1)} copy-done((bf16[9,256,256]{2,1,0:T(8,128)(2,1)S(1)}, bf16[9,256,256]{2,1,0:T(8,128)(2,1)}, u32[]{:S(2)}) %copy-start.4) | copy-done | bytes 1179672
  3.7 1.1 %copy-done.5 = bf16[2,11,2,32,256]{4,3,2,1,0:T(8,128)(2,1)S(1)} copy-done((bf16[2,11,2,32,256]{4,3,2,1,0:T(8,128)(2,1)S(1)}, bf16[2,11,2,32,256]{4,3,2,1,0:T(8,128)(2,1)}, u32[]{:S(2)}) %copy-start.5) | copy-done | bytes 720920
  4.8 0.7 copy-done.6
  5.5 4.9 %forward.1 = (bf16[16,16,256]{2,1,0:T(8,128)(2,1)S(1)}, f32[22,64,256]{2,1,0:T(8,128)S(1)}, bf16[2,768,768]{2,1,0:T(8,128)(2,1)}) custom-call(s32[6]{0:T(128)S(1)} %stack.27.place_ref, s32[2,176]{1,0:T(2,128)S(1)} %copy-done.6, bf16[2,256]{1,0:T(2,128)(2,1)S(1)} %copy-done.2, bf16[1024,256]{1,0:T(8,128)(2,1)S(1)} %copy-done, ...), custom_call_target="tpu_custom_call" | custom-call | flops 1200000000 | bytes 3000000 | tf_op jit(solution)/shard_map/forward/forward/pallas_call | solution.py:255
  10.4 20.8 %all_to_all.20.grad_ref.got_ref = bf16[16,16,256]{2,1,0:T(8,128)(2,1)S(1)} all-to-all(bf16[16,16,256]{2,1,0:T(8,128)(2,1)S(1)} %get-tuple-element.14), channel_id=1, replica_groups=mesh['zl'=2,'x'=4,'c'=2,'zh'=4,'y'=4] {'zh','y'}, dimensions={0} | all-to-all | bytes 262144 | tf_op jit(solution)/shard_map/forward/all_to_all | solution.py:271
  31.2 1.7 %copy-done.7 = bf16[2,768,768]{2,1,0:T(8,128)(2,1)S(1)} copy-done((bf16[2,768,768]{2,1,0:T(8,128)(2,1)S(1)}, bf16[2,768,768]{2,1,0:T(8,128)(2,1)}, u32[]{:S(2)}) %copy-start.7) | copy-done | bytes 2359320
  32.9 1.4 %backward.1 = (f32[2304,128]{1,0:T(8,128)S(1)}, bf16[2304,128]{1,0:T(8,128)(2,1)S(1)}) custom-call(bf16[16,16,256]{2,1,0:T(8,128)(2,1)S(1)} %all_to_all.20.grad_ref.got_ref, f32[22,64,256]{2,1,0:T(8,128)S(1)} %get-tuple-element.15.slope_ref, bf16[2,768,768]{2,1,0:T(8,128)(2,1)S(1)} %copy-done.7), custom_call_target="tpu_custom_call" | custom-call | flops 1200000000 | bytes 3000000 | tf_op jit(solution)/shard_map/backward/backward/pallas_call | solution.py:274
  34.3 2.2 %collective-permute-start = (bf16[2304,128]{1,0:T(8,128)(2,1)S(1)}, bf16[2304,128]{1,0:T(8,128)(2,1)S(1)}, u32[]{:S(2)}, u32[]{:S(2)}) collective-permute-start(bf16[2304,128]{1,0:T(8,128)(2,1)S(1)} %get-tuple-element.18), channel_id=1, source_target_pairs={{0,16},{16,0},{1,17},{17,1},{2,18},{18,2},{3,19},{19,3},{4,20},{20... | collective-permute-start | bytes 1769480 | tf_op jit(solution)/shard_map/backward/ppermute | solution.py:282
  36.5 0.2 join.1
  36.7 1.5 %collective-permute-done.got_ref = bf16[2304,128]{1,0:T(8,128)(2,1)S(1)} collective-permute-done((bf16[2304,128]{1,0:T(8,128)(2,1)S(1)}, bf16[2304,128]{1,0:T(8,128)(2,1)S(1)}, u32[]{:S(2)}, u32[]{:S(2)}) %collective-permute-start) | collective-permute-done | bytes 589856 | tf_op jit(solution)/shard_map/backward/ppermute | solution.py:282
  38.1 0.8 pack.1
  39.0 16.9 %all_to_all.21.got_ref = bf16[16,160,128]{2,1,0:T(8,128)(2,1)S(1)} all-to-all(bf16[16,160,128]{2,1,0:T(8,128)(2,1)S(1)} %pack.1), channel_id=1, replica_groups=mesh['zl'=2,'x'=4,'c'=2,'zh'=4,'y'=4] {'x','y'}, dimensions={0} | all-to-all | bytes 1310720 | tf_op jit(solution)/shard_map/conv_scatter/all_to_all | solution.py:297
  55.8 0.7 middle.1
  56.5 14.2 %all_to_all.22.got_ref = bf16[8,176,128]{2,1,0:T(8,128)(2,1)S(1)} all-to-all(bf16[8,176,128]{2,1,0:T(8,128)(2,1)S(1)} %middle.1), channel_id=1, replica_groups=mesh['zl'=2,'x'=4,'c'=2,'zh'=4,'y'=4] {'zh','zl'}, dimensions={0} | all-to-all | bytes 720896 | tf_op jit(solution)/shard_map/conv_middle/all_to_all | solution.py:303
  70.7 0.6 finish.1
  71.3 13.2 %all_to_all.23.own_ref = bf16[16,152,128]{2,1,0:T(8,128)(2,1)S(1)} all-to-all(bf16[16,152,128]{2,1,0:T(8,128)(2,1)S(1)} %get-tuple-element.21), channel_id=1, replica_groups=mesh['zl'=2,'x'=4,'c'=2,'zh'=4,'y'=4] {'x','y'}, dimensions={0} | all-to-all | bytes 1245184 | tf_op jit(solution)/shard_map/conv_gather/all_to_all | solution.py:313
  84.5 4.1 %collective-permute-start.1 = (bf16[16,152,128]{2,1,0:T(8,128)(2,1)S(1)}, bf16[16,152,128]{2,1,0:T(8,128)(2,1)S(1)}, u32[]{:S(2)}, u32[]{:S(2)}) collective-permute-start(bf16[16,152,128]{2,1,0:T(8,128)(2,1)S(1)} %all_to_all.23.own_ref), channel_id=1, source_target_pairs={{0,16},{16,0},{1,17},{17,1},{2,18},{18,2},{3,19},{19,3},{4,20},{20... | collective-permute-start | bytes 1867784 | tf_op jit(solution)/shard_map/conv_gather/ppermute | solution.py:314
  88.6 0.0 collective-permute-start.2
  88.6 1.7 %collective-permute-done.2 = bf16[16,384]{1,0:T(8,128)(2,1)S(1)} collective-permute-done((bf16[16,384]{1,0:T(8,128)(2,1)S(1)}, bf16[16,384]{1,0:T(8,128)(2,1)S(1)}, u32[]{:S(2)}, u32[]{:S(2)}) %collective-permute-start.2) | collective-permute-done | bytes 12320 | tf_op jit(solution)/shard_map/join_grad/ppermute | solution.py:320
  90.3 0.9 fusion
  91.2 2.1 %spread.1 = (f32[9,256,256]{2,1,0:T(8,128)}, f32[2,256]{1,0:T(2,128)}) custom-call(s32[6]{0:T(128)S(1)} %stack.27.place_ref, bf16[16,152,128]{2,1,0:T(8,128)(2,1)S(1)} %all_to_all.23.own_ref, bf16[16,152,128]{2,1,0:T(8,128)(2,1)S(1)} %collective-permute-done.1.other_ref), custom_call_target="tpu_custom_call" | custom-call | flops 1000000 | bytes 3000000 | tf_op jit(solution)/shard_map/conv_gather/spread/pallas_call | solution.py:315
  (13 shorter events, 0.0 us)
Async XLA Ops:
  0.7 1.0 %copy-start = (bf16[1024,256]{1,0:T(8,128)(2,1)S(1)}, bf16[1024,256]{1,0:T(8,128)(2,1)}, u32[]{:S(2)}) copy-start(bf16[1024,256]{1,0:T(8,128)(2,1)} %join_ref.1) | copy-start | bytes 1572868
  1.8 0.7 copy-start.2
  2.4 1.3 %copy-start.4 = (bf16[9,256,256]{2,1,0:T(8,128)(2,1)S(1)}, bf16[9,256,256]{2,1,0:T(8,128)(2,1)}, u32[]{:S(2)}) copy-start(bf16[9,256,256]{2,1,0:T(8,128)(2,1)} %conv_hbm.1) | copy-start | bytes 3538948
  3.7 1.1 %copy-start.5 = (bf16[2,11,2,32,256]{4,3,2,1,0:T(8,128)(2,1)S(1)}, bf16[2,11,2,32,256]{4,3,2,1,0:T(8,128)(2,1)}, u32[]{:S(2)}) copy-start(bf16[2,11,2,32,256]{4,3,2,1,0:T(8,128)(2,1)} %param.5) | copy-start | bytes 2162692
  4.8 0.7 copy-start.6
  31.2 1.7 %copy-start.7 = (bf16[2,768,768]{2,1,0:T(8,128)(2,1)S(1)}, bf16[2,768,768]{2,1,0:T(8,128)(2,1)}, u32[]{:S(2)}) copy-start(bf16[2,768,768]{2,1,0:T(8,128)(2,1)} %get-tuple-element.16.turned_ref) | copy-start | bytes 7077892
  32.9 3.6 %copy-start.1 = (bf16[1024,256]{1,0:T(8,128)(2,1)S(1)}, bf16[1024,256]{1,0:T(8,128)(2,1)}, u32[]{:S(2)}) copy-start(bf16[1024,256]{1,0:T(8,128)(2,1)} %join_ref.1) | copy-start | bytes 1572868
  32.9 5.2 %copy-start.3 = (bf16[2,256]{1,0:T(2,128)(2,1)S(1)}, bf16[2,256]{1,0:T(2,128)(2,1)}, u32[]{:S(2)}) copy-start(bf16[2,256]{1,0:T(2,128)(2,1)} %grad_ref.1) | copy-start | bytes 3076
  34.3 3.8 %collective-permute-start = (bf16[2304,128]{1,0:T(8,128)(2,1)S(1)}, bf16[2304,128]{1,0:T(8,128)(2,1)S(1)}, u32[]{:S(2)}, u32[]{:S(2)}) collective-permute-start(bf16[2304,128]{1,0:T(8,128)(2,1)S(1)} %get-tuple-element.18), channel_id=1, source_target_pairs={{0,16},{16,0},{1,17},{17,1},{2,18},{18,2},{3,19},{19,3},{4,20},{20... | collective-permute-start | bytes 1769480 | tf_op jit(solution)/shard_map/backward/ppermute | solution.py:282
  84.5 6.7 %collective-permute-start.1 = (bf16[16,152,128]{2,1,0:T(8,128)(2,1)S(1)}, bf16[16,152,128]{2,1,0:T(8,128)(2,1)S(1)}, u32[]{:S(2)}, u32[]{:S(2)}) collective-permute-start(bf16[16,152,128]{2,1,0:T(8,128)(2,1)S(1)} %all_to_all.23.own_ref), channel_id=1, source_target_pairs={{0,16},{16,0},{1,17},{17,1},{2,18},{18,2},{3,19},{19,3},{4,20},{20... | collective-permute-start | bytes 1867784 | tf_op jit(solution)/shard_map/conv_gather/ppermute | solution.py:314
  88.6 1.7 %collective-permute-start.2 = (bf16[16,384]{1,0:T(8,128)(2,1)S(1)}, bf16[16,384]{1,0:T(8,128)(2,1)S(1)}, u32[]{:S(2)}, u32[]{:S(2)}) collective-permute-start(bf16[16,384]{1,0:T(8,128)(2,1)S(1)} %get-tuple-element.24), channel_id=1, source_target_pairs={{0,16},{16,0},{1,17},{17,1},{2,18},{18,2},{3,19},{19,3},{4,20},{20... | collective-permute-start | bytes 36872 | tf_op jit(solution)/shard_map/join_grad/ppermute | solution.py:320

commit v3 on v2

--- a/solution.py
+++ b/solution.py
@@ -216,18 +216,43 @@
     rest_ref[...] = rows_ref[...].astype(BF)
 
 
-def spread_kernel(place_ref, own_ref, other_ref, conv_ref, latent_ref):
-    core, own_x = place_ref[0], place_ref[2]
-    for ref, half in ((own_ref, core), (other_ref, 1 - core)):
-        for g in range(144):
-            s, i = g // 8, 16 * (g % 8)
-            start = pl.multiple_of(half * 128 + i, 16)
-            lanes = slice(128 * (s % 2), 128 * (s % 2) + 128)
-            offset = 16 * (g % 9)
-            conv_ref[s // 2, pl.ds(start, 16), lanes] = ref[g // 9, offset : offset + 16, :].astype(F32)
+def spread_half(ref, conv_ref):
+    for g in range(144):
+        s, i, offset = g // 8, 16 * (g % 8), 16 * (g % 9)
+        lanes = slice(128 * (s % 2), 128 * (s % 2) + 128)
+        conv_ref[s // 2, i : i + 16, lanes] = ref[g // 9, offset : offset + 16, :].astype(F32)
+
+
+def spread_own_kernel(place_ref, own_ref, conv_ref, latent_ref):
+    spread_half(own_ref, conv_ref)
     for y in range(4):
-        row = own_ref[4 * own_x + y, 144:152, :].astype(F32)[0:1]
+        row = own_ref[4 * place_ref[2] + y, 144:152, :].astype(F32)[0:1]
         latent_ref[y // 2 : y // 2 + 1, 128 * (y % 2) : 128 * (y % 2) + 128] = row
+
+
+def spread_other_kernel(place_ref, other_ref, begun_ref, conv_ref):
+    spread_half(other_ref, conv_ref)
+
+
+def spread(kernel, name, place, blocks, begun=None):
+    own = begun is None
+    whole = pl.BlockSpec((16, 152, 128), lambda i, at: (0, 0, 0))
+    half = pl.BlockSpec((9, 128, 256), lambda i, at: (0, at[0] if own else 1 - at[0], 0))
+    conv_shape = shape(9, 256, 256)
+    return pl.pallas_call(
+        kernel,
+        out_shape=[conv_shape, shape(2, 256)] if own else [conv_shape],
+        grid_spec=pltpu.PrefetchScalarGridSpec(
+            num_scalar_prefetch=1,
+            grid=(1,),
+            in_specs=[whole] if own else [whole, HBM],
+            out_specs=[half, pl.BlockSpec((2, 256), lambda i, at: (0, 0))] if own else [half],
+        ),
+        input_output_aliases={} if own else {2: 0},
+        compiler_params=params(),
+        cost_estimate=pl.CostEstimate(flops=1_000_000, bytes_accessed=2_000_000, transcendentals=0),
+        name=name,
+    )(place, blocks, *(() if own else (begun,)))
 
 
 def shape(*dims, dtype=F32):
@@ -245,6 +270,10 @@
         cost_estimate=pl.CostEstimate(flops=flops, bytes_accessed=moved, transcendentals=0),
         name=name,
     )
+
+
+def in_hbm(array):
+    return pltpu.with_memory_space_constraint(array, pltpu.HBM)
 
 
 def on_device(view_maps, conv_weight, join_weight, valid_cams, latent_grad):
@@ -267,7 +296,7 @@
                 pltpu.SemaphoreType.DMA((5,)),
             ],
             flops=1_200_000_000,
-        )(place, valid_cams, latent_grad, join_weight, view_maps.reshape(22, 64, 256), conv_weight)
+        )(place, *map(in_hbm, (valid_cams, latent_grad, join_weight, view_maps.reshape(22, 64, 256), conv_weight)))
         cam_shares = lax.all_to_all(shares, ("zh", "y"), 0, 0)
 
     with jax.named_scope("backward"):
@@ -312,15 +341,16 @@
         )(place, lines)
         own = lax.all_to_all(summed, ("x", "y"), 0, 0)
         other = lax.ppermute(own, "c", SWAP)
-        conv_grad, latent = call(spread_kernel, "spread", [shape(9, 256, 256), shape(2, 256)], [SM, VM, VM])(
-            place, own, other
-        )
+        begun, latent = spread(spread_own_kernel, "spread_own", place, own)
 
     with jax.named_scope("join_grad"):
         rest_other = lax.ppermute(rest, "c", SWAP)
         both = jnp.concatenate([rest, rest_other], 0)
         rows = lax.dynamic_slice_in_dim(both, place[0] * 64, 64, 1)
         join_grad = lax.dot_general(rows, both[:, 128:], (((0,), (0,)), ((), ())), preferred_element_type=F32)
+
+    with jax.named_scope("conv_end"):
+        (conv_grad,) = spread(spread_other_kernel, "spread_other", place, other, begun)
     return (latent, conv_grad, join_grad)
 
 

time: 93.7 us -> 87.9 us (0.938)
  local copies, waits for them, and re-layouts: 6.55 us -> 0.11 us
    unnamed x17 -> x5, local copies, waits for them, and re-layouts: 6.46 us -> 0.01 us
    pallas_call x1 -> x2, Pallas kernels: 2.11 us -> 3.27 us  [spread(): pl.pallas_call(kernel, out_shape=[conv_shape, shape(2, 256)] if own else...]
  transfers between devices with their start and end apart: 3 -> 3, of which waited for: 2 -> 2; matrix products, arithmetic and copies ran while one was open for 1% -> 1% of each run, Pallas kernels for 0% -> 2%
where the time goes in v3:
time: 87.9 us; the launch traced here: 87.7 us
  blocking collectives  65.2 us (74%)
  Pallas kernels  11.4 us (13%)
  starting transfers between devices  6.26 us (7%)
  waiting for transfers between devices  3.14 us (4%)
  matrix products  0.88 us (1%)
    all_to_all x1, blocking collectives, on_device(): cam_shares = lax.all_to_all(shares, ('zh', 'y'), 0, 0)  20.9 us
    all_to_all x1, blocking collectives, on_device(): blocks = lax.all_to_all(packed, ('x', 'y'), 0, 0)  16.9 us
    all_to_all x1, blocking collectives, on_device(): lines = lax.all_to_all(middle, ('zh', 'zl'), 0, 0)  14.2 us
    all_to_all x1, blocking collectives, on_device(): own = lax.all_to_all(summed, ('x', 'y'), 0, 0)  13.2 us
    pallas_call x1, Pallas kernels, on_device(): call(forward_kernel, 'forward', [shape(16, 16, 256, dtype=BF), shape(22,...  4.37 us
    ppermute x1, starting transfers between devices, on_device(): other = lax.ppermute(own, 'c', SWAP)  4.07 us
    pallas_call x2, Pallas kernels, spread(): pl.pallas_call(kernel, out_shape=[conv_shape, shape(2, 256)] if own else...  3.27 us
    ppermute x1, starting transfers between devices, on_device(): got = lax.ppermute(send, 'c', SWAP)  2.19 us
  transfers between devices with their start and end apart: 3, of which 2 were waited for; matrix products, arithmetic and copies ran while one was open for 1% of the time, Pallas kernels for 2%

profile of v3, /device:TPU:1, one launch (start us, length us, event | category | flops | bytes accessed | tf_op | source)
XLA Modules:
  0.0 87.7 jit_solution(7222265009092621371)
XLA Ops:
  0.6 0.1 stack.27.place_ref
  0.7 4.4 %forward.1 = (bf16[16,16,256]{2,1,0:T(8,128)(2,1)S(1)}, f32[22,64,256]{2,1,0:T(8,128)S(1)}, bf16[2,768,768]{2,1,0:T(8,128)(2,1)S(1)}) custom-call(s32[6]{0:T(128)S(1)} %stack.27.place_ref, s32[2,176]{1,0:T(2,128)} %valid_hbm.1, bf16[2,256]{1,0:T(2,128)(2,1)} %grad_ref.1, bf16[1024,256]{1,0:T(8,128)(2,1)} %join_ref.1, bf16[22,64,256]{2,1,0:T(8,128)(2,1)} %bitcast.7, ...), custom_call_target="tpu_custom_call" | custom-call | flops 1200000000 | bytes 3000000 | tf_op jit(solution)/shard_map/forward/forward/pallas_call | solution.py:284
  5.1 0.0 copy-start
  5.1 20.9 %all_to_all.20.grad_ref.got_ref = bf16[16,16,256]{2,1,0:T(8,128)(2,1)S(1)} all-to-all(bf16[16,16,256]{2,1,0:T(8,128)(2,1)S(1)} %get-tuple-element.14), channel_id=1, replica_groups=mesh['zl'=2,'x'=4,'c'=2,'zh'=4,'y'=4] {'zh','y'}, dimensions={0} | all-to-all | bytes 262144 | tf_op jit(solution)/shard_map/forward/all_to_all | solution.py:300
  26.0 0.0 copy-start.1
  26.1 1.4 %backward.1 = (f32[2304,128]{1,0:T(8,128)S(1)}, bf16[2304,128]{1,0:T(8,128)(2,1)S(1)}) custom-call(bf16[16,16,256]{2,1,0:T(8,128)(2,1)S(1)} %all_to_all.20.grad_ref.got_ref, f32[22,64,256]{2,1,0:T(8,128)S(1)} %get-tuple-element.15.slope_ref, bf16[2,768,768]{2,1,0:T(8,128)(2,1)S(1)} %get-tuple-element.16.turned_ref), custom_call_target="tpu_custom_call" | custom-call | flops 1200000000 | bytes 3000000 | tf_op jit(solution)/shard_map/backward/backward/pallas_call | solution.py:303
  27.5 2.2 %collective-permute-start = (bf16[2304,128]{1,0:T(8,128)(2,1)S(1)}, bf16[2304,128]{1,0:T(8,128)(2,1)S(1)}, u32[]{:S(2)}, u32[]{:S(2)}) collective-permute-start(bf16[2304,128]{1,0:T(8,128)(2,1)S(1)} %get-tuple-element.18), channel_id=1, source_target_pairs={{0,16},{16,0},{1,17},{17,1},{2,18},{18,2},{3,19},{19,3},{4,20},{20... | collective-permute-start | bytes 1769480 | tf_op jit(solution)/shard_map/backward/ppermute | solution.py:311
  29.6 0.0 copy-done
  29.6 0.2 join.1
  29.8 1.5 %collective-permute-done.got_ref = bf16[2304,128]{1,0:T(8,128)(2,1)S(1)} collective-permute-done((bf16[2304,128]{1,0:T(8,128)(2,1)S(1)}, bf16[2304,128]{1,0:T(8,128)(2,1)S(1)}, u32[]{:S(2)}, u32[]{:S(2)}) %collective-permute-start) | collective-permute-done | bytes 589856 | tf_op jit(solution)/shard_map/backward/ppermute | solution.py:311
  31.3 0.0 copy-done.1
  31.3 0.8 pack.1
  32.1 16.9 %all_to_all.21.got_ref = bf16[16,160,128]{2,1,0:T(8,128)(2,1)S(1)} all-to-all(bf16[16,160,128]{2,1,0:T(8,128)(2,1)S(1)} %pack.1), channel_id=1, replica_groups=mesh['zl'=2,'x'=4,'c'=2,'zh'=4,'y'=4] {'x','y'}, dimensions={0} | all-to-all | bytes 1310720 | tf_op jit(solution)/shard_map/conv_scatter/all_to_all | solution.py:326
  49.0 0.7 middle.1
  49.7 14.2 %all_to_all.22.got_ref = bf16[8,176,128]{2,1,0:T(8,128)(2,1)S(1)} all-to-all(bf16[8,176,128]{2,1,0:T(8,128)(2,1)S(1)} %middle.1), channel_id=1, replica_groups=mesh['zl'=2,'x'=4,'c'=2,'zh'=4,'y'=4] {'zh','zl'}, dimensions={0} | all-to-all | bytes 720896 | tf_op jit(solution)/shard_map/conv_middle/all_to_all | solution.py:332
  63.9 0.6 finish.1
  64.5 13.2 %all_to_all.23.own_ref = bf16[16,152,128]{2,1,0:T(8,128)(2,1)S(1)} all-to-all(bf16[16,152,128]{2,1,0:T(8,128)(2,1)S(1)} %get-tuple-element.21), channel_id=1, replica_groups=mesh['zl'=2,'x'=4,'c'=2,'zh'=4,'y'=4] {'x','y'}, dimensions={0} | all-to-all | bytes 1245184 | tf_op jit(solution)/shard_map/conv_gather/all_to_all | solution.py:342
  77.7 4.1 %collective-permute-start.1 = (bf16[16,152,128]{2,1,0:T(8,128)(2,1)S(1)}, bf16[16,152,128]{2,1,0:T(8,128)(2,1)S(1)}, u32[]{:S(2)}, u32[]{:S(2)}) collective-permute-start(bf16[16,152,128]{2,1,0:T(8,128)(2,1)S(1)} %all_to_all.23.own_ref), channel_id=1, source_target_pairs={{0,16},{16,0},{1,17},{17,1},{2,18},{18,2},{3,19},{19,3},{4,20},{20... | collective-permute-start | bytes 1867784 | tf_op jit(solution)/shard_map/conv_gather/ppermute | solution.py:343
  81.8 0.0 collective-permute-start.2
  81.8 1.7 %collective-permute-done.2 = bf16[16,384]{1,0:T(8,128)(2,1)S(1)} collective-permute-done((bf16[16,384]{1,0:T(8,128)(2,1)S(1)}, bf16[16,384]{1,0:T(8,128)(2,1)S(1)}, u32[]{:S(2)}, u32[]{:S(2)}) %collective-permute-start.2) | collective-permute-done | bytes 12320 | tf_op jit(solution)/shard_map/join_grad/ppermute | solution.py:347
  83.5 0.9 %fusion = f32[64,256]{1,0:T(8,128)} fusion(bf16[32,384]{1,0:T(8,128)(2,1)S(1)} %constant_dynamic-update-slice_fusion, s32[]{:T(128)S(6)} %select_n.3), kind=kOutput, calls=%fused_computation | convolution fusion | flops 1048576 | bytes 90116 | tf_op jit(solution)/shard_map/join_grad/dot_general | solution.py:350
  84.4 1.6 %spread_own.1 = (f32[9,256,256]{2,1,0:T(8,128)}, f32[2,256]{1,0:T(2,128)}) custom-call(s32[6]{0:T(128)S(1)} %stack.27.place_ref, bf16[16,152,128]{2,1,0:T(8,128)(2,1)S(1)} %all_to_all.23.own_ref), custom_call_target="tpu_custom_call" | custom-call | flops 1000000 | bytes 2000000 | tf_op jit(solution)/shard_map/conv_gather/spread_own/pallas_call | solution.py:242
  86.0 0.0 collective-permute-done.1.other_ref
  86.0 1.6 %spread_other.1 = f32[9,256,256]{2,1,0:T(8,128)} custom-call(s32[6]{0:T(128)S(1)} %stack.27.place_ref, bf16[16,152,128]{2,1,0:T(8,128)(2,1)S(1)} %collective-permute-done.1.other_ref, f32[9,256,256]{2,1,0:T(8,128)} %get-tuple-element.23.begun_ref), custom_call_target="tpu_custom_call", output_to_operand_aliasing={{}: (2, {})} | custom-call | flops 1000000 | bytes 2000000 | tf_op jit(solution)/shard_map/conv_end/spread_other/pallas_call | solution.py:242
  (2 shorter events, 0.0 us)
Async XLA Ops:
  5.1 24.5 %copy-start = (bf16[1024,256]{1,0:T(8,128)(2,1)S(1)}, bf16[1024,256]{1,0:T(8,128)(2,1)}, u32[]{:S(2)}) copy-start(bf16[1024,256]{1,0:T(8,128)(2,1)} %join_ref.1) | copy-start | bytes 1572868
  26.0 5.2 %copy-start.1 = (bf16[2,256]{1,0:T(2,128)(2,1)S(1)}, bf16[2,256]{1,0:T(2,128)(2,1)}, u32[]{:S(2)}) copy-start(bf16[2,256]{1,0:T(2,128)(2,1)} %grad_ref.1) | copy-start | bytes 3076
  27.5 3.8 %collective-permute-start = (bf16[2304,128]{1,0:T(8,128)(2,1)S(1)}, bf16[2304,128]{1,0:T(8,128)(2,1)S(1)}, u32[]{:S(2)}, u32[]{:S(2)}) collective-permute-start(bf16[2304,128]{1,0:T(8,128)(2,1)S(1)} %get-tuple-element.18), channel_id=1, source_target_pairs={{0,16},{16,0},{1,17},{17,1},{2,18},{18,2},{3,19},{19,3},{4,20},{20... | collective-permute-start | bytes 1769480 | tf_op jit(solution)/shard_map/backward/ppermute | solution.py:311
  77.7 8.3 %collective-permute-start.1 = (bf16[16,152,128]{2,1,0:T(8,128)(2,1)S(1)}, bf16[16,152,128]{2,1,0:T(8,128)(2,1)S(1)}, u32[]{:S(2)}, u32[]{:S(2)}) collective-permute-start(bf16[16,152,128]{2,1,0:T(8,128)(2,1)S(1)} %all_to_all.23.own_ref), channel_id=1, source_target_pairs={{0,16},{16,0},{1,17},{17,1},{2,18},{18,2},{3,19},{19,3},{4,20},{20... | collective-permute-start | bytes 1867784 | tf_op jit(solution)/shard_map/conv_gather/ppermute | solution.py:343
  81.8 1.7 %collective-permute-start.2 = (bf16[16,384]{1,0:T(8,128)(2,1)S(1)}, bf16[16,384]{1,0:T(8,128)(2,1)S(1)}, u32[]{:S(2)}, u32[]{:S(2)}) collective-permute-start(bf16[16,384]{1,0:T(8,128)(2,1)S(1)} %get-tuple-element.24), channel_id=1, source_target_pairs={{0,16},{16,0},{1,17},{17,1},{2,18},{18,2},{3,19},{19,3},{4,20},{20... | collective-permute-start | bytes 36872 | tf_op jit(solution)/shard_map/join_grad/ppermute | solution.py:347

commit v4 on v2

--- a/solution.py
+++ b/solution.py
@@ -116,7 +116,7 @@
                 turned_ref[r, pl.ds(start, 128), :] = turned[128 * half : 128 * half + 128]
 
 
-def backward_kernel(grad_ref, slope_ref, turned_ref, mine_ref, send_ref, grads):
+def send_kernel(grad_ref, slope_ref, turned_ref, pre_ref, send_ref, grads):
     for k in range(16):
         block = grad_ref[k, 0:8, :].astype(F32)
         for f in range(2):
@@ -131,21 +131,31 @@
         parts.append(jnp.zeros((KDIM - 704, 256), BF))
         pre.append(jnp.concatenate(parts, 0))
 
-    def put(dy, value):
-        for slot, ref in enumerate((mine_ref, send_ref)):
-            for dx in range(3):
-                for h in range(2):
-                    s = (dy * 3 + dx) * 2 + h
-                    ref[128 * s : 128 * s + 128, :] = value[
-                        slot * 384 + dx * 128 : slot * 384 + dx * 128 + 128, 128 * h : 128 * h + 128
-                    ].astype(ref.dtype)
-
-    put(0, dot(turned_ref[0], pre[1]))
-    put(1, dot(turned_ref[0], pre[0]) + dot(turned_ref[1], pre[1]))
-    put(2, dot(turned_ref[1], pre[0]))
-
-
-def join_kernel(got_ref, join_ref, joined_ref, latent_ref):
+    for r in range(2):
+        pre_ref[r] = pre[r]
+    half_taps(turned_ref, pre_ref, 1, send_ref)
+
+
+def half_taps(turned_ref, pre_ref, slot, out_ref):
+    part = slice(384 * slot, 384 * slot + 384)
+    top, low = turned_ref[0, part], turned_ref[1, part]
+    for dy in range(3):
+        if dy == 0:
+            value = dot(top, pre_ref[1])
+        elif dy == 1:
+            value = dot(top, pre_ref[0]) + dot(low, pre_ref[1])
+        else:
+            value = dot(low, pre_ref[0])
+        for dx in range(3):
+            for h in range(2):
+                s = (dy * 3 + dx) * 2 + h
+                out_ref[128 * s : 128 * s + 128, :] = value[
+                    128 * dx : 128 * dx + 128, 128 * h : 128 * h + 128
+                ].astype(out_ref.dtype)
+
+
+def mine_kernel(turned_ref, pre_ref, got_ref, join_ref, mine_ref, joined_ref, latent_ref):
+    half_taps(turned_ref, pre_ref, 0, mine_ref)
     pooled = jnp.sum(got_ref[:, 8:16, :].astype(F32), axis=0)
     joined = pooled.astype(BF)
     joined_ref[...] = joined.astype(F32)
@@ -216,18 +226,53 @@
     rest_ref[...] = rows_ref[...].astype(BF)
 
 
-def spread_kernel(place_ref, own_ref, other_ref, conv_ref, latent_ref):
-    core, own_x = place_ref[0], place_ref[2]
-    for ref, half in ((own_ref, core), (other_ref, 1 - core)):
-        for g in range(144):
-            s, i = g // 8, 16 * (g % 8)
-            start = pl.multiple_of(half * 128 + i, 16)
+def spread_half(ref, half, conv_hbm, slabs, sems):
+    copies = []
+    for t in range(9):
+        for g in range(16 * t, 16 * t + 16):
+            s, i, offset = g // 8, 16 * (g % 8), 16 * (g % 9)
             lanes = slice(128 * (s % 2), 128 * (s % 2) + 128)
-            offset = 16 * (g % 9)
-            conv_ref[s // 2, pl.ds(start, 16), lanes] = ref[g // 9, offset : offset + 16, :].astype(F32)
+            slabs[t, i : i + 16, lanes] = ref[g // 9, offset : offset + 16, :].astype(F32)
+        rows = pl.ds(pl.multiple_of(128 * half, 128), 128)
+        copies.append(pltpu.make_async_copy(slabs.at[t], conv_hbm.at[t, rows], sems.at[t]))
+        copies[t].start()
+    return copies
+
+
+def spread_own_kernel(place_ref, own_ref, conv_hbm, latent_ref, slabs, sems):
+    copies = spread_half(own_ref, place_ref[0], conv_hbm, slabs, sems)
     for y in range(4):
-        row = own_ref[4 * own_x + y, 144:152, :].astype(F32)[0:1]
+        row = own_ref[4 * place_ref[2] + y, 144:152, :].astype(F32)[0:1]
         latent_ref[y // 2 : y // 2 + 1, 128 * (y % 2) : 128 * (y % 2) + 128] = row
+    for copy in copies:
+        copy.wait()
+
+
+def spread_other_kernel(place_ref, other_ref, rest_ref, rest_other_ref, begun_hbm, conv_hbm, join_ref, slabs, sems):
+    core = place_ref[0]
+    copies = spread_half(other_ref, 1 - core, conv_hbm, slabs, sems)
+    total = jnp.zeros((64, 256), F32)
+    for ref in (rest_ref, rest_other_ref):
+        rows = ref[...]
+        joined = jnp.where(core == 0, rows[:, 0:64], rows[:, 64:128])
+        total = total + lax.dot_general(joined, rows[:, 128:384], (((0,), (0,)), ((), ())), preferred_element_type=F32)
+    join_ref[...] = total
+    for copy in copies:
+        copy.wait()
+
+
+def spread(kernel, name, out_shape, in_specs, aliases):
+    return pl.pallas_call(
+        kernel,
+        out_shape=out_shape,
+        in_specs=in_specs,
+        out_specs=[HBM, VM],
+        scratch_shapes=[pltpu.VMEM((9, 128, 256), F32), pltpu.SemaphoreType.DMA((9,))],
+        input_output_aliases=aliases,
+        compiler_params=params(),
+        cost_estimate=pl.CostEstimate(flops=1_000_000, bytes_accessed=2_000_000, transcendentals=0),
+        name=name,
+    )
 
 
 def shape(*dims, dtype=F32):
@@ -245,6 +290,10 @@
         cost_estimate=pl.CostEstimate(flops=flops, bytes_accessed=moved, transcendentals=0),
         name=name,
     )
+
+
+def in_hbm(array):
+    return pltpu.with_memory_space_constraint(array, pltpu.HBM)
 
 
 def on_device(view_maps, conv_weight, join_weight, valid_cams, latent_grad):
@@ -267,24 +316,26 @@
                 pltpu.SemaphoreType.DMA((5,)),
             ],
             flops=1_200_000_000,
-        )(place, valid_cams, latent_grad, join_weight, view_maps.reshape(22, 64, 256), conv_weight)
+        )(place, *map(in_hbm, (valid_cams, latent_grad, join_weight, view_maps.reshape(22, 64, 256), conv_weight)))
         cam_shares = lax.all_to_all(shares, ("zh", "y"), 0, 0)
 
     with jax.named_scope("backward"):
-        mine, send = call(
-            backward_kernel,
-            "backward",
-            [shape(2304, 128), shape(2304, 128, dtype=BF)],
+        pre_grad, send = call(
+            send_kernel,
+            "backward_send",
+            [shape(2, KDIM, 256, dtype=BF), shape(2304, 128, dtype=BF)],
             [VM, VM, VM],
             [pltpu.VMEM((2, 64, 256), F32)],
-            flops=1_200_000_000,
+            flops=600_000_000,
         )(cam_shares, slope, turned)
         got = lax.ppermute(send, "c", SWAP)
-
-    with jax.named_scope("join"):
-        joined, latent_part = call(join_kernel, "join", [shape(8, 256), shape(2, 256)], [VM, VM])(
-            cam_shares, join_weight
-        )
+        mine, joined, latent_part = call(
+            mine_kernel,
+            "backward_mine",
+            [shape(2304, 128), shape(8, 256), shape(2, 256)],
+            [VM, VM, VM, VM],
+            flops=600_000_000,
+        )(turned, pre_grad, cam_shares, join_weight)
 
     with jax.named_scope("conv_scatter"):
         (packed,) = call(
@@ -312,15 +363,15 @@
         )(place, lines)
         own = lax.all_to_all(summed, ("x", "y"), 0, 0)
         other = lax.ppermute(own, "c", SWAP)
-        conv_grad, latent = call(spread_kernel, "spread", [shape(9, 256, 256), shape(2, 256)], [SM, VM, VM])(
-            place, own, other
-        )
-
-    with jax.named_scope("join_grad"):
+        begun, latent = spread(
+            spread_own_kernel, "spread_own", [shape(9, 256, 256), shape(2, 256)], [SM, VM], {}
+        )(place, own)
+
+    with jax.named_scope("end"):
         rest_other = lax.ppermute(rest, "c", SWAP)
-        both = jnp.concatenate([rest, rest_other], 0)
-        rows = lax.dynamic_slice_in_dim(both, place[0] * 64, 64, 1)
-        join_grad = lax.dot_general(rows, both[:, 128:], (((0,), (0,)), ((), ())), preferred_element_type=F32)
+        conv_grad, join_grad = spread(
+            spread_other_kernel, "spread_other", [shape(9, 256, 256), shape(64, 256)], [SM, VM, VM, VM, HBM], {4: 0}
+        )(place, other, rest, rest_other, begun)
     return (latent, conv_grad, join_grad)
 
 

time: 93.7 us -> 86.1 us (0.919)
  local copies, waits for them, and re-layouts: 6.55 us -> 0.1 us
  waiting for transfers between devices: 3.14 us -> 0.82 us
  Pallas kernels: 10.7 us -> 12.7 us
    unnamed x17 -> x4, local copies, waits for them, and re-layouts: 6.46 us -> 0.01 us
    pallas_call x3 -> x4, Pallas kernels: 3.69 us -> 6.21 us  [the longest x1 2.38 us: on_device(): spread(spread_other_kernel, 'spread_other', [shape(9, 256, 256), shape(64...]
    ppermute x1, waiting for transfers between devices: 1.69 us -> 0.01 us  [on_device(): rest_other = lax.ppermute(rest, 'c', SWAP)]
  transfers between devices with their start and end apart: 3 -> 3, of which waited for: 2 -> 1; matrix products, arithmetic and copies ran while one was open for 1% -> 0% of each run, Pallas kernels for 0% -> 4%
where the time goes in v4:
time: 86.1 us; the launch traced here: 85.8 us
  blocking collectives  65.2 us (76%)
  Pallas kernels  12.7 us (15%)
  starting transfers between devices  6.27 us (7%)
    all_to_all x1, blocking collectives, on_device(): cam_shares = lax.all_to_all(shares, ('zh', 'y'), 0, 0)  20.9 us
    all_to_all x1, blocking collectives, on_device(): blocks = lax.all_to_all(packed, ('x', 'y'), 0, 0)  16.9 us
    all_to_all x1, blocking collectives, on_device(): lines = lax.all_to_all(middle, ('zh', 'zl'), 0, 0)  14.2 us
    all_to_all x1, blocking collectives, on_device(): own = lax.all_to_all(summed, ('x', 'y'), 0, 0)  13.2 us
    pallas_call x1, Pallas kernels, on_device(): call(forward_kernel, 'forward', [shape(16, 16, 256, dtype=BF), shape(22,...  4.37 us
    ppermute x1, starting transfers between devices, on_device(): other = lax.ppermute(own, 'c', SWAP)  4.07 us
    pallas_call x1, Pallas kernels, on_device(): spread(spread_other_kernel, 'spread_other', [shape(9, 256, 256), shape(64...  2.38 us
    pallas_call x1, Pallas kernels, on_device(): spread(spread_own_kernel, 'spread_own', [shape(9, 256, 256), shape(2, 256...  2.2 us
  transfers between devices with their start and end apart: 3, of which 1 were waited for; matrix products, arithmetic and copies ran while one was open for 0% of the time, Pallas kernels for 4%

profile of v4, /device:TPU:1, one launch (start us, length us, event | category | flops | bytes accessed | tf_op | source)
XLA Modules:
  0.0 85.8 jit_solution(17748423339774256970)
XLA Ops:
  0.6 0.1 stack.27.place_ref
  0.7 4.4 %forward.1 = (bf16[16,16,256]{2,1,0:T(8,128)(2,1)S(1)}, f32[22,64,256]{2,1,0:T(8,128)S(1)}, bf16[2,768,768]{2,1,0:T(8,128)(2,1)S(1)}) custom-call(s32[6]{0:T(128)S(1)} %stack.27.place_ref, s32[2,176]{1,0:T(2,128)} %valid_hbm.1, bf16[2,256]{1,0:T(2,128)(2,1)} %grad_ref.1, bf16[1024,256]{1,0:T(8,128)(2,1)} %join_ref.1, bf16[22,64,256]{2,1,0:T(8,128)(2,1)} %bitcast.7, ...), custom_call_target="tpu_custom_call" | custom-call | flops 1200000000 | bytes 3000000 | tf_op jit(solution)/shard_map/forward/forward/pallas_call | solution.py:304
  5.1 0.0 copy-start
  5.1 20.9 %all_to_all.20.grad_ref.got_ref = bf16[16,16,256]{2,1,0:T(8,128)(2,1)S(1)} all-to-all(bf16[16,16,256]{2,1,0:T(8,128)(2,1)S(1)} %get-tuple-element.18), channel_id=1, replica_groups=mesh['zl'=2,'x'=4,'c'=2,'zh'=4,'y'=4] {'zh','y'}, dimensions={0} | all-to-all | bytes 262144 | tf_op jit(solution)/shard_map/forward/all_to_all | solution.py:320
  26.0 0.8 backward_send.1
  26.9 0.0 copy-start.1
  26.9 2.2 %collective-permute-start = (bf16[2304,128]{1,0:T(8,128)(2,1)S(1)}, bf16[2304,128]{1,0:T(8,128)(2,1)S(1)}, u32[]{:S(2)}, u32[]{:S(2)}) collective-permute-start(bf16[2304,128]{1,0:T(8,128)(2,1)S(1)} %get-tuple-element.22), channel_id=1, source_target_pairs={{0,16},{16,0},{1,17},{17,1},{2,18},{18,2},{3,19},{19,3},{4,20},{20... | collective-permute-start | bytes 1769480 | tf_op jit(solution)/shard_map/backward/ppermute | solution.py:331
  29.1 0.0 copy-done
  29.1 0.8 backward_mine.1
  29.9 0.8 collective-permute-done.got_ref
  30.7 0.0 copy-done.1
  30.7 0.8 pack.1
  31.5 16.9 %all_to_all.21.got_ref = bf16[16,160,128]{2,1,0:T(8,128)(2,1)S(1)} all-to-all(bf16[16,160,128]{2,1,0:T(8,128)(2,1)S(1)} %pack.1), channel_id=1, replica_groups=mesh['zl'=2,'x'=4,'c'=2,'zh'=4,'y'=4] {'x','y'}, dimensions={0} | all-to-all | bytes 1310720 | tf_op jit(solution)/shard_map/conv_scatter/all_to_all | solution.py:348
  48.4 0.7 middle.1
  49.1 14.2 %all_to_all.22.got_ref = bf16[8,176,128]{2,1,0:T(8,128)(2,1)S(1)} all-to-all(bf16[8,176,128]{2,1,0:T(8,128)(2,1)S(1)} %middle.1), channel_id=1, replica_groups=mesh['zl'=2,'x'=4,'c'=2,'zh'=4,'y'=4] {'zh','zl'}, dimensions={0} | all-to-all | bytes 720896 | tf_op jit(solution)/shard_map/conv_middle/all_to_all | solution.py:354
  63.3 0.6 finish.1
  63.9 13.2 %all_to_all.23.own_ref = bf16[16,152,128]{2,1,0:T(8,128)(2,1)S(1)} all-to-all(bf16[16,152,128]{2,1,0:T(8,128)(2,1)S(1)} %get-tuple-element.25), channel_id=1, replica_groups=mesh['zl'=2,'x'=4,'c'=2,'zh'=4,'y'=4] {'x','y'}, dimensions={0} | all-to-all | bytes 1245184 | tf_op jit(solution)/shard_map/conv_gather/all_to_all | solution.py:364
  77.1 4.1 %collective-permute-start.1 = (bf16[16,152,128]{2,1,0:T(8,128)(2,1)S(1)}, bf16[16,152,128]{2,1,0:T(8,128)(2,1)S(1)}, u32[]{:S(2)}, u32[]{:S(2)}) collective-permute-start(bf16[16,152,128]{2,1,0:T(8,128)(2,1)S(1)} %all_to_all.23.own_ref), channel_id=1, source_target_pairs={{0,16},{16,0},{1,17},{17,1},{2,18},{18,2},{3,19},{19,3},{4,20},{20... | collective-permute-start | bytes 1867784 | tf_op jit(solution)/shard_map/conv_gather/ppermute | solution.py:365
  81.2 0.0 collective-permute-start.2
  81.2 2.2 %spread_own.1 = (f32[9,256,256]{2,1,0:T(8,128)}, f32[2,256]{1,0:T(2,128)}) custom-call(s32[6]{0:T(128)S(1)} %stack.27.place_ref, bf16[16,152,128]{2,1,0:T(8,128)(2,1)S(1)} %all_to_all.23.own_ref), custom_call_target="tpu_custom_call" | custom-call | flops 1000000 | bytes 2000000 | tf_op jit(solution)/shard_map/conv_gather/spread_own/pallas_call | solution.py:366
  83.4 0.0 collective-permute-done.2.rest_other_ref
  83.4 0.0 collective-permute-done.1.other_ref
  83.4 2.4 %spread_other.1 = (f32[9,256,256]{2,1,0:T(8,128)}, f32[64,256]{1,0:T(8,128)}) custom-call(s32[6]{0:T(128)S(1)} %stack.27.place_ref, bf16[16,152,128]{2,1,0:T(8,128)(2,1)S(1)} %collective-permute-done.1.other_ref, bf16[16,384]{1,0:T(8,128)(2,1)S(1)} %get-tuple-element.27.rest_ref, ...), custom_call_target="tpu_custom_call", output_to_operand_aliasing={{0}: (4, {})} | custom-call | flops 1000000 | bytes 2000000 | tf_op jit(solution)/shard_map/end/spread_other/pallas_call | solution.py:372
Async XLA Ops:
  5.1 24.0 %copy-start = (bf16[1024,256]{1,0:T(8,128)(2,1)S(1)}, bf16[1024,256]{1,0:T(8,128)(2,1)}, u32[]{:S(2)}) copy-start(bf16[1024,256]{1,0:T(8,128)(2,1)} %join_ref.1) | copy-start | bytes 1572868
  26.9 3.8 %copy-start.1 = (bf16[2,256]{1,0:T(2,128)(2,1)S(1)}, bf16[2,256]{1,0:T(2,128)(2,1)}, u32[]{:S(2)}) copy-start(bf16[2,256]{1,0:T(2,128)(2,1)} %grad_ref.1) | copy-start | bytes 3076
  26.9 3.8 %collective-permute-start = (bf16[2304,128]{1,0:T(8,128)(2,1)S(1)}, bf16[2304,128]{1,0:T(8,128)(2,1)S(1)}, u32[]{:S(2)}, u32[]{:S(2)}) collective-permute-start(bf16[2304,128]{1,0:T(8,128)(2,1)S(1)} %get-tuple-element.22), channel_id=1, source_target_pairs={{0,16},{16,0},{1,17},{17,1},{2,18},{18,2},{3,19},{19,3},{4,20},{20... | collective-permute-start | bytes 1769480 | tf_op jit(solution)/shard_map/backward/ppermute | solution.py:331
  77.1 6.3 %collective-permute-start.1 = (bf16[16,152,128]{2,1,0:T(8,128)(2,1)S(1)}, bf16[16,152,128]{2,1,0:T(8,128)(2,1)S(1)}, u32[]{:S(2)}, u32[]{:S(2)}) collective-permute-start(bf16[16,152,128]{2,1,0:T(8,128)(2,1)S(1)} %all_to_all.23.own_ref), channel_id=1, source_target_pairs={{0,16},{16,0},{1,17},{17,1},{2,18},{18,2},{3,19},{19,3},{4,20},{20... | collective-permute-start | bytes 1867784 | tf_op jit(solution)/shard_map/conv_gather/ppermute | solution.py:365
  81.2 2.2 %collective-permute-start.2 = (bf16[16,384]{1,0:T(8,128)(2,1)S(1)}, bf16[16,384]{1,0:T(8,128)(2,1)S(1)}, u32[]{:S(2)}, u32[]{:S(2)}) collective-permute-start(bf16[16,384]{1,0:T(8,128)(2,1)S(1)} %get-tuple-element.27.rest_ref), channel_id=1, source_target_pairs={{0,16},{16,0},{1,17},{17,1},{2,18},{18,2},{3,19},{19,3},{4,20},{20... | collective-permute-start | bytes 36872 | tf_op jit(solution)/shard_map/end/ppermute | solution.py:371

commit v5 on v4

--- a/solution.py
+++ b/solution.py
@@ -10,6 +10,7 @@
 BF = jnp.bfloat16
 F32 = jnp.float32
 SWAP = [(0, 1), (1, 0)]
+BLOCK = ("zl", "x", "y")
 KDIM = 768
 
 VM = pl.BlockSpec(memory_space=pltpu.VMEM)
@@ -164,101 +165,85 @@
         latent_ref[j : j + 1, :] = sum(parts[pos][4 * j + pos : 4 * j + pos + 1] for pos in range(4))
 
 
-def pack_kernel(place_ref, mine_ref, got_ref, joined_ref, latent_ref, grad_ref, out_ref, tail):
-    total = (mine_ref[...] + got_ref[...].astype(F32)).astype(BF)
-    out_ref[:, 0:144, :] = total.reshape(16, 144, 128)
+def pack_kernel(place_ref, mine_ref, got_ref, joined_ref, latent_ref, grad_ref, out_ref, last):
+    head = (mine_ref[0:2048] + got_ref[0:2048].astype(F32)).astype(BF)
+    out_ref[:, 0:64, :] = head.reshape(32, 64, 128)
+    foot = mine_ref[2048:2304] + got_ref[2048:2304].astype(F32)
     grad = grad_ref[...].astype(F32)
-    tail[...] = jnp.zeros((16, 128), F32)
+    last[...] = jnp.zeros((16, 128), F32)
     for j in range(2):
         for h in range(2):
-            tail[5 + 2 * j + h : 6 + 2 * j + h, :] = grad[j : j + 1, 128 * h : 128 * h + 128]
-    for x in range(4):
-        own = jnp.where(place_ref[2] == x, 1.0, 0.0)
+            last[11 + 2 * j + h : 12 + 2 * j + h, :] = grad[j : j + 1, 128 * h : 128 * h + 128]
+    for z in range(2):
+        for x in range(4):
+            t = 4 * z + x
+            lanes = slice(128 * (t % 2), 128 * (t % 2) + 128)
+            for j in range(2):
+                row = 4 * j + t // 2
+                last[9 + j : 10 + j, :] = joined_ref[row : row + 1, lanes]
+            own = jnp.where(jnp.logical_and(place_ref[2] == x, place_ref[4] == z), 1.0, 0.0)
+            for y in range(4):
+                b = 4 * t + y
+                last[0:8, :] = foot[8 * b : 8 * b + 8]
+                last[8:9, :] = latent_ref[y // 2 : y // 2 + 1, 128 * (y % 2) : 128 * (y % 2) + 128] * own
+                out_ref[b, 64:80, :] = last[...].astype(BF)
+
+
+def middle_kernel(place_ref, got_ref, out_ref, rest_ref, rows_ref):
+    head = jnp.sum(got_ref[:, 0:64, :].astype(F32), axis=0).astype(BF)
+    foot = jnp.sum(got_ref[:, 64:80, :].astype(F32), axis=0).astype(BF)
+    for z in range(4):
+        out_ref[z, 0:64, :] = head
+        out_ref[z, 64:80, :] = foot
+    for k in range(8):
+        last = got_ref[4 * k + place_ref[3], 64:80, :].astype(F32)
         for j in range(2):
-            for z in range(2):
-                t = 4 * z + x
-                row = 4 * j + t // 2
-                lanes = slice(128 * (t % 2), 128 * (t % 2) + 128)
-                tail[1 + 2 * j + z : 2 + 2 * j + z, :] = joined_ref[row : row + 1, lanes]
-        for y in range(4):
-            tail[0:1, :] = latent_ref[y // 2 : y // 2 + 1, 128 * (y % 2) : 128 * (y % 2) + 128] * own
-            out_ref[4 * x + y, 144:160, :] = tail[...].astype(BF)
-
-
-def middle_kernel(place_ref, got_ref, out_ref, ends):
-    own_y = place_ref[3]
-    conv = jnp.sum(got_ref[:, 0:144, :].astype(F32), axis=0)
-    end = jnp.sum(got_ref[:, 144:160, :].astype(F32), axis=0)
-    ends[...] = jnp.zeros((2, 32, 128), F32)
-    for x in range(4):
-        block = got_ref[4 * x + own_y, 144:160, :].astype(F32)
-        for z in range(2):
-            for j in range(2):
-                ends[z, 1 + 2 * x + j : 2 + 2 * x + j, :] = block[1 + 2 * j + z : 2 + 2 * j + z]
-            ends[z, 9 + 4 * x : 13 + 4 * x, :] = block[5:9]
-    for z in range(2):
-        ends[z, 0:1, :] = end[0:1]
-    conv = conv.astype(BF)
-    for z in range(8):
-        out_ref[z, 0:144, :] = conv
-        out_ref[z, 144:176, :] = ends[z % 2].astype(BF)
-
-
-def finish_kernel(place_ref, got_ref, out_ref, rest_ref, rows_ref):
-    own_high, own_low = place_ref[4], place_ref[5]
-    conv = jnp.sum(got_ref[:, 0:144, :].astype(F32), axis=0).astype(BF)
-    latent = jnp.zeros((8, 128), F32)
-    for z in range(4):
-        latent = latent + got_ref[2 * z + own_low, 144:176, :].astype(F32)[0:8]
-    latent = latent.astype(BF)
-    for k in range(16):
-        out_ref[k, 0:144, :] = conv
-        out_ref[k, 144:152, :] = latent
-    for z in range(2):
-        block = got_ref[2 * own_high + z, 144:176, :].astype(F32)
-        rows_ref[8 * z : 8 * z + 8, 0:128] = block[1:9]
-        for x in range(4):
-            for j in range(2):
-                for h in range(2):
-                    row = 9 + 4 * x + 2 * j + h
-                    at = 8 * z + 2 * x + j
-                    rows_ref[at : at + 1, 128 + 128 * h : 256 + 128 * h] = block[row : row + 1]
+            at = slice(2 * k + j, 2 * k + j + 1)
+            rows_ref[at, 0:128] = last[9 + j : 10 + j]
+            for h in range(2):
+                row = 11 + 2 * j + h
+                rows_ref[at, 128 + 128 * h : 256 + 128 * h] = last[row : row + 1]
     rest_ref[...] = rows_ref[...].astype(BF)
 
 
-def spread_half(ref, half, conv_hbm, slabs, sems):
-    copies = []
-    for t in range(9):
-        for g in range(16 * t, 16 * t + 16):
-            s, i, offset = g // 8, 16 * (g % 8), 16 * (g % 9)
-            lanes = slice(128 * (s % 2), 128 * (s % 2) + 128)
-            slabs[t, i : i + 16, lanes] = ref[g // 9, offset : offset + 16, :].astype(F32)
-        rows = pl.ds(pl.multiple_of(128 * half, 128), 128)
-        copies.append(pltpu.make_async_copy(slabs.at[t], conv_hbm.at[t, rows], sems.at[t]))
-        copies[t].start()
-    return copies
-
-
-def spread_own_kernel(place_ref, own_ref, conv_hbm, latent_ref, slabs, sems):
-    copies = spread_half(own_ref, place_ref[0], conv_hbm, slabs, sems)
+def finish_kernel(got_ref, out_ref):
+    total = jnp.sum(got_ref[...].astype(F32), axis=0).astype(BF)
+    for b in range(32):
+        out_ref[b] = total
+
+
+def spread_half(ref, half, conv_hbm, slabs, sem):
+    for b in range(32):
+        s, i = b // 2, 64 * (b % 2)
+        lanes = slice(128 * (s % 2), 128 * (s % 2) + 128)
+        slabs[s // 2, i : i + 64, lanes] = ref[b, 0:64, :].astype(F32)
+        s, i = b // 16, 8 * (b % 16)
+        slabs[8, i : i + 8, 128 * s : 128 * s + 128] = ref[b, 64:80, :].astype(F32)[0:8]
+    rows = pl.ds(pl.multiple_of(128 * half, 128), 128)
+    copy = pltpu.make_async_copy(slabs, conv_hbm.at[:, rows], sem)
+    copy.start()
+    return copy
+
+
+def spread_own_kernel(place_ref, own_ref, conv_hbm, latent_ref, slabs, sem):
+    copy = spread_half(own_ref, place_ref[0], conv_hbm, slabs, sem)
+    first = 16 * place_ref[4] + 4 * place_ref[2]
     for y in range(4):
-        row = own_ref[4 * place_ref[2] + y, 144:152, :].astype(F32)[0:1]
+        row = own_ref[first + y, 64:80, :].astype(F32)[8:9]
         latent_ref[y // 2 : y // 2 + 1, 128 * (y % 2) : 128 * (y % 2) + 128] = row
-    for copy in copies:
-        copy.wait()
-
-
-def spread_other_kernel(place_ref, other_ref, rest_ref, rest_other_ref, begun_hbm, conv_hbm, join_ref, slabs, sems):
+    copy.wait()
+
+
+def spread_other_kernel(place_ref, other_ref, rest_ref, rest_other_ref, begun_hbm, conv_hbm, join_ref, slabs, sem):
     core = place_ref[0]
-    copies = spread_half(other_ref, 1 - core, conv_hbm, slabs, sems)
+    copy = spread_half(other_ref, 1 - core, conv_hbm, slabs, sem)
     total = jnp.zeros((64, 256), F32)
     for ref in (rest_ref, rest_other_ref):
         rows = ref[...]
         joined = jnp.where(core == 0, rows[:, 0:64], rows[:, 64:128])
         total = total + lax.dot_general(joined, rows[:, 128:384], (((0,), (0,)), ((), ())), preferred_element_type=F32)
     join_ref[...] = total
-    for copy in copies:
-        copy.wait()
+    copy.wait()
 
 
 def spread(kernel, name, out_shape, in_specs, aliases):
@@ -267,7 +252,7 @@
         out_shape=out_shape,
         in_specs=in_specs,
         out_specs=[HBM, VM],
-        scratch_shapes=[pltpu.VMEM((9, 128, 256), F32), pltpu.SemaphoreType.DMA((9,))],
+        scratch_shapes=[pltpu.VMEM((9, 128, 256), F32), pltpu.SemaphoreType.DMA],
         input_output_aliases=aliases,
         compiler_params=params(),
         cost_estimate=pl.CostEstimate(flops=1_000_000, bytes_accessed=2_000_000, transcendentals=0),
@@ -297,7 +282,7 @@
 
 
 def on_device(view_maps, conv_weight, join_weight, valid_cams, latent_grad):
-    names = ("c", ("zh", "y"), "x", "y", "zh", "zl")
+    names = ("c", ("zh", "y"), "x", "y", "zl")
     place = jnp.stack([lax.axis_index(name).astype(jnp.int32) for name in names])
 
     with jax.named_scope("forward"):
@@ -341,27 +326,25 @@
         (packed,) = call(
             pack_kernel,
             "pack",
-            [shape(16, 160, 128, dtype=BF)],
+            [shape(32, 80, 128, dtype=BF)],
             [SM, VM, VM, VM, VM, VM],
             [pltpu.VMEM((16, 128), F32)],
         )(place, mine, got, joined, latent_part, latent_grad)
-        blocks = lax.all_to_all(packed, ("x", "y"), 0, 0)
+        blocks = lax.all_to_all(packed, BLOCK, 0, 0)
 
     with jax.named_scope("conv_middle"):
-        (middle,) = call(
-            middle_kernel, "middle", [shape(8, 176, 128, dtype=BF)], [SM, VM], [pltpu.VMEM((2, 32, 128), F32)]
-        )(place, blocks)
-        lines = lax.all_to_all(middle, ("zh", "zl"), 0, 0)
-
-    with jax.named_scope("conv_gather"):
-        summed, rest = call(
-            finish_kernel,
-            "finish",
-            [shape(16, 152, 128, dtype=BF), shape(16, 384, dtype=BF)],
+        middle, rest = call(
+            middle_kernel,
+            "middle",
+            [shape(4, 80, 128, dtype=BF), shape(16, 384, dtype=BF)],
             [SM, VM],
             [pltpu.VMEM((16, 384), F32)],
-        )(place, lines)
-        own = lax.all_to_all(summed, ("x", "y"), 0, 0)
+        )(place, blocks)
+        lines = lax.all_to_all(middle, "zh", 0, 0)
+
+    with jax.named_scope("conv_gather"):
+        (summed,) = call(finish_kernel, "finish", [shape(32, 80, 128, dtype=BF)], [VM])(lines)
+        own = lax.all_to_all(summed, BLOCK, 0, 0)
         other = lax.ppermute(own, "c", SWAP)
         begun, latent = spread(
             spread_own_kernel, "spread_own", [shape(9, 256, 256), shape(2, 256)], [SM, VM], {}

time: 86.1 us -> 82.3 us (0.956)
  blocking collectives: 65.2 us -> 61.6 us
    all_to_all x3, blocking collectives: 44.3 us -> 40.7 us  [the longest x1 17 us: on_device(): blocks = lax.all_to_all(packed, BLOCK, 0, 0)]
where the time goes in v5:
time: 82.3 us; the launch traced here: 82 us
  blocking collectives  61.6 us (75%)
  Pallas kernels  12.2 us (15%)
  starting transfers between devices  6.51 us (8%)
    all_to_all x1, blocking collectives, on_device(): cam_shares = lax.all_to_all(shares, ('zh', 'y'), 0, 0)  20.9 us
    all_to_all x1, blocking collectives, on_device(): blocks = lax.all_to_all(packed, BLOCK, 0, 0)  17 us
    all_to_all x1, blocking collectives, on_device(): own = lax.all_to_all(summed, BLOCK, 0, 0)  14.2 us
    all_to_all x1, blocking collectives, on_device(): lines = lax.all_to_all(middle, 'zh', 0, 0)  9.44 us
    pallas_call x1, Pallas kernels, on_device(): call(forward_kernel, 'forward', [shape(16, 16, 256, dtype=BF), shape(22,...  4.37 us
    ppermute x1, starting transfers between devices, on_device(): other = lax.ppermute(own, 'c', SWAP)  4.31 us
    pallas_call x1, Pallas kernels, on_device(): spread(spread_other_kernel, 'spread_other', [shape(9, 256, 256), shape(64...  2.39 us
    pallas_call x1, Pallas kernels, on_device(): spread(spread_own_kernel, 'spread_own', [shape(9, 256, 256), shape(2, 256...  2.22 us
  transfers between devices with their start and end apart: 3, of which 1 were waited for; matrix products, arithmetic and copies ran while one was open for 0% of the time, Pallas kernels for 4%

profile of v5, /device:TPU:1, one launch (start us, length us, event | category | flops | bytes accessed | tf_op | source)
XLA Modules:
  0.0 82.0 jit_solution(8926756723011677813)
XLA Ops:
  0.6 0.1 stack.23.place_ref
  0.7 4.4 %forward.1 = (bf16[16,16,256]{2,1,0:T(8,128)(2,1)S(1)}, f32[22,64,256]{2,1,0:T(8,128)S(1)}, bf16[2,768,768]{2,1,0:T(8,128)(2,1)S(1)}) custom-call(s32[5]{0:T(128)S(1)} %stack.23.place_ref, s32[2,176]{1,0:T(2,128)} %valid_hbm.1, bf16[2,256]{1,0:T(2,128)(2,1)} %grad_ref.1, bf16[1024,256]{1,0:T(8,128)(2,1)} %join_ref.1, bf16[22,64,256]{2,1,0:T(8,128)(2,1)} %bitcast.6, ...), custom_call_target="tpu_custom_call" | custom-call | flops 1200000000 | bytes 3000000 | tf_op jit(solution)/shard_map/forward/forward/pallas_call | solution.py:289
  5.1 0.0 copy-start
  5.1 20.9 %all_to_all.20.grad_ref.got_ref = bf16[16,16,256]{2,1,0:T(8,128)(2,1)S(1)} all-to-all(bf16[16,16,256]{2,1,0:T(8,128)(2,1)S(1)} %get-tuple-element.18), channel_id=1, replica_groups=mesh['zl'=2,'x'=4,'c'=2,'zh'=4,'y'=4] {'zh','y'}, dimensions={0} | all-to-all | bytes 262144 | tf_op jit(solution)/shard_map/forward/all_to_all | solution.py:305
  26.0 0.8 backward_send.1
  26.9 0.0 copy-start.1
  26.9 2.2 %collective-permute-start = (bf16[2304,128]{1,0:T(8,128)(2,1)S(1)}, bf16[2304,128]{1,0:T(8,128)(2,1)S(1)}, u32[]{:S(2)}, u32[]{:S(2)}) collective-permute-start(bf16[2304,128]{1,0:T(8,128)(2,1)S(1)} %get-tuple-element.22), channel_id=1, source_target_pairs={{0,16},{16,0},{1,17},{17,1},{2,18},{18,2},{3,19},{19,3},{4,20},{20... | collective-permute-start | bytes 1769480 | tf_op jit(solution)/shard_map/backward/ppermute | solution.py:316
  29.1 0.0 copy-done
  29.1 0.8 backward_mine.1
  29.9 0.8 collective-permute-done.got_ref
  30.7 0.0 copy-done.1
  30.7 0.9 %pack.1 = bf16[32,80,128]{2,1,0:T(8,128)(2,1)S(1)} custom-call(s32[5]{0:T(128)S(1)} %stack.23.place_ref, f32[2304,128]{1,0:T(8,128)S(1)} %get-tuple-element.21.mine_ref, bf16[2304,128]{1,0:T(8,128)(2,1)S(1)} %collective-permute-done.got_ref, f32[8,256]{1,0:T(8,128)S(1)} %get-tuple-element.23.joined_ref, f32[2,256]{1,0:T(2,128)S(1)} %get-tuple-element.24.latent_ref, ...), custom_call_target="tpu_custom_call" | custom-call | flops 1000000 | bytes 3000000 | tf_op jit(solution)/shard_map/conv_scatter/pack/pallas_call | solution.py:326
  31.6 17.0 %all_to_all.21.got_ref = bf16[32,80,128]{2,1,0:T(8,128)(2,1)S(1)} all-to-all(bf16[32,80,128]{2,1,0:T(8,128)(2,1)S(1)} %pack.1), channel_id=1, replica_groups=mesh['zl'=2,'x'=4,'c'=2,'zh'=4,'y'=4] {'zl','x','y'}, dimensions={0} | all-to-all | bytes 1310720 | tf_op jit(solution)/shard_map/conv_scatter/all_to_all | solution.py:333
  48.7 0.7 middle.1
  49.3 9.4 %all_to_all.22.got_ref = bf16[4,80,128]{2,1,0:T(8,128)(2,1)S(1)} all-to-all(bf16[4,80,128]{2,1,0:T(8,128)(2,1)S(1)} %get-tuple-element.25), channel_id=1, replica_groups=mesh['zl'=2,'x'=4,'c'=2,'zh'=4,'y'=4] {'zh'}, dimensions={0} | all-to-all | bytes 163840 | tf_op jit(solution)/shard_map/conv_middle/all_to_all | solution.py:343
  58.8 14.2 %all_to_all.23.own_ref = bf16[32,80,128]{2,1,0:T(8,128)(2,1)S(1)} all-to-all(bf16[32,80,128]{2,1,0:T(8,128)(2,1)S(1)} %finish.1), channel_id=1, replica_groups=mesh['zl'=2,'x'=4,'c'=2,'zh'=4,'y'=4] {'zl','x','y'}, dimensions={0} | all-to-all | bytes 1310720 | tf_op jit(solution)/shard_map/conv_gather/all_to_all | solution.py:347
  73.1 4.3 %collective-permute-start.1 = (bf16[32,80,128]{2,1,0:T(8,128)(2,1)S(1)}, bf16[32,80,128]{2,1,0:T(8,128)(2,1)S(1)}, u32[]{:S(2)}, u32[]{:S(2)}) collective-permute-start(bf16[32,80,128]{2,1,0:T(8,128)(2,1)S(1)} %all_to_all.23.own_ref), channel_id=1, source_target_pairs={{0,16},{16,0},{1,17},{17,1},{2,18},{18,2},{3,19},{19,3},{4,20},{20... | collective-permute-start | bytes 1966088 | tf_op jit(solution)/shard_map/conv_gather/ppermute | solution.py:348
  77.4 0.0 collective-permute-start.2
  77.4 2.2 %spread_own.1 = (f32[9,256,256]{2,1,0:T(8,128)}, f32[2,256]{1,0:T(2,128)}) custom-call(s32[5]{0:T(128)S(1)} %stack.23.place_ref, bf16[32,80,128]{2,1,0:T(8,128)(2,1)S(1)} %all_to_all.23.own_ref), custom_call_target="tpu_custom_call" | custom-call | flops 1000000 | bytes 2000000 | tf_op jit(solution)/shard_map/conv_gather/spread_own/pallas_call | solution.py:349
  79.6 0.0 collective-permute-done.2.rest_other_ref
  79.6 0.0 collective-permute-done.1.other_ref
  79.6 2.4 %spread_other.1 = (f32[9,256,256]{2,1,0:T(8,128)}, f32[64,256]{1,0:T(8,128)}) custom-call(s32[5]{0:T(128)S(1)} %stack.23.place_ref, bf16[32,80,128]{2,1,0:T(8,128)(2,1)S(1)} %collective-permute-done.1.other_ref, bf16[16,384]{1,0:T(8,128)(2,1)S(1)} %get-tuple-element.27.rest_ref, ...), custom_call_target="tpu_custom_call", output_to_operand_aliasing={{0}: (4, {})} | custom-call | flops 1000000 | bytes 2000000 | tf_op jit(solution)/shard_map/end/spread_other/pallas_call | solution.py:355
  (1 shorter events, 0.0 us)
Async XLA Ops:
  5.1 24.0 %copy-start = (bf16[1024,256]{1,0:T(8,128)(2,1)S(1)}, bf16[1024,256]{1,0:T(8,128)(2,1)}, u32[]{:S(2)}) copy-start(bf16[1024,256]{1,0:T(8,128)(2,1)} %join_ref.1) | copy-start | bytes 1572868
  26.9 3.8 %copy-start.1 = (bf16[2,256]{1,0:T(2,128)(2,1)S(1)}, bf16[2,256]{1,0:T(2,128)(2,1)}, u32[]{:S(2)}) copy-start(bf16[2,256]{1,0:T(2,128)(2,1)} %grad_ref.1) | copy-start | bytes 3076
  26.9 3.8 %collective-permute-start = (bf16[2304,128]{1,0:T(8,128)(2,1)S(1)}, bf16[2304,128]{1,0:T(8,128)(2,1)S(1)}, u32[]{:S(2)}, u32[]{:S(2)}) collective-permute-start(bf16[2304,128]{1,0:T(8,128)(2,1)S(1)} %get-tuple-element.22), channel_id=1, source_target_pairs={{0,16},{16,0},{1,17},{17,1},{2,18},{18,2},{3,19},{19,3},{4,20},{20... | collective-permute-start | bytes 1769480 | tf_op jit(solution)/shard_map/backward/ppermute | solution.py:316
  73.1 6.6 %collective-permute-start.1 = (bf16[32,80,128]{2,1,0:T(8,128)(2,1)S(1)}, bf16[32,80,128]{2,1,0:T(8,128)(2,1)S(1)}, u32[]{:S(2)}, u32[]{:S(2)}) collective-permute-start(bf16[32,80,128]{2,1,0:T(8,128)(2,1)S(1)} %all_to_all.23.own_ref), channel_id=1, source_target_pairs={{0,16},{16,0},{1,17},{17,1},{2,18},{18,2},{3,19},{19,3},{4,20},{20... | collective-permute-start | bytes 1966088 | tf_op jit(solution)/shard_map/conv_gather/ppermute | solution.py:348
  77.4 2.2 %collective-permute-start.2 = (bf16[16,384]{1,0:T(8,128)(2,1)S(1)}, bf16[16,384]{1,0:T(8,128)(2,1)S(1)}, u32[]{:S(2)}, u32[]{:S(2)}) collective-permute-start(bf16[16,384]{1,0:T(8,128)(2,1)S(1)} %get-tuple-element.27.rest_ref), channel_id=1, source_target_pairs={{0,16},{16,0},{1,17},{17,1},{2,18},{18,2},{3,19},{19,3},{4,20},{20... | collective-permute-start | bytes 36872 | tf_op jit(solution)/shard_map/end/ppermute | solution.py:354

commit v6 on v5

--- a/solution.py
+++ b/solution.py
@@ -14,7 +14,6 @@
 KDIM = 768
 
 VM = pl.BlockSpec(memory_space=pltpu.VMEM)
-SM = pl.BlockSpec(memory_space=pltpu.SMEM)
 HBM = pl.BlockSpec(memory_space=pltpu.HBM)
 
 
@@ -32,7 +31,7 @@
 
 
 def forward_kernel(
-    place_ref, valid_hbm, grad_hbm, join_hbm, maps_hbm, conv_hbm,
+    valid_hbm, grad_hbm, join_hbm, maps_hbm, conv_hbm,
     out_ref, slope_ref, turned_ref,
     valid_ref, grad_ref, join_ref, maps_ref, conv_ref, rows_ref, sems,
 ):
@@ -50,7 +49,7 @@
     ]
     for load in loads:
         load.start()
-    core, cam = place_ref[0], place_ref[1]
+    core, cam = lax.axis_index("c"), lax.axis_index("zh") * 4 + lax.axis_index("y")
     loads[0].wait()
     valid = valid_ref[...].astype(F32)
     count = jnp.sum(valid, axis=1, keepdims=True)
@@ -165,12 +164,13 @@
         latent_ref[j : j + 1, :] = sum(parts[pos][4 * j + pos : 4 * j + pos + 1] for pos in range(4))
 
 
-def pack_kernel(place_ref, mine_ref, got_ref, joined_ref, latent_ref, grad_ref, out_ref, last):
+def pack_kernel(mine_ref, got_ref, joined_ref, latent_ref, grad_ref, out_ref, last):
     head = (mine_ref[0:2048] + got_ref[0:2048].astype(F32)).astype(BF)
     out_ref[:, 0:64, :] = head.reshape(32, 64, 128)
     foot = mine_ref[2048:2304] + got_ref[2048:2304].astype(F32)
     grad = grad_ref[...].astype(F32)
     last[...] = jnp.zeros((16, 128), F32)
+    own_x, own_z = lax.axis_index("x"), lax.axis_index("zl")
     for j in range(2):
         for h in range(2):
             last[11 + 2 * j + h : 12 + 2 * j + h, :] = grad[j : j + 1, 128 * h : 128 * h + 128]
@@ -181,7 +181,7 @@
             for j in range(2):
                 row = 4 * j + t // 2
                 last[9 + j : 10 + j, :] = joined_ref[row : row + 1, lanes]
-            own = jnp.where(jnp.logical_and(place_ref[2] == x, place_ref[4] == z), 1.0, 0.0)
+            own = jnp.where(jnp.logical_and(own_x == x, own_z == z), 1.0, 0.0)
             for y in range(4):
                 b = 4 * t + y
                 last[0:8, :] = foot[8 * b : 8 * b + 8]
@@ -189,14 +189,15 @@
                 out_ref[b, 64:80, :] = last[...].astype(BF)
 
 
-def middle_kernel(place_ref, got_ref, out_ref, rest_ref, rows_ref):
+def middle_kernel(got_ref, out_ref, rest_ref, rows_ref):
     head = jnp.sum(got_ref[:, 0:64, :].astype(F32), axis=0).astype(BF)
     foot = jnp.sum(got_ref[:, 64:80, :].astype(F32), axis=0).astype(BF)
+    own_y = lax.axis_index("y")
     for z in range(4):
         out_ref[z, 0:64, :] = head
         out_ref[z, 64:80, :] = foot
     for k in range(8):
-        last = got_ref[4 * k + place_ref[3], 64:80, :].astype(F32)
+        last = got_ref[4 * k + own_y, 64:80, :].astype(F32)
         for j in range(2):
             at = slice(2 * k + j, 2 * k + j + 1)
             rows_ref[at, 0:128] = last[9 + j : 10 + j]
@@ -225,34 +226,40 @@
     return copy
 
 
-def spread_own_kernel(place_ref, own_ref, conv_hbm, latent_ref, slabs, sem):
-    copy = spread_half(own_ref, place_ref[0], conv_hbm, slabs, sem)
-    first = 16 * place_ref[4] + 4 * place_ref[2]
+def spread_own_kernel(own_ref, conv_hbm, latent_hbm, slabs, latent_ref, sems):
+    copy = spread_half(own_ref, lax.axis_index("c"), conv_hbm, slabs, sems.at[0])
+    first = 16 * lax.axis_index("zl") + 4 * lax.axis_index("x")
     for y in range(4):
         row = own_ref[first + y, 64:80, :].astype(F32)[8:9]
         latent_ref[y // 2 : y // 2 + 1, 128 * (y % 2) : 128 * (y % 2) + 128] = row
+    small = pltpu.make_async_copy(latent_ref, latent_hbm, sems.at[1])
+    small.start()
     copy.wait()
-
-
-def spread_other_kernel(place_ref, other_ref, rest_ref, rest_other_ref, begun_hbm, conv_hbm, join_ref, slabs, sem):
-    core = place_ref[0]
-    copy = spread_half(other_ref, 1 - core, conv_hbm, slabs, sem)
+    small.wait()
+
+
+def spread_other_kernel(other_ref, rest_ref, rest_other_ref, begun_hbm, conv_hbm, join_hbm, slabs, join_ref, sems):
+    core = lax.axis_index("c")
+    copy = spread_half(other_ref, 1 - core, conv_hbm, slabs, sems.at[0])
     total = jnp.zeros((64, 256), F32)
     for ref in (rest_ref, rest_other_ref):
         rows = ref[...]
         joined = jnp.where(core == 0, rows[:, 0:64], rows[:, 64:128])
         total = total + lax.dot_general(joined, rows[:, 128:384], (((0,), (0,)), ((), ())), preferred_element_type=F32)
     join_ref[...] = total
+    small = pltpu.make_async_copy(join_ref, join_hbm, sems.at[1])
+    small.start()
     copy.wait()
-
-
-def spread(kernel, name, out_shape, in_specs, aliases):
+    small.wait()
+
+
+def spread(kernel, name, small, in_specs, aliases):
     return pl.pallas_call(
         kernel,
-        out_shape=out_shape,
+        out_shape=[shape(9, 256, 256), shape(*small)],
         in_specs=in_specs,
-        out_specs=[HBM, VM],
-        scratch_shapes=[pltpu.VMEM((9, 128, 256), F32), pltpu.SemaphoreType.DMA],
+        out_specs=[HBM, HBM],
+        scratch_shapes=[pltpu.VMEM((9, 128, 256), F32), pltpu.VMEM(small, F32), pltpu.SemaphoreType.DMA((2,))],
         input_output_aliases=aliases,
         compiler_params=params(),
         cost_estimate=pl.CostEstimate(flops=1_000_000, bytes_accessed=2_000_000, transcendentals=0),
@@ -282,15 +289,12 @@
 
 
 def on_device(view_maps, conv_weight, join_weight, valid_cams, latent_grad):
-    names = ("c", ("zh", "y"), "x", "y", "zl")
-    place = jnp.stack([lax.axis_index(name).astype(jnp.int32) for name in names])
-
     with jax.named_scope("forward"):
         shares, slope, turned = call(
             forward_kernel,
             "forward",
             [shape(16, 16, 256, dtype=BF), shape(22, 64, 256), shape(2, 768, KDIM, dtype=BF)],
-            [SM, HBM, HBM, HBM, HBM, HBM],
+            [HBM, HBM, HBM, HBM, HBM],
             [
                 pltpu.VMEM((2, 176), jnp.int32),
                 pltpu.VMEM((2, 256), BF),
@@ -301,7 +305,7 @@
                 pltpu.SemaphoreType.DMA((5,)),
             ],
             flops=1_200_000_000,
-        )(place, *map(in_hbm, (valid_cams, latent_grad, join_weight, view_maps.reshape(22, 64, 256), conv_weight)))
+        )(*map(in_hbm, (valid_cams, latent_grad, join_weight, view_maps.reshape(22, 64, 256), conv_weight)))
         cam_shares = lax.all_to_all(shares, ("zh", "y"), 0, 0)
 
     with jax.named_scope("backward"):
@@ -327,9 +331,9 @@
             pack_kernel,
             "pack",
             [shape(32, 80, 128, dtype=BF)],
-            [SM, VM, VM, VM, VM, VM],
+            [VM, VM, VM, VM, VM],
             [pltpu.VMEM((16, 128), F32)],
-        )(place, mine, got, joined, latent_part, latent_grad)
+        )(mine, got, joined, latent_part, latent_grad)
         blocks = lax.all_to_all(packed, BLOCK, 0, 0)
 
     with jax.named_scope("conv_middle"):
@@ -337,24 +341,22 @@
             middle_kernel,
             "middle",
             [shape(4, 80, 128, dtype=BF), shape(16, 384, dtype=BF)],
-            [SM, VM],
+            [VM],
             [pltpu.VMEM((16, 384), F32)],
-        )(place, blocks)
+        )(blocks)
         lines = lax.all_to_all(middle, "zh", 0, 0)
 
     with jax.named_scope("conv_gather"):
         (summed,) = call(finish_kernel, "finish", [shape(32, 80, 128, dtype=BF)], [VM])(lines)
         own = lax.all_to_all(summed, BLOCK, 0, 0)
         other = lax.ppermute(own, "c", SWAP)
-        begun, latent = spread(
-            spread_own_kernel, "spread_own", [shape(9, 256, 256), shape(2, 256)], [SM, VM], {}
-        )(place, own)
+        begun, latent = spread(spread_own_kernel, "spread_own", (2, 256), [VM], {})(own)
 
     with jax.named_scope("end"):
         rest_other = lax.ppermute(rest, "c", SWAP)
         conv_grad, join_grad = spread(
-            spread_other_kernel, "spread_other", [shape(9, 256, 256), shape(64, 256)], [SM, VM, VM, VM, HBM], {4: 0}
-        )(place, other, rest, rest_other, begun)
+            spread_other_kernel, "spread_other", (64, 256), [VM, VM, VM, HBM], {3: 0}
+        )(other, rest, rest_other, begun)
     return (latent, conv_grad, join_grad)
 
 

time: 82.3 us -> 78.8 us (0.957)
  Pallas kernels: 12.2 us -> 8.29 us
    pallas_call x3, Pallas kernels: 5.51 us -> 2.71 us  [the longest x1 1.23 us: on_device(): spread(spread_other_kernel, 'spread_other', (64, 256), [VM, VM, VM, HBM],...]
  transfers between devices with their start and end apart: 3 -> 3, of which waited for: 1 -> 2; matrix products, arithmetic and copies ran while one was open for 0% -> 0% of each run, Pallas kernels for 4% -> 2%
where the time goes in v6:
time: 78.8 us; the launch traced here: 78.6 us
  blocking collectives  61.7 us (78%)
  Pallas kernels  8.29 us (11%)
  starting transfers between devices  6.5 us (8%)
  waiting for transfers between devices  1.44 us (2%)
    all_to_all x1, blocking collectives, on_device(): cam_shares = lax.all_to_all(shares, ('zh', 'y'), 0, 0)  20.9 us
    all_to_all x1, blocking collectives, on_device(): blocks = lax.all_to_all(packed, BLOCK, 0, 0)  17.1 us
    all_to_all x1, blocking collectives, on_device(): own = lax.all_to_all(summed, BLOCK, 0, 0)  14.2 us
    all_to_all x1, blocking collectives, on_device(): lines = lax.all_to_all(middle, 'zh', 0, 0)  9.44 us
    ppermute x1, starting transfers between devices, on_device(): other = lax.ppermute(own, 'c', SWAP)  4.31 us
    pallas_call x1, Pallas kernels, on_device(): call(forward_kernel, 'forward', [shape(16, 16, 256, dtype=BF), shape(22,...  3.79 us
    ppermute x1, starting transfers between devices, on_device(): got = lax.ppermute(send, 'c', SWAP)  2.19 us
  transfers between devices with their start and end apart: 3, of which 2 were waited for; matrix products, arithmetic and copies ran while one was open for 0% of the time, Pallas kernels for 2%

profile of v6, /device:TPU:1, one launch (start us, length us, event | category | flops | bytes accessed | tf_op | source)
XLA Modules:
  0.0 78.6 jit_solution(7111649727898923979)
XLA Ops:
  0.6 3.8 %forward.1 = (bf16[16,16,256]{2,1,0:T(8,128)(2,1)S(1)}, f32[22,64,256]{2,1,0:T(8,128)S(1)}, bf16[2,768,768]{2,1,0:T(8,128)(2,1)S(1)}) custom-call(s32[2,176]{1,0:T(2,128)} %valid_hbm.1, bf16[2,256]{1,0:T(2,128)(2,1)} %grad_ref.1, bf16[1024,256]{1,0:T(8,128)(2,1)} %join_ref.1, bf16[22,64,256]{2,1,0:T(8,128)(2,1)} %bitcast.1, bf16[9,256,256]{2,1,0:T(8,128)(2,1)} %conv_hbm.1), custom_call_target="tpu_custom_call" | custom-call | flops 1200000000 | bytes 3000000 | tf_op jit(solution)/shard_map/forward/forward/pallas_call | solution.py:293
  4.4 0.0 copy-start
  4.4 20.9 %all_to_all.20.grad_ref.got_ref = bf16[16,16,256]{2,1,0:T(8,128)(2,1)S(1)} all-to-all(bf16[16,16,256]{2,1,0:T(8,128)(2,1)S(1)} %get-tuple-element.18), channel_id=1, replica_groups=mesh['zl'=2,'x'=4,'c'=2,'zh'=4,'y'=4] {'zh','y'}, dimensions={0} | all-to-all | bytes 262144 | tf_op jit(solution)/shard_map/forward/all_to_all | solution.py:309
  25.4 0.8 %backward_send.1 = (bf16[2,768,256]{2,1,0:T(8,128)(2,1)S(1)}, bf16[2304,128]{1,0:T(8,128)(2,1)S(1)}) custom-call(bf16[16,16,256]{2,1,0:T(8,128)(2,1)S(1)} %all_to_all.20.grad_ref.got_ref, f32[22,64,256]{2,1,0:T(8,128)S(1)} %get-tuple-element.19.slope_ref, bf16[2,768,768]{2,1,0:T(8,128)(2,1)S(1)} %get-tuple-element.17.turned_ref), custom_call_target="tpu_custom_call" | custom-call | flops 600000000 | bytes 3000000 | tf_op jit(solution)/shard_map/backward/backward_send/pallas_call | solution.py:312
  26.2 0.0 copy-start.1
  26.2 2.2 %collective-permute-start = (bf16[2304,128]{1,0:T(8,128)(2,1)S(1)}, bf16[2304,128]{1,0:T(8,128)(2,1)S(1)}, u32[]{:S(2)}, u32[]{:S(2)}) collective-permute-start(bf16[2304,128]{1,0:T(8,128)(2,1)S(1)} %get-tuple-element.22), channel_id=1, source_target_pairs={{0,16},{16,0},{1,17},{17,1},{2,18},{18,2},{3,19},{19,3},{4,20},{20... | collective-permute-start | bytes 1769480 | tf_op jit(solution)/shard_map/backward/ppermute | solution.py:320
  28.4 0.0 copy-done
  28.4 0.8 %backward_mine.1 = (f32[2304,128]{1,0:T(8,128)S(1)}, f32[8,256]{1,0:T(8,128)S(1)}, f32[2,256]{1,0:T(2,128)S(1)}) custom-call(bf16[2,768,768]{2,1,0:T(8,128)(2,1)S(1)} %get-tuple-element.17.turned_ref, bf16[2,768,256]{2,1,0:T(8,128)(2,1)S(1)} %get-tuple-element.20.pre_ref, bf16[16,16,256]{2,1,0:T(8,128)(2,1)S(1)} %all_to_all.20.grad_ref.got_ref, ...), custom_call_target="tpu_custom_call" | custom-call | flops 600000000 | bytes 3000000 | tf_op jit(solution)/shard_map/backward/backward_mine/pallas_call | solution.py:321
  29.2 0.8 %collective-permute-done.got_ref = bf16[2304,128]{1,0:T(8,128)(2,1)S(1)} collective-permute-done((bf16[2304,128]{1,0:T(8,128)(2,1)S(1)}, bf16[2304,128]{1,0:T(8,128)(2,1)S(1)}, u32[]{:S(2)}, u32[]{:S(2)}) %collective-permute-start) | collective-permute-done | bytes 589856 | tf_op jit(solution)/shard_map/backward/ppermute | solution.py:320
  30.0 0.0 copy-done.1
  30.0 0.4 pack.1
  30.4 17.1 %all_to_all.21.got_ref = bf16[32,80,128]{2,1,0:T(8,128)(2,1)S(1)} all-to-all(bf16[32,80,128]{2,1,0:T(8,128)(2,1)S(1)} %pack.1), channel_id=1, replica_groups=mesh['zl'=2,'x'=4,'c'=2,'zh'=4,'y'=4] {'zl','x','y'}, dimensions={0} | all-to-all | bytes 1310720 | tf_op jit(solution)/shard_map/conv_scatter/all_to_all | solution.py:337
  47.4 0.1 middle.1
  47.6 9.4 %all_to_all.22.got_ref = bf16[4,80,128]{2,1,0:T(8,128)(2,1)S(1)} all-to-all(bf16[4,80,128]{2,1,0:T(8,128)(2,1)S(1)} %get-tuple-element.25), channel_id=1, replica_groups=mesh['zl'=2,'x'=4,'c'=2,'zh'=4,'y'=4] {'zh'}, dimensions={0} | all-to-all | bytes 163840 | tf_op jit(solution)/shard_map/conv_middle/all_to_all | solution.py:347
  57.1 14.2 %all_to_all.23.own_ref = bf16[32,80,128]{2,1,0:T(8,128)(2,1)S(1)} all-to-all(bf16[32,80,128]{2,1,0:T(8,128)(2,1)S(1)} %finish.1), channel_id=1, replica_groups=mesh['zl'=2,'x'=4,'c'=2,'zh'=4,'y'=4] {'zl','x','y'}, dimensions={0} | all-to-all | bytes 1310720 | tf_op jit(solution)/shard_map/conv_gather/all_to_all | solution.py:351
  71.3 4.3 %collective-permute-start.1 = (bf16[32,80,128]{2,1,0:T(8,128)(2,1)S(1)}, bf16[32,80,128]{2,1,0:T(8,128)(2,1)S(1)}, u32[]{:S(2)}, u32[]{:S(2)}) collective-permute-start(bf16[32,80,128]{2,1,0:T(8,128)(2,1)S(1)} %all_to_all.23.own_ref), channel_id=1, source_target_pairs={{0,16},{16,0},{1,17},{17,1},{2,18},{18,2},{3,19},{19,3},{4,20},{20... | collective-permute-start | bytes 1966088 | tf_op jit(solution)/shard_map/conv_gather/ppermute | solution.py:352
  75.6 0.0 collective-permute-start.2
  75.6 1.1 %spread_own.1 = (f32[9,256,256]{2,1,0:T(8,128)}, f32[2,256]{1,0:T(2,128)}) custom-call(bf16[32,80,128]{2,1,0:T(8,128)(2,1)S(1)} %all_to_all.23.own_ref), custom_call_target="tpu_custom_call" | custom-call | flops 1000000 | bytes 2000000 | tf_op jit(solution)/shard_map/conv_gather/spread_own/pallas_call | solution.py:353
  76.7 0.6 collective-permute-done.2.rest_other_ref
  77.3 0.0 collective-permute-done.1.other_ref
  77.3 1.2 %spread_other.1 = (f32[9,256,256]{2,1,0:T(8,128)}, f32[64,256]{1,0:T(8,128)}) custom-call(bf16[32,80,128]{2,1,0:T(8,128)(2,1)S(1)} %collective-permute-done.1.other_ref, bf16[16,384]{1,0:T(8,128)(2,1)S(1)} %get-tuple-element.27.rest_ref, bf16[16,384]{1,0:T(8,128)(2,1)S(1)} %collective-permute-done.2.rest_other_ref, ...), custom_call_target="tpu_custom_call", output_to_operand_aliasing={{0}: (3, {})} | custom-call | flops 1000000 | bytes 2000000 | tf_op jit(solution)/shard_map/end/spread_other/pallas_call | solution.py:357
  (1 shorter events, 0.0 us)
Async XLA Ops:
  4.4 23.9 %copy-start = (bf16[1024,256]{1,0:T(8,128)(2,1)S(1)}, bf16[1024,256]{1,0:T(8,128)(2,1)}, u32[]{:S(2)}) copy-start(bf16[1024,256]{1,0:T(8,128)(2,1)} %join_ref.1) | copy-start | bytes 1572868
  26.2 3.8 %copy-start.1 = (bf16[2,256]{1,0:T(2,128)(2,1)S(1)}, bf16[2,256]{1,0:T(2,128)(2,1)}, u32[]{:S(2)}) copy-start(bf16[2,256]{1,0:T(2,128)(2,1)} %grad_ref.1) | copy-start | bytes 3076
  26.2 3.8 %collective-permute-start = (bf16[2304,128]{1,0:T(8,128)(2,1)S(1)}, bf16[2304,128]{1,0:T(8,128)(2,1)S(1)}, u32[]{:S(2)}, u32[]{:S(2)}) collective-permute-start(bf16[2304,128]{1,0:T(8,128)(2,1)S(1)} %get-tuple-element.22), channel_id=1, source_target_pairs={{0,16},{16,0},{1,17},{17,1},{2,18},{18,2},{3,19},{19,3},{4,20},{20... | collective-permute-start | bytes 1769480 | tf_op jit(solution)/shard_map/backward/ppermute | solution.py:320
  71.3 6.1 %collective-permute-start.1 = (bf16[32,80,128]{2,1,0:T(8,128)(2,1)S(1)}, bf16[32,80,128]{2,1,0:T(8,128)(2,1)S(1)}, u32[]{:S(2)}, u32[]{:S(2)}) collective-permute-start(bf16[32,80,128]{2,1,0:T(8,128)(2,1)S(1)} %all_to_all.23.own_ref), channel_id=1, source_target_pairs={{0,16},{16,0},{1,17},{17,1},{2,18},{18,2},{3,19},{19,3},{4,20},{20... | collective-permute-start | bytes 1966088 | tf_op jit(solution)/shard_map/conv_gather/ppermute | solution.py:352
  75.6 1.7 %collective-permute-start.2 = (bf16[16,384]{1,0:T(8,128)(2,1)S(1)}, bf16[16,384]{1,0:T(8,128)(2,1)S(1)}, u32[]{:S(2)}, u32[]{:S(2)}) collective-permute-start(bf16[16,384]{1,0:T(8,128)(2,1)S(1)} %get-tuple-element.27.rest_ref), channel_id=1, source_target_pairs={{0,16},{16,0},{1,17},{17,1},{2,18},{18,2},{3,19},{19,3},{4,20},{20... | collective-permute-start | bytes 36872 | tf_op jit(solution)/shard_map/end/ppermute | solution.py:356

commit v7 on v6

--- a/solution.py
+++ b/solution.py
@@ -39,11 +39,11 @@
         pltpu.make_async_copy(source, target, sems.at[i])
         for i, (source, target) in enumerate(
             (
-                (valid_hbm, valid_ref),
-                (grad_hbm, grad_ref),
-                (join_hbm, join_ref),
                 (maps_hbm, maps_ref),
                 (conv_hbm, conv_ref),
+                (valid_hbm, valid_ref),
+                (join_hbm, join_ref),
+                (grad_hbm, grad_ref),
             )
         )
     ]
@@ -51,6 +51,26 @@
         load.start()
     core, cam = lax.axis_index("c"), lax.axis_index("zh") * 4 + lax.axis_index("y")
     loads[0].wait()
+    m = 22 * 32
+    keep_first, keep_last = edge_masks(m)
+    for r in range(2):
+        rows = maps_ref[:, 32 * r : 32 * r + 32, :].reshape(m, 256).astype(F32)
+        for dx in range(3):
+            if dx == 0:
+                shifted = jnp.where(keep_first, pltpu.roll(rows, 1, 0), 0.0)
+            elif dx == 1:
+                shifted = rows
+            else:
+                shifted = jnp.where(keep_last, pltpu.roll(rows, m - 1, 0), 0.0)
+            shifted = jnp.concatenate([shifted, jnp.zeros((KDIM - m, 256), F32)], 0)
+            turned = shifted.astype(BF).T
+            for half in range(2):
+                slot = core if half == 0 else 1 - core
+                start = pl.multiple_of(slot * 384 + dx * 128, 128)
+                turned_ref[r, pl.ds(start, 128), :] = turned[128 * half : 128 * half + 128]
+
+    loads[1].wait()
+    loads[2].wait()
     valid = valid_ref[...].astype(F32)
     count = jnp.sum(valid, axis=1, keepdims=True)
     lane = lax.broadcasted_iota(jnp.int32, (2, 176), 1)
@@ -58,19 +78,6 @@
     n = 11 * 32
     not_first, not_last = edge_masks(n)
 
-    loads[1].wait()
-    loads[2].wait()
-    grad = grad_ref[...]
-    for pos in range(4):
-        part = lax.dot_general(
-            grad, join_ref[256 * pos : 256 * pos + 256, :], (((1,), (1,)), ((), ())), preferred_element_type=F32
-        )
-        for j in range(2):
-            rows_ref[4 * j + pos : 4 * j + pos + 1, :] = part[j : j + 1]
-    out_ref[:, 0:8, :] = jnp.broadcast_to(rows_ref[0:8, :].astype(BF)[None], (16, 8, 256))
-
-    loads[3].wait()
-    loads[4].wait()
     for f in range(2):
         at = f * 11
         top = maps_ref[at : at + 11, 0:32, :].reshape(n, 256)
@@ -97,23 +104,16 @@
                 rows_ref[start : start + 4, :] = pooled[4 * k : 4 * k + 4]
     out_ref[:, 8:16, :] = rows_ref[...].reshape(16, 8, 256).astype(BF)
 
-    m = 22 * 32
-    keep_first, keep_last = edge_masks(m)
-    for r in range(2):
-        rows = maps_ref[:, 32 * r : 32 * r + 32, :].reshape(m, 256).astype(F32)
-        for dx in range(3):
-            if dx == 0:
-                shifted = jnp.where(keep_first, pltpu.roll(rows, 1, 0), 0.0)
-            elif dx == 1:
-                shifted = rows
-            else:
-                shifted = jnp.where(keep_last, pltpu.roll(rows, m - 1, 0), 0.0)
-            shifted = jnp.concatenate([shifted, jnp.zeros((KDIM - m, 256), F32)], 0)
-            turned = shifted.T.astype(BF)
-            for half in range(2):
-                slot = core if half == 0 else 1 - core
-                start = pl.multiple_of(slot * 384 + dx * 128, 128)
-                turned_ref[r, pl.ds(start, 128), :] = turned[128 * half : 128 * half + 128]
+    loads[3].wait()
+    loads[4].wait()
+    grad = grad_ref[...]
+    for pos in range(4):
+        part = lax.dot_general(
+            grad, join_ref[256 * pos : 256 * pos + 256, :], (((1,), (1,)), ((), ())), preferred_element_type=F32
+        )
+        for j in range(2):
+            rows_ref[4 * j + pos : 4 * j + pos + 1, :] = part[j : j + 1]
+    out_ref[:, 0:8, :] = jnp.broadcast_to(rows_ref[0:8, :].astype(BF)[None], (16, 8, 256))
 
 
 def send_kernel(grad_ref, slope_ref, turned_ref, pre_ref, send_ref, grads):
@@ -193,9 +193,8 @@
     head = jnp.sum(got_ref[:, 0:64, :].astype(F32), axis=0).astype(BF)
     foot = jnp.sum(got_ref[:, 64:80, :].astype(F32), axis=0).astype(BF)
     own_y = lax.axis_index("y")
-    for z in range(4):
-        out_ref[z, 0:64, :] = head
-        out_ref[z, 64:80, :] = foot
+    out_ref[0:64, :] = head
+    out_ref[64:80, :] = foot
     for k in range(8):
         last = got_ref[4 * k + own_y, 64:80, :].astype(F32)
         for j in range(2):
@@ -207,8 +206,9 @@
     rest_ref[...] = rows_ref[...].astype(BF)
 
 
-def finish_kernel(got_ref, out_ref):
-    total = jnp.sum(got_ref[...].astype(F32), axis=0).astype(BF)
+def finish_kernel(own_ref, one_ref, two_ref, three_ref, out_ref):
+    own, one, two, three = (ref[...].astype(F32) for ref in (own_ref, one_ref, two_ref, three_ref))
+    total = ((own + two) + (one + three)).astype(BF)
     for b in range(32):
         out_ref[b] = total
 
@@ -340,14 +340,14 @@
         middle, rest = call(
             middle_kernel,
             "middle",
-            [shape(4, 80, 128, dtype=BF), shape(16, 384, dtype=BF)],
+            [shape(80, 128, dtype=BF), shape(16, 384, dtype=BF)],
             [VM],
             [pltpu.VMEM((16, 384), F32)],
         )(blocks)
-        lines = lax.all_to_all(middle, "zh", 0, 0)
+        away = [lax.ppermute(middle, "zh", [(i, (i + k) % 4) for i in range(4)]) for k in (1, 2, 3)]
 
     with jax.named_scope("conv_gather"):
-        (summed,) = call(finish_kernel, "finish", [shape(32, 80, 128, dtype=BF)], [VM])(lines)
+        (summed,) = call(finish_kernel, "finish", [shape(32, 80, 128, dtype=BF)], [VM] * 4)(middle, *away)
         own = lax.all_to_all(summed, BLOCK, 0, 0)
         other = lax.ppermute(own, "c", SWAP)
         begun, latent = spread(spread_own_kernel, "spread_own", (2, 256), [VM], {})(own)

time: 78.8 us -> 78.1 us (level)
  blocking collectives: 61.7 us -> 52.5 us
  waiting for transfers between devices: 1.44 us -> 6.28 us
  starting transfers between devices: 6.5 us -> 10.3 us
    all_to_all x1 -> x0, blocking collectives: 9.44 us -> none  [on_device(): lines = lax.all_to_all(middle, 'zh', 0, 0)]
    ppermute x0 -> x3, waiting for transfers between devices: none -> 4.84 us  [on_device(): lax.ppermute(middle, 'zh', [(i, (i + k) % 4) for i in range(4)])]
    ppermute x0 -> x3, starting transfers between devices: none -> 3.82 us  [on_device(): lax.ppermute(middle, 'zh', [(i, (i + k) % 4) for i in range(4)])]
  transfers between devices with their start and end apart: 3 -> 6, of which waited for: 2 -> 4; matrix products, arithmetic and copies ran while one was open for 0% -> 0% of each run, Pallas kernels for 2% -> 2%
where the time goes in v7:
time: 78.1 us; the launch traced here: 77.9 us
  blocking collectives  52.5 us (67%)
  starting transfers between devices  10.3 us (13%)
  Pallas kernels  8.08 us (10%)
  waiting for transfers between devices  6.28 us (8%)
    all_to_all x1, blocking collectives, on_device(): cam_shares = lax.all_to_all(shares, ('zh', 'y'), 0, 0)  20.9 us
    all_to_all x1, blocking collectives, on_device(): blocks = lax.all_to_all(packed, BLOCK, 0, 0)  17 us
    all_to_all x1, blocking collectives, on_device(): own = lax.all_to_all(summed, BLOCK, 0, 0)  14.5 us
    ppermute x3, waiting for transfers between devices, on_device(): lax.ppermute(middle, 'zh', [(i, (i + k) % 4) for i in range(4)])  4.84 us
    ppermute x1, starting transfers between devices, on_device(): other = lax.ppermute(own, 'c', SWAP)  4.31 us
    ppermute x3, starting transfers between devices, on_device(): lax.ppermute(middle, 'zh', [(i, (i + k) % 4) for i in range(4)])  3.82 us
    pallas_call x1, Pallas kernels, on_device(): call(forward_kernel, 'forward', [shape(16, 16, 256, dtype=BF), shape(22,...  3.59 us
    ppermute x1, starting transfers between devices, on_device(): got = lax.ppermute(send, 'c', SWAP)  2.19 us
  transfers between devices with their start and end apart: 6, of which 4 were waited for; matrix products, arithmetic and copies ran while one was open for 0% of the time, Pallas kernels for 2%

profile of v7, /device:TPU:1, one launch (start us, length us, event | category | flops | bytes accessed | tf_op | source)
XLA Modules:
  0.0 77.9 jit_solution(10160882199379874371)
XLA Ops:
  0.6 3.6 %forward.1 = (bf16[16,16,256]{2,1,0:T(8,128)(2,1)S(1)}, f32[22,64,256]{2,1,0:T(8,128)S(1)}, bf16[2,768,768]{2,1,0:T(8,128)(2,1)S(1)}) custom-call(s32[2,176]{1,0:T(2,128)} %valid_hbm.1, bf16[2,256]{1,0:T(2,128)(2,1)} %grad_ref.1, bf16[1024,256]{1,0:T(8,128)(2,1)} %join_ref.1, bf16[22,64,256]{2,1,0:T(8,128)(2,1)} %bitcast.1, bf16[9,256,256]{2,1,0:T(8,128)(2,1)} %conv_hbm.1), custom_call_target="tpu_custom_call" | custom-call | flops 1200000000 | bytes 3000000 | tf_op jit(solution)/shard_map/forward/forward/pallas_call | solution.py:293
  4.2 0.0 copy-start
  4.2 20.9 %all_to_all.15.grad_ref.got_ref = bf16[16,16,256]{2,1,0:T(8,128)(2,1)S(1)} all-to-all(bf16[16,16,256]{2,1,0:T(8,128)(2,1)S(1)} %get-tuple-element.18), channel_id=1, replica_groups=mesh['zl'=2,'x'=4,'c'=2,'zh'=4,'y'=4] {'zh','y'}, dimensions={0} | all-to-all | bytes 262144 | tf_op jit(solution)/shard_map/forward/all_to_all | solution.py:309
  25.2 0.8 %backward_send.1 = (bf16[2,768,256]{2,1,0:T(8,128)(2,1)S(1)}, bf16[2304,128]{1,0:T(8,128)(2,1)S(1)}) custom-call(bf16[16,16,256]{2,1,0:T(8,128)(2,1)S(1)} %all_to_all.15.grad_ref.got_ref, f32[22,64,256]{2,1,0:T(8,128)S(1)} %get-tuple-element.19.slope_ref, bf16[2,768,768]{2,1,0:T(8,128)(2,1)S(1)} %get-tuple-element.17.turned_ref), custom_call_target="tpu_custom_call" | custom-call | flops 600000000 | bytes 3000000 | tf_op jit(solution)/shard_map/backward/backward_send/pallas_call | solution.py:312
  26.0 0.0 copy-start.1
  26.0 2.2 %collective-permute-start = (bf16[2304,128]{1,0:T(8,128)(2,1)S(1)}, bf16[2304,128]{1,0:T(8,128)(2,1)S(1)}, u32[]{:S(2)}, u32[]{:S(2)}) collective-permute-start(bf16[2304,128]{1,0:T(8,128)(2,1)S(1)} %get-tuple-element.22), channel_id=1, source_target_pairs={{0,16},{16,0},{1,17},{17,1},{2,18},{18,2},{3,19},{19,3},{4,20},{20... | collective-permute-start | bytes 1769480 | tf_op jit(solution)/shard_map/backward/ppermute | solution.py:320
  28.2 0.8 %backward_mine.1 = (f32[2304,128]{1,0:T(8,128)S(1)}, f32[8,256]{1,0:T(8,128)S(1)}, f32[2,256]{1,0:T(2,128)S(1)}) custom-call(bf16[2,768,768]{2,1,0:T(8,128)(2,1)S(1)} %get-tuple-element.17.turned_ref, bf16[2,768,256]{2,1,0:T(8,128)(2,1)S(1)} %get-tuple-element.20.pre_ref, bf16[16,16,256]{2,1,0:T(8,128)(2,1)S(1)} %all_to_all.15.grad_ref.got_ref, ...), custom_call_target="tpu_custom_call" | custom-call | flops 600000000 | bytes 3000000 | tf_op jit(solution)/shard_map/backward/backward_mine/pallas_call | solution.py:321
  29.0 0.8 %collective-permute-done.got_ref = bf16[2304,128]{1,0:T(8,128)(2,1)S(1)} collective-permute-done((bf16[2304,128]{1,0:T(8,128)(2,1)S(1)}, bf16[2304,128]{1,0:T(8,128)(2,1)S(1)}, u32[]{:S(2)}, u32[]{:S(2)}) %collective-permute-start) | collective-permute-done | bytes 589856 | tf_op jit(solution)/shard_map/backward/ppermute | solution.py:320
  29.8 0.4 pack.1
  30.2 17.0 %all_to_all.16.got_ref = bf16[32,80,128]{2,1,0:T(8,128)(2,1)S(1)} all-to-all(bf16[32,80,128]{2,1,0:T(8,128)(2,1)S(1)} %pack.1), channel_id=1, replica_groups=mesh['zl'=2,'x'=4,'c'=2,'zh'=4,'y'=4] {'zl','x','y'}, dimensions={0} | all-to-all | bytes 1310720 | tf_op jit(solution)/shard_map/conv_scatter/all_to_all | solution.py:337
  47.2 0.1 middle.1
  47.4 0.1 collective-permute-start.3
  47.4 3.7 %collective-permute-start.2 = (bf16[80,128]{1,0:T(8,128)(2,1)S(1)}, bf16[80,128]{1,0:T(8,128)(2,1)S(1)}, u32[]{:S(2)}, u32[]{:S(2)}) collective-permute-start(bf16[80,128]{1,0:T(8,128)(2,1)S(1)} %get-tuple-element.25.own_ref), channel_id=1, source_target_pairs={{0,8},{4,12},{8,0},{12,4},{1,9},{5,13},{9,1},{13,5},{2,10},{6,14},... | collective-permute-start | bytes 61448 | tf_op jit(solution)/shard_map/conv_middle/ppermute | solution.py:347
  51.2 0.0 collective-permute-start.1
  51.2 0.0 collective-permute-done.3.three_ref
  51.2 2.9 %collective-permute-done.2.two_ref = bf16[80,128]{1,0:T(8,128)(2,1)S(1)} collective-permute-done((bf16[80,128]{1,0:T(8,128)(2,1)S(1)}, bf16[80,128]{1,0:T(8,128)(2,1)S(1)}, u32[]{:S(2)}, u32[]{:S(2)}) %collective-permute-start.2) | collective-permute-done | bytes 20512 | tf_op jit(solution)/shard_map/conv_middle/ppermute | solution.py:347
  54.1 1.9 %collective-permute-done.1.one_ref = bf16[80,128]{1,0:T(8,128)(2,1)S(1)} collective-permute-done((bf16[80,128]{1,0:T(8,128)(2,1)S(1)}, bf16[80,128]{1,0:T(8,128)(2,1)S(1)}, u32[]{:S(2)}, u32[]{:S(2)}) %collective-permute-start.1) | collective-permute-done | bytes 20512 | tf_op jit(solution)/shard_map/conv_middle/ppermute | solution.py:347
  56.1 14.5 %all_to_all.17.own_ref = bf16[32,80,128]{2,1,0:T(8,128)(2,1)S(1)} all-to-all(bf16[32,80,128]{2,1,0:T(8,128)(2,1)S(1)} %finish.1), channel_id=1, replica_groups=mesh['zl'=2,'x'=4,'c'=2,'zh'=4,'y'=4] {'zl','x','y'}, dimensions={0} | all-to-all | bytes 1310720 | tf_op jit(solution)/shard_map/conv_gather/all_to_all | solution.py:351
  70.6 4.3 %collective-permute-start.4 = (bf16[32,80,128]{2,1,0:T(8,128)(2,1)S(1)}, bf16[32,80,128]{2,1,0:T(8,128)(2,1)S(1)}, u32[]{:S(2)}, u32[]{:S(2)}) collective-permute-start(bf16[32,80,128]{2,1,0:T(8,128)(2,1)S(1)} %all_to_all.17.own_ref), channel_id=1, source_target_pairs={{0,16},{16,0},{1,17},{17,1},{2,18},{18,2},{3,19},{19,3},{4,20},{20... | collective-permute-start | bytes 1966088 | tf_op jit(solution)/shard_map/conv_gather/ppermute | solution.py:352
  74.9 0.0 collective-permute-start.5
  74.9 1.1 %spread_own.1 = (f32[9,256,256]{2,1,0:T(8,128)}, f32[2,256]{1,0:T(2,128)}) custom-call(bf16[32,80,128]{2,1,0:T(8,128)(2,1)S(1)} %all_to_all.17.own_ref), custom_call_target="tpu_custom_call" | custom-call | flops 1000000 | bytes 2000000 | tf_op jit(solution)/shard_map/conv_gather/spread_own/pallas_call | solution.py:353
  76.0 0.6 collective-permute-done.5.rest_other_ref
  76.7 0.0 collective-permute-done.4.other_ref
  76.7 1.2 %spread_other.1 = (f32[9,256,256]{2,1,0:T(8,128)}, f32[64,256]{1,0:T(8,128)}) custom-call(bf16[32,80,128]{2,1,0:T(8,128)(2,1)S(1)} %collective-permute-done.4.other_ref, bf16[16,384]{1,0:T(8,128)(2,1)S(1)} %get-tuple-element.27.rest_ref, bf16[16,384]{1,0:T(8,128)(2,1)S(1)} %collective-permute-done.5.rest_other_ref, ...), custom_call_target="tpu_custom_call", output_to_operand_aliasing={{0}: (3, {})} | custom-call | flops 1000000 | bytes 2000000 | tf_op jit(solution)/shard_map/end/spread_other/pallas_call | solution.py:357
  (3 shorter events, 0.1 us)
Async XLA Ops:
  4.2 23.9 %copy-start = (bf16[1024,256]{1,0:T(8,128)(2,1)S(1)}, bf16[1024,256]{1,0:T(8,128)(2,1)}, u32[]{:S(2)}) copy-start(bf16[1024,256]{1,0:T(8,128)(2,1)} %join_ref.1) | copy-start | bytes 1572868
  26.0 3.8 %copy-start.1 = (bf16[2,256]{1,0:T(2,128)(2,1)S(1)}, bf16[2,256]{1,0:T(2,128)(2,1)}, u32[]{:S(2)}) copy-start(bf16[2,256]{1,0:T(2,128)(2,1)} %grad_ref.1) | copy-start | bytes 3076
  26.0 3.8 %collective-permute-start = (bf16[2304,128]{1,0:T(8,128)(2,1)S(1)}, bf16[2304,128]{1,0:T(8,128)(2,1)S(1)}, u32[]{:S(2)}, u32[]{:S(2)}) collective-permute-start(bf16[2304,128]{1,0:T(8,128)(2,1)S(1)} %get-tuple-element.22), channel_id=1, source_target_pairs={{0,16},{16,0},{1,17},{17,1},{2,18},{18,2},{3,19},{19,3},{4,20},{20... | collective-permute-start | bytes 1769480 | tf_op jit(solution)/shard_map/backward/ppermute | solution.py:320
  47.4 3.8 %collective-permute-start.3 = (bf16[80,128]{1,0:T(8,128)(2,1)S(1)}, bf16[80,128]{1,0:T(8,128)(2,1)S(1)}, u32[]{:S(2)}, u32[]{:S(2)}) collective-permute-start(bf16[80,128]{1,0:T(8,128)(2,1)S(1)} %get-tuple-element.25.own_ref), channel_id=1, source_target_pairs={{0,12},{4,0},{8,4},{12,8},{1,13},{5,1},{9,5},{13,9},{2,14},{6,2},{... | collective-permute-start | bytes 61448 | tf_op jit(solution)/shard_map/conv_middle/ppermute | solution.py:347
  47.4 6.6 %collective-permute-start.2 = (bf16[80,128]{1,0:T(8,128)(2,1)S(1)}, bf16[80,128]{1,0:T(8,128)(2,1)S(1)}, u32[]{:S(2)}, u32[]{:S(2)}) collective-permute-start(bf16[80,128]{1,0:T(8,128)(2,1)S(1)} %get-tuple-element.25.own_ref), channel_id=1, source_target_pairs={{0,8},{4,12},{8,0},{12,4},{1,9},{5,13},{9,1},{13,5},{2,10},{6,14},... | collective-permute-start | bytes 61448 | tf_op jit(solution)/shard_map/conv_middle/ppermute | solution.py:347
  51.2 4.8 %collective-permute-start.1 = (bf16[80,128]{1,0:T(8,128)(2,1)S(1)}, bf16[80,128]{1,0:T(8,128)(2,1)S(1)}, u32[]{:S(2)}, u32[]{:S(2)}) collective-permute-start(bf16[80,128]{1,0:T(8,128)(2,1)S(1)} %get-tuple-element.25.own_ref), channel_id=1, source_target_pairs={{0,4},{4,8},{8,12},{12,0},{1,5},{5,9},{9,13},{13,1},{2,6},{6,10},{... | collective-permute-start | bytes 61448 | tf_op jit(solution)/shard_map/conv_middle/ppermute | solution.py:347
  70.6 6.1 %collective-permute-start.4 = (bf16[32,80,128]{2,1,0:T(8,128)(2,1)S(1)}, bf16[32,80,128]{2,1,0:T(8,128)(2,1)S(1)}, u32[]{:S(2)}, u32[]{:S(2)}) collective-permute-start(bf16[32,80,128]{2,1,0:T(8,128)(2,1)S(1)} %all_to_all.17.own_ref), channel_id=1, source_target_pairs={{0,16},{16,0},{1,17},{17,1},{2,18},{18,2},{3,19},{19,3},{4,20},{20... | collective-permute-start | bytes 1966088 | tf_op jit(solution)/shard_map/conv_gather/ppermute | solution.py:352
  74.9 1.7 %collective-permute-start.5 = (bf16[16,384]{1,0:T(8,128)(2,1)S(1)}, bf16[16,384]{1,0:T(8,128)(2,1)S(1)}, u32[]{:S(2)}, u32[]{:S(2)}) collective-permute-start(bf16[16,384]{1,0:T(8,128)(2,1)S(1)} %get-tuple-element.27.rest_ref), channel_id=1, source_target_pairs={{0,16},{16,0},{1,17},{17,1},{2,18},{18,2},{3,19},{19,3},{4,20},{20... | collective-permute-start | bytes 36872 | tf_op jit(solution)/shard_map/end/ppermute | solution.py:356

commit v8 on v7

--- a/solution.py
+++ b/solution.py
@@ -164,53 +164,61 @@
         latent_ref[j : j + 1, :] = sum(parts[pos][4 * j + pos : 4 * j + pos + 1] for pos in range(4))
 
 
-def pack_kernel(mine_ref, got_ref, joined_ref, latent_ref, grad_ref, out_ref, last):
+def pack_kernel(mine_ref, got_ref, joined_ref, latent_ref, grad_ref, out_ref, latents, others):
     head = (mine_ref[0:2048] + got_ref[0:2048].astype(F32)).astype(BF)
     out_ref[:, 0:64, :] = head.reshape(32, 64, 128)
     foot = mine_ref[2048:2304] + got_ref[2048:2304].astype(F32)
     grad = grad_ref[...].astype(F32)
-    last[...] = jnp.zeros((16, 128), F32)
-    own_x, own_z = lax.axis_index("x"), lax.axis_index("zl")
+    latents[...] = jnp.zeros((8, 128), F32)
+    others[...] = jnp.zeros((8, 128), F32)
     for j in range(2):
         for h in range(2):
-            last[11 + 2 * j + h : 12 + 2 * j + h, :] = grad[j : j + 1, 128 * h : 128 * h + 128]
-    for z in range(2):
-        for x in range(4):
-            t = 4 * z + x
-            lanes = slice(128 * (t % 2), 128 * (t % 2) + 128)
-            for j in range(2):
-                row = 4 * j + t // 2
-                last[9 + j : 10 + j, :] = joined_ref[row : row + 1, lanes]
-            own = jnp.where(jnp.logical_and(own_x == x, own_z == z), 1.0, 0.0)
-            for y in range(4):
-                b = 4 * t + y
-                last[0:8, :] = foot[8 * b : 8 * b + 8]
-                last[8:9, :] = latent_ref[y // 2 : y // 2 + 1, 128 * (y % 2) : 128 * (y % 2) + 128] * own
-                out_ref[b, 64:80, :] = last[...].astype(BF)
-
-
-def middle_kernel(got_ref, out_ref, rest_ref, rows_ref):
-    head = jnp.sum(got_ref[:, 0:64, :].astype(F32), axis=0).astype(BF)
-    foot = jnp.sum(got_ref[:, 64:80, :].astype(F32), axis=0).astype(BF)
-    own_y = lax.axis_index("y")
-    out_ref[0:64, :] = head
-    out_ref[64:80, :] = foot
-    for k in range(8):
-        last = got_ref[4 * k + own_y, 64:80, :].astype(F32)
+            lanes = slice(128 * h, 128 * h + 128)
+            latents[2 * j + h : 2 * j + h + 1, :] = latent_ref[j : j + 1, lanes]
+            others[2 + 2 * j + h : 3 + 2 * j + h, :] = grad[j : j + 1, lanes]
+    line = lax.axis_index("zl") * 4 + lax.axis_index("x")
+    for t in range(8):
+        lanes = slice(128 * (t % 2), 128 * (t % 2) + 128)
         for j in range(2):
-            at = slice(2 * k + j, 2 * k + j + 1)
-            rows_ref[at, 0:128] = last[9 + j : 10 + j]
+            row = 4 * j + t // 2
+            others[j : j + 1, :] = joined_ref[row : row + 1, lanes]
+        last = jnp.where(line == t, latents[...], others[...])
+        for y in range(4):
+            b = 4 * t + y
+            out_ref[b, 64:80, :] = jnp.concatenate([foot[8 * b : 8 * b + 8], last], 0).astype(BF)
+
+
+def middle_kernel(got_ref, joined_ref, grad_ref, out_ref, rest_ref, rows_ref):
+    out_ref[0:64, :] = jnp.sum(got_ref[:, 0:64, :].astype(F32), axis=0).astype(BF)
+    line, own_y = lax.axis_index("zl") * 4 + lax.axis_index("x"), lax.axis_index("y")
+    foot = jnp.sum(got_ref[:, 64:80, :].astype(F32), axis=0)[0:8]
+    latents = got_ref[4 * line, 64:80, :].astype(F32)
+    for y in range(1, 4):
+        latents = latents + got_ref[4 * line + y, 64:80, :].astype(F32)
+    out_ref[64:80, :] = jnp.concatenate([foot, latents[8:16]], 0).astype(BF)
+    grad = grad_ref[...].astype(F32)
+    for t in range(8):
+        last = got_ref[4 * t + own_y, 64:80, :].astype(F32)
+        own = line == t
+        lanes = slice(128 * (t % 2), 128 * (t % 2) + 128)
+        for j in range(2):
+            at = slice(2 * t + j, 2 * t + j + 1)
+            row = 4 * j + t // 2
+            rows_ref[at, 0:128] = jnp.where(own, joined_ref[row : row + 1, lanes], last[8 + j : 9 + j])
             for h in range(2):
-                row = 11 + 2 * j + h
-                rows_ref[at, 128 + 128 * h : 256 + 128 * h] = last[row : row + 1]
+                row = 10 + 2 * j + h
+                share = grad[j : j + 1, 128 * h : 128 * h + 128]
+                rows_ref[at, 128 + 128 * h : 256 + 128 * h] = jnp.where(own, share, last[row : row + 1])
     rest_ref[...] = rows_ref[...].astype(BF)
 
 
-def finish_kernel(own_ref, one_ref, two_ref, three_ref, out_ref):
+def finish_kernel(own_ref, one_ref, two_ref, three_ref, out_ref, latent_ref):
     own, one, two, three = (ref[...].astype(F32) for ref in (own_ref, one_ref, two_ref, three_ref))
-    total = ((own + two) + (one + three)).astype(BF)
+    total = (own + two) + (one + three)
+    latent_ref[...] = total[72:80]
+    conv = total[0:72].astype(BF)
     for b in range(32):
-        out_ref[b] = total
+        out_ref[b] = conv
 
 
 def spread_half(ref, half, conv_hbm, slabs, sem):
@@ -219,19 +227,18 @@
         lanes = slice(128 * (s % 2), 128 * (s % 2) + 128)
         slabs[s // 2, i : i + 64, lanes] = ref[b, 0:64, :].astype(F32)
         s, i = b // 16, 8 * (b % 16)
-        slabs[8, i : i + 8, 128 * s : 128 * s + 128] = ref[b, 64:80, :].astype(F32)[0:8]
+        slabs[8, i : i + 8, 128 * s : 128 * s + 128] = ref[b, 64:72, :].astype(F32)
     rows = pl.ds(pl.multiple_of(128 * half, 128), 128)
     copy = pltpu.make_async_copy(slabs, conv_hbm.at[:, rows], sem)
     copy.start()
     return copy
 
 
-def spread_own_kernel(own_ref, conv_hbm, latent_hbm, slabs, latent_ref, sems):
+def spread_own_kernel(own_ref, sums_ref, conv_hbm, latent_hbm, slabs, latent_ref, sems):
     copy = spread_half(own_ref, lax.axis_index("c"), conv_hbm, slabs, sems.at[0])
-    first = 16 * lax.axis_index("zl") + 4 * lax.axis_index("x")
-    for y in range(4):
-        row = own_ref[first + y, 64:80, :].astype(F32)[8:9]
-        latent_ref[y // 2 : y // 2 + 1, 128 * (y % 2) : 128 * (y % 2) + 128] = row
+    for j in range(2):
+        for h in range(2):
+            latent_ref[j : j + 1, 128 * h : 128 * h + 128] = sums_ref[2 * j + h : 2 * j + h + 1]
     small = pltpu.make_async_copy(latent_ref, latent_hbm, sems.at[1])
     small.start()
     copy.wait()
@@ -332,7 +339,7 @@
             "pack",
             [shape(32, 80, 128, dtype=BF)],
             [VM, VM, VM, VM, VM],
-            [pltpu.VMEM((16, 128), F32)],
+            [pltpu.VMEM((8, 128), F32), pltpu.VMEM((8, 128), F32)],
         )(mine, got, joined, latent_part, latent_grad)
         blocks = lax.all_to_all(packed, BLOCK, 0, 0)
 
@@ -341,16 +348,20 @@
             middle_kernel,
             "middle",
             [shape(80, 128, dtype=BF), shape(16, 384, dtype=BF)],
-            [VM],
+            [VM, VM, VM],
             [pltpu.VMEM((16, 384), F32)],
-        )(blocks)
+        )(blocks, joined, latent_grad)
         away = [lax.ppermute(middle, "zh", [(i, (i + k) % 4) for i in range(4)]) for k in (1, 2, 3)]
 
     with jax.named_scope("conv_gather"):
-        (summed,) = call(finish_kernel, "finish", [shape(32, 80, 128, dtype=BF)], [VM] * 4)(middle, *away)
+        summed, latent_sums = call(
+            finish_kernel, "finish", [shape(32, 72, 128, dtype=BF), shape(8, 128)], [VM] * 4
+        )(middle, *away)
         own = lax.all_to_all(summed, BLOCK, 0, 0)
         other = lax.ppermute(own, "c", SWAP)
-        begun, latent = spread(spread_own_kernel, "spread_own", (2, 256), [VM], {})(own)
+        begun, latent = spread(spread_own_kernel, "spread_own", (2, 256), [VM, VM], {})(
+            own, latent_sums
+        )
 
     with jax.named_scope("end"):
         rest_other = lax.ppermute(rest, "c", SWAP)

time: 78.1 us -> 77.6 us (level)
  no operation moved by 1% of the time
where the time goes in v8:
time: 77.6 us; the launch traced here: 77.4 us
  blocking collectives  52.2 us (67%)
  starting transfers between devices  10.4 us (13%)
  Pallas kernels  7.94 us (10%)
  waiting for transfers between devices  6.18 us (8%)
    all_to_all x1, blocking collectives, on_device(): cam_shares = lax.all_to_all(shares, ('zh', 'y'), 0, 0)  20.9 us
    all_to_all x1, blocking collectives, on_device(): blocks = lax.all_to_all(packed, BLOCK, 0, 0)  17.1 us
    all_to_all x1, blocking collectives, on_device(): own = lax.all_to_all(summed, BLOCK, 0, 0)  14.2 us
    ppermute x3, waiting for transfers between devices, on_device(): lax.ppermute(middle, 'zh', [(i, (i + k) % 4) for i in range(4)])  4.84 us
    ppermute x1, starting transfers between devices, on_device(): other = lax.ppermute(own, 'c', SWAP)  4.39 us
    ppermute x3, starting transfers between devices, on_device(): lax.ppermute(middle, 'zh', [(i, (i + k) % 4) for i in range(4)])  3.82 us
    pallas_call x1, Pallas kernels, on_device(): call(forward_kernel, 'forward', [shape(16, 16, 256, dtype=BF), shape(22,...  3.59 us
    ppermute x1, starting transfers between devices, on_device(): got = lax.ppermute(send, 'c', SWAP)  2.19 us
  transfers between devices with their start and end apart: 6, of which 4 were waited for; matrix products, arithmetic and copies ran while one was open for 0% of the time, Pallas kernels for 2%

profile of v8, /device:TPU:1, one launch (start us, length us, event | category | flops | bytes accessed | tf_op | source)
XLA Modules:
  0.0 77.4 jit_solution(13883404048027738948)
XLA Ops:
  0.6 3.6 %forward.1 = (bf16[16,16,256]{2,1,0:T(8,128)(2,1)S(1)}, f32[22,64,256]{2,1,0:T(8,128)S(1)}, bf16[2,768,768]{2,1,0:T(8,128)(2,1)S(1)}) custom-call(s32[2,176]{1,0:T(2,128)} %valid_hbm.1, bf16[2,256]{1,0:T(2,128)(2,1)} %grad_ref.3, bf16[1024,256]{1,0:T(8,128)(2,1)} %join_ref.1, bf16[22,64,256]{2,1,0:T(8,128)(2,1)} %bitcast.1, bf16[9,256,256]{2,1,0:T(8,128)(2,1)} %conv_hbm.1), custom_call_target="tpu_custom_call" | custom-call | flops 1200000000 | bytes 3000000 | tf_op jit(solution)/shard_map/forward/forward/pallas_call | solution.py:300
  4.2 0.0 copy-start
  4.2 20.9 %all_to_all.15.grad_ref.got_ref = bf16[16,16,256]{2,1,0:T(8,128)(2,1)S(1)} all-to-all(bf16[16,16,256]{2,1,0:T(8,128)(2,1)S(1)} %get-tuple-element.20), channel_id=1, replica_groups=mesh['zl'=2,'x'=4,'c'=2,'zh'=4,'y'=4] {'zh','y'}, dimensions={0} | all-to-all | bytes 262144 | tf_op jit(solution)/shard_map/forward/all_to_all | solution.py:316
  25.2 0.8 %backward_send.1 = (bf16[2,768,256]{2,1,0:T(8,128)(2,1)S(1)}, bf16[2304,128]{1,0:T(8,128)(2,1)S(1)}) custom-call(bf16[16,16,256]{2,1,0:T(8,128)(2,1)S(1)} %all_to_all.15.grad_ref.got_ref, f32[22,64,256]{2,1,0:T(8,128)S(1)} %get-tuple-element.21.slope_ref, bf16[2,768,768]{2,1,0:T(8,128)(2,1)S(1)} %get-tuple-element.19.turned_ref), custom_call_target="tpu_custom_call" | custom-call | flops 600000000 | bytes 3000000 | tf_op jit(solution)/shard_map/backward/backward_send/pallas_call | solution.py:319
  26.0 0.0 copy-start.1
  26.0 2.2 %collective-permute-start = (bf16[2304,128]{1,0:T(8,128)(2,1)S(1)}, bf16[2304,128]{1,0:T(8,128)(2,1)S(1)}, u32[]{:S(2)}, u32[]{:S(2)}) collective-permute-start(bf16[2304,128]{1,0:T(8,128)(2,1)S(1)} %get-tuple-element.24), channel_id=1, source_target_pairs={{0,16},{16,0},{1,17},{17,1},{2,18},{18,2},{3,19},{19,3},{4,20},{20... | collective-permute-start | bytes 1769480 | tf_op jit(solution)/shard_map/backward/ppermute | solution.py:327
  28.2 0.8 %backward_mine.1 = (f32[2304,128]{1,0:T(8,128)S(1)}, f32[8,256]{1,0:T(8,128)S(1)}, f32[2,256]{1,0:T(2,128)S(1)}) custom-call(bf16[2,768,768]{2,1,0:T(8,128)(2,1)S(1)} %get-tuple-element.19.turned_ref, bf16[2,768,256]{2,1,0:T(8,128)(2,1)S(1)} %get-tuple-element.22.pre_ref, bf16[16,16,256]{2,1,0:T(8,128)(2,1)S(1)} %all_to_all.15.grad_ref.got_ref, ...), custom_call_target="tpu_custom_call" | custom-call | flops 600000000 | bytes 3000000 | tf_op jit(solution)/shard_map/backward/backward_mine/pallas_call | solution.py:328
  29.0 0.8 %collective-permute-done.got_ref = bf16[2304,128]{1,0:T(8,128)(2,1)S(1)} collective-permute-done((bf16[2304,128]{1,0:T(8,128)(2,1)S(1)}, bf16[2304,128]{1,0:T(8,128)(2,1)S(1)}, u32[]{:S(2)}, u32[]{:S(2)}) %collective-permute-start) | collective-permute-done | bytes 589856 | tf_op jit(solution)/shard_map/backward/ppermute | solution.py:327
  29.8 0.2 pack.1
  30.0 17.1 %all_to_all.16.got_ref = bf16[32,80,128]{2,1,0:T(8,128)(2,1)S(1)} all-to-all(bf16[32,80,128]{2,1,0:T(8,128)(2,1)S(1)} %pack.1), channel_id=1, replica_groups=mesh['zl'=2,'x'=4,'c'=2,'zh'=4,'y'=4] {'zl','x','y'}, dimensions={0} | all-to-all | bytes 1310720 | tf_op jit(solution)/shard_map/conv_scatter/all_to_all | solution.py:344
  47.1 0.1 middle.1
  47.2 0.1 collective-permute-start.3
  47.3 3.7 %collective-permute-start.2 = (bf16[80,128]{1,0:T(8,128)(2,1)S(1)}, bf16[80,128]{1,0:T(8,128)(2,1)S(1)}, u32[]{:S(2)}, u32[]{:S(2)}) collective-permute-start(bf16[80,128]{1,0:T(8,128)(2,1)S(1)} %get-tuple-element.27.own_ref), channel_id=1, source_target_pairs={{0,8},{4,12},{8,0},{12,4},{1,9},{5,13},{9,1},{13,5},{2,10},{6,14},... | collective-permute-start | bytes 61448 | tf_op jit(solution)/shard_map/conv_middle/ppermute | solution.py:354
  51.0 0.0 collective-permute-start.1
  51.0 0.0 collective-permute-done.3.three_ref
  51.1 2.9 %collective-permute-done.2.two_ref = bf16[80,128]{1,0:T(8,128)(2,1)S(1)} collective-permute-done((bf16[80,128]{1,0:T(8,128)(2,1)S(1)}, bf16[80,128]{1,0:T(8,128)(2,1)S(1)}, u32[]{:S(2)}, u32[]{:S(2)}) %collective-permute-start.2) | collective-permute-done | bytes 20512 | tf_op jit(solution)/shard_map/conv_middle/ppermute | solution.py:354
  53.9 1.9 %collective-permute-done.1.one_ref = bf16[80,128]{1,0:T(8,128)(2,1)S(1)} collective-permute-done((bf16[80,128]{1,0:T(8,128)(2,1)S(1)}, bf16[80,128]{1,0:T(8,128)(2,1)S(1)}, u32[]{:S(2)}, u32[]{:S(2)}) %collective-permute-start.1) | collective-permute-done | bytes 20512 | tf_op jit(solution)/shard_map/conv_middle/ppermute | solution.py:354
  55.9 0.1 finish.1
  55.9 14.2 %all_to_all.17.own_ref = bf16[32,72,128]{2,1,0:T(8,128)(2,1)S(1)} all-to-all(bf16[32,72,128]{2,1,0:T(8,128)(2,1)S(1)} %get-tuple-element.28), channel_id=1, replica_groups=mesh['zl'=2,'x'=4,'c'=2,'zh'=4,'y'=4] {'zl','x','y'}, dimensions={0} | all-to-all | bytes 1179648 | tf_op jit(solution)/shard_map/conv_gather/all_to_all | solution.py:360
  70.1 4.4 %collective-permute-start.4 = (bf16[32,72,128]{2,1,0:T(8,128)(2,1)S(1)}, bf16[32,72,128]{2,1,0:T(8,128)(2,1)S(1)}, u32[]{:S(2)}, u32[]{:S(2)}) collective-permute-start(bf16[32,72,128]{2,1,0:T(8,128)(2,1)S(1)} %all_to_all.17.own_ref), channel_id=1, source_target_pairs={{0,16},{16,0},{1,17},{17,1},{2,18},{18,2},{3,19},{19,3},{4,20},{20... | collective-permute-start | bytes 1769480 | tf_op jit(solution)/shard_map/conv_gather/ppermute | solution.py:361
  74.5 0.0 collective-permute-start.5
  74.5 1.1 %spread_own.1 = (f32[9,256,256]{2,1,0:T(8,128)}, f32[2,256]{1,0:T(2,128)}) custom-call(bf16[32,72,128]{2,1,0:T(8,128)(2,1)S(1)} %all_to_all.17.own_ref, f32[8,128]{1,0:T(8,128)S(1)} %get-tuple-element.29.sums_ref), custom_call_target="tpu_custom_call" | custom-call | flops 1000000 | bytes 2000000 | tf_op jit(solution)/shard_map/conv_gather/spread_own/pallas_call | solution.py:362
  75.6 0.5 collective-permute-done.5.rest_other_ref
  76.2 1.2 %spread_other.1 = (f32[9,256,256]{2,1,0:T(8,128)}, f32[64,256]{1,0:T(8,128)}) custom-call(bf16[32,72,128]{2,1,0:T(8,128)(2,1)S(1)} %collective-permute-done.4.other_ref, bf16[16,384]{1,0:T(8,128)(2,1)S(1)} %get-tuple-element.31.rest_ref, bf16[16,384]{1,0:T(8,128)(2,1)S(1)} %collective-permute-done.5.rest_other_ref, ...), custom_call_target="tpu_custom_call", output_to_operand_aliasing={{0}: (3, {})} | custom-call | flops 1000000 | bytes 2000000 | tf_op jit(solution)/shard_map/end/spread_other/pallas_call | solution.py:368
  (3 shorter events, 0.0 us)
Async XLA Ops:
  4.2 23.9 %copy-start = (bf16[1024,256]{1,0:T(8,128)(2,1)S(1)}, bf16[1024,256]{1,0:T(8,128)(2,1)}, u32[]{:S(2)}) copy-start(bf16[1024,256]{1,0:T(8,128)(2,1)} %join_ref.1) | copy-start | bytes 1572868
  26.0 3.8 %copy-start.1 = (bf16[2,256]{1,0:T(2,128)(2,1)S(1)}, bf16[2,256]{1,0:T(2,128)(2,1)}, u32[]{:S(2)}) copy-start(bf16[2,256]{1,0:T(2,128)(2,1)} %grad_ref.3) | copy-start | bytes 3076
  26.0 3.8 %collective-permute-start = (bf16[2304,128]{1,0:T(8,128)(2,1)S(1)}, bf16[2304,128]{1,0:T(8,128)(2,1)S(1)}, u32[]{:S(2)}, u32[]{:S(2)}) collective-permute-start(bf16[2304,128]{1,0:T(8,128)(2,1)S(1)} %get-tuple-element.24), channel_id=1, source_target_pairs={{0,16},{16,0},{1,17},{17,1},{2,18},{18,2},{3,19},{19,3},{4,20},{20... | collective-permute-start | bytes 1769480 | tf_op jit(solution)/shard_map/backward/ppermute | solution.py:327
  47.2 3.8 %collective-permute-start.3 = (bf16[80,128]{1,0:T(8,128)(2,1)S(1)}, bf16[80,128]{1,0:T(8,128)(2,1)S(1)}, u32[]{:S(2)}, u32[]{:S(2)}) collective-permute-start(bf16[80,128]{1,0:T(8,128)(2,1)S(1)} %get-tuple-element.27.own_ref), channel_id=1, source_target_pairs={{0,12},{4,0},{8,4},{12,8},{1,13},{5,1},{9,5},{13,9},{2,14},{6,2},{... | collective-permute-start | bytes 61448 | tf_op jit(solution)/shard_map/conv_middle/ppermute | solution.py:354
  47.3 6.6 %collective-permute-start.2 = (bf16[80,128]{1,0:T(8,128)(2,1)S(1)}, bf16[80,128]{1,0:T(8,128)(2,1)S(1)}, u32[]{:S(2)}, u32[]{:S(2)}) collective-permute-start(bf16[80,128]{1,0:T(8,128)(2,1)S(1)} %get-tuple-element.27.own_ref), channel_id=1, source_target_pairs={{0,8},{4,12},{8,0},{12,4},{1,9},{5,13},{9,1},{13,5},{2,10},{6,14},... | collective-permute-start | bytes 61448 | tf_op jit(solution)/shard_map/conv_middle/ppermute | solution.py:354
  51.0 4.8 %collective-permute-start.1 = (bf16[80,128]{1,0:T(8,128)(2,1)S(1)}, bf16[80,128]{1,0:T(8,128)(2,1)S(1)}, u32[]{:S(2)}, u32[]{:S(2)}) collective-permute-start(bf16[80,128]{1,0:T(8,128)(2,1)S(1)} %get-tuple-element.27.own_ref), channel_id=1, source_target_pairs={{0,4},{4,8},{8,12},{12,0},{1,5},{5,9},{9,13},{13,1},{2,6},{6,10},{... | collective-permute-start | bytes 61448 | tf_op jit(solution)/shard_map/conv_middle/ppermute | solution.py:354
  70.1 6.0 %collective-permute-start.4 = (bf16[32,72,128]{2,1,0:T(8,128)(2,1)S(1)}, bf16[32,72,128]{2,1,0:T(8,128)(2,1)S(1)}, u32[]{:S(2)}, u32[]{:S(2)}) collective-permute-start(bf16[32,72,128]{2,1,0:T(8,128)(2,1)S(1)} %all_to_all.17.own_ref), channel_id=1, source_target_pairs={{0,16},{16,0},{1,17},{17,1},{2,18},{18,2},{3,19},{19,3},{4,20},{20... | collective-permute-start | bytes 1769480 | tf_op jit(solution)/shard_map/conv_gather/ppermute | solution.py:361
  74.5 1.6 %collective-permute-start.5 = (bf16[16,384]{1,0:T(8,128)(2,1)S(1)}, bf16[16,384]{1,0:T(8,128)(2,1)S(1)}, u32[]{:S(2)}, u32[]{:S(2)}) collective-permute-start(bf16[16,384]{1,0:T(8,128)(2,1)S(1)} %get-tuple-element.31.rest_ref), channel_id=1, source_target_pairs={{0,16},{16,0},{1,17},{17,1},{2,18},{18,2},{3,19},{19,3},{4,20},{20... | collective-permute-start | bytes 36872 | tf_op jit(solution)/shard_map/end/ppermute | solution.py:367

commit v9 on v8

--- a/solution.py
+++ b/solution.py
@@ -351,7 +351,7 @@
             [VM, VM, VM],
             [pltpu.VMEM((16, 384), F32)],
         )(blocks, joined, latent_grad)
-        away = [lax.ppermute(middle, "zh", [(i, (i + k) % 4) for i in range(4)]) for k in (1, 2, 3)]
+        away = [lax.ppermute(middle, "zh", [(i, i ^ k) for i in range(4)]) for k in (1, 2, 3)]
 
     with jax.named_scope("conv_gather"):
         summed, latent_sums = call(

time: 77.6 us -> 76.4 us (0.985)
  waiting for transfers between devices: 6.18 us -> 3.27 us
  starting transfers between devices: 10.4 us -> 12.1 us
    ppermute x3, waiting for transfers between devices: 4.84 us -> 1.93 us  [on_device(): lax.ppermute(middle, 'zh', [(i, i ^ k) for i in range(4)])]
    ppermute x3, starting transfers between devices: 3.82 us -> 5.74 us  [on_device(): lax.ppermute(middle, 'zh', [(i, i ^ k) for i in range(4)])]
  transfers between devices with their start and end apart: 6 -> 6, of which waited for: 4 -> 4; matrix products, arithmetic and copies ran while one was open for 0% -> 0% of each run, Pallas kernels for 2% -> 3%
where the time goes in v9:
time: 76.4 us; the launch traced here: 76.2 us
  blocking collectives  52.2 us (68%)
  starting transfers between devices  12.1 us (16%)
  Pallas kernels  7.94 us (10%)
  waiting for transfers between devices  3.27 us (4%)
    all_to_all x1, blocking collectives, on_device(): cam_shares = lax.all_to_all(shares, ('zh', 'y'), 0, 0)  20.9 us
    all_to_all x1, blocking collectives, on_device(): blocks = lax.all_to_all(packed, BLOCK, 0, 0)  17.1 us
    all_to_all x1, blocking collectives, on_device(): own = lax.all_to_all(summed, BLOCK, 0, 0)  14.2 us
    ppermute x3, starting transfers between devices, on_device(): lax.ppermute(middle, 'zh', [(i, i ^ k) for i in range(4)])  5.74 us
    ppermute x1, starting transfers between devices, on_device(): other = lax.ppermute(own, 'c', SWAP)  4.18 us
    pallas_call x1, Pallas kernels, on_device(): call(forward_kernel, 'forward', [shape(16, 16, 256, dtype=BF), shape(22,...  3.59 us
    ppermute x1, starting transfers between devices, on_device(): got = lax.ppermute(send, 'c', SWAP)  2.19 us
    ppermute x3, waiting for transfers between devices, on_device(): lax.ppermute(middle, 'zh', [(i, i ^ k) for i in range(4)])  1.93 us
  transfers between devices with their start and end apart: 6, of which 4 were waited for; matrix products, arithmetic and copies ran while one was open for 0% of the time, Pallas kernels for 3%

profile of v9, /device:TPU:1, one launch (start us, length us, event | category | flops | bytes accessed | tf_op | source)
XLA Modules:
  0.0 76.2 jit_solution(569802613024999971)
XLA Ops:
  0.6 3.6 %forward.1 = (bf16[16,16,256]{2,1,0:T(8,128)(2,1)S(1)}, f32[22,64,256]{2,1,0:T(8,128)S(1)}, bf16[2,768,768]{2,1,0:T(8,128)(2,1)S(1)}) custom-call(s32[2,176]{1,0:T(2,128)} %valid_hbm.1, bf16[2,256]{1,0:T(2,128)(2,1)} %grad_ref.3, bf16[1024,256]{1,0:T(8,128)(2,1)} %join_ref.1, bf16[22,64,256]{2,1,0:T(8,128)(2,1)} %bitcast.1, bf16[9,256,256]{2,1,0:T(8,128)(2,1)} %conv_hbm.1), custom_call_target="tpu_custom_call" | custom-call | flops 1200000000 | bytes 3000000 | tf_op jit(solution)/shard_map/forward/forward/pallas_call | solution.py:300
  4.2 0.0 copy-start
  4.2 20.9 %all_to_all.15.grad_ref.got_ref = bf16[16,16,256]{2,1,0:T(8,128)(2,1)S(1)} all-to-all(bf16[16,16,256]{2,1,0:T(8,128)(2,1)S(1)} %get-tuple-element.20), channel_id=1, replica_groups=mesh['zl'=2,'x'=4,'c'=2,'zh'=4,'y'=4] {'zh','y'}, dimensions={0} | all-to-all | bytes 262144 | tf_op jit(solution)/shard_map/forward/all_to_all | solution.py:316
  25.2 0.8 %backward_send.1 = (bf16[2,768,256]{2,1,0:T(8,128)(2,1)S(1)}, bf16[2304,128]{1,0:T(8,128)(2,1)S(1)}) custom-call(bf16[16,16,256]{2,1,0:T(8,128)(2,1)S(1)} %all_to_all.15.grad_ref.got_ref, f32[22,64,256]{2,1,0:T(8,128)S(1)} %get-tuple-element.21.slope_ref, bf16[2,768,768]{2,1,0:T(8,128)(2,1)S(1)} %get-tuple-element.19.turned_ref), custom_call_target="tpu_custom_call" | custom-call | flops 600000000 | bytes 3000000 | tf_op jit(solution)/shard_map/backward/backward_send/pallas_call | solution.py:319
  26.0 0.0 copy-start.1
  26.0 2.2 %collective-permute-start = (bf16[2304,128]{1,0:T(8,128)(2,1)S(1)}, bf16[2304,128]{1,0:T(8,128)(2,1)S(1)}, u32[]{:S(2)}, u32[]{:S(2)}) collective-permute-start(bf16[2304,128]{1,0:T(8,128)(2,1)S(1)} %get-tuple-element.24), channel_id=1, source_target_pairs={{0,16},{16,0},{1,17},{17,1},{2,18},{18,2},{3,19},{19,3},{4,20},{20... | collective-permute-start | bytes 1769480 | tf_op jit(solution)/shard_map/backward/ppermute | solution.py:327
  28.2 0.8 %backward_mine.1 = (f32[2304,128]{1,0:T(8,128)S(1)}, f32[8,256]{1,0:T(8,128)S(1)}, f32[2,256]{1,0:T(2,128)S(1)}) custom-call(bf16[2,768,768]{2,1,0:T(8,128)(2,1)S(1)} %get-tuple-element.19.turned_ref, bf16[2,768,256]{2,1,0:T(8,128)(2,1)S(1)} %get-tuple-element.22.pre_ref, bf16[16,16,256]{2,1,0:T(8,128)(2,1)S(1)} %all_to_all.15.grad_ref.got_ref, ...), custom_call_target="tpu_custom_call" | custom-call | flops 600000000 | bytes 3000000 | tf_op jit(solution)/shard_map/backward/backward_mine/pallas_call | solution.py:328
  29.0 0.8 %collective-permute-done.got_ref = bf16[2304,128]{1,0:T(8,128)(2,1)S(1)} collective-permute-done((bf16[2304,128]{1,0:T(8,128)(2,1)S(1)}, bf16[2304,128]{1,0:T(8,128)(2,1)S(1)}, u32[]{:S(2)}, u32[]{:S(2)}) %collective-permute-start) | collective-permute-done | bytes 589856 | tf_op jit(solution)/shard_map/backward/ppermute | solution.py:327
  29.8 0.2 pack.1
  30.0 17.1 %all_to_all.16.got_ref = bf16[32,80,128]{2,1,0:T(8,128)(2,1)S(1)} all-to-all(bf16[32,80,128]{2,1,0:T(8,128)(2,1)S(1)} %pack.1), channel_id=1, replica_groups=mesh['zl'=2,'x'=4,'c'=2,'zh'=4,'y'=4] {'zl','x','y'}, dimensions={0} | all-to-all | bytes 1310720 | tf_op jit(solution)/shard_map/conv_scatter/all_to_all | solution.py:344
  47.1 0.1 middle.1
  47.2 0.1 collective-permute-start.3
  47.3 3.7 %collective-permute-start.2 = (bf16[80,128]{1,0:T(8,128)(2,1)S(1)}, bf16[80,128]{1,0:T(8,128)(2,1)S(1)}, u32[]{:S(2)}, u32[]{:S(2)}) collective-permute-start(bf16[80,128]{1,0:T(8,128)(2,1)S(1)} %get-tuple-element.27.own_ref), channel_id=1, source_target_pairs={{0,8},{4,12},{8,0},{12,4},{1,9},{5,13},{9,1},{13,5},{2,10},{6,14},... | collective-permute-start | bytes 61448 | tf_op jit(solution)/shard_map/conv_middle/ppermute | solution.py:354
  51.1 1.9 %collective-permute-start.1 = (bf16[80,128]{1,0:T(8,128)(2,1)S(1)}, bf16[80,128]{1,0:T(8,128)(2,1)S(1)}, u32[]{:S(2)}, u32[]{:S(2)}) collective-permute-start(bf16[80,128]{1,0:T(8,128)(2,1)S(1)} %get-tuple-element.27.own_ref), channel_id=1, source_target_pairs={{0,4},{4,0},{8,12},{12,8},{1,5},{5,1},{9,13},{13,9},{2,6},{6,2},{1... | collective-permute-start | bytes 61448 | tf_op jit(solution)/shard_map/conv_middle/ppermute | solution.py:354
  53.0 0.0 collective-permute-done.3.three_ref
  53.0 1.0 %collective-permute-done.2.two_ref = bf16[80,128]{1,0:T(8,128)(2,1)S(1)} collective-permute-done((bf16[80,128]{1,0:T(8,128)(2,1)S(1)}, bf16[80,128]{1,0:T(8,128)(2,1)S(1)}, u32[]{:S(2)}, u32[]{:S(2)}) %collective-permute-start.2) | collective-permute-done | bytes 20512 | tf_op jit(solution)/shard_map/conv_middle/ppermute | solution.py:354
  53.9 0.9 %collective-permute-done.1.one_ref = bf16[80,128]{1,0:T(8,128)(2,1)S(1)} collective-permute-done((bf16[80,128]{1,0:T(8,128)(2,1)S(1)}, bf16[80,128]{1,0:T(8,128)(2,1)S(1)}, u32[]{:S(2)}, u32[]{:S(2)}) %collective-permute-start.1) | collective-permute-done | bytes 20512 | tf_op jit(solution)/shard_map/conv_middle/ppermute | solution.py:354
  54.9 0.1 finish.1
  54.9 14.2 %all_to_all.17.own_ref = bf16[32,72,128]{2,1,0:T(8,128)(2,1)S(1)} all-to-all(bf16[32,72,128]{2,1,0:T(8,128)(2,1)S(1)} %get-tuple-element.28), channel_id=1, replica_groups=mesh['zl'=2,'x'=4,'c'=2,'zh'=4,'y'=4] {'zl','x','y'}, dimensions={0} | all-to-all | bytes 1179648 | tf_op jit(solution)/shard_map/conv_gather/all_to_all | solution.py:360
  69.1 4.2 %collective-permute-start.4 = (bf16[32,72,128]{2,1,0:T(8,128)(2,1)S(1)}, bf16[32,72,128]{2,1,0:T(8,128)(2,1)S(1)}, u32[]{:S(2)}, u32[]{:S(2)}) collective-permute-start(bf16[32,72,128]{2,1,0:T(8,128)(2,1)S(1)} %all_to_all.17.own_ref), channel_id=1, source_target_pairs={{0,16},{16,0},{1,17},{17,1},{2,18},{18,2},{3,19},{19,3},{4,20},{20... | collective-permute-start | bytes 1769480 | tf_op jit(solution)/shard_map/conv_gather/ppermute | solution.py:361
  73.3 0.0 collective-permute-start.5
  73.3 1.1 %spread_own.1 = (f32[9,256,256]{2,1,0:T(8,128)}, f32[2,256]{1,0:T(2,128)}) custom-call(bf16[32,72,128]{2,1,0:T(8,128)(2,1)S(1)} %all_to_all.17.own_ref, f32[8,128]{1,0:T(8,128)S(1)} %get-tuple-element.29.sums_ref), custom_call_target="tpu_custom_call" | custom-call | flops 1000000 | bytes 2000000 | tf_op jit(solution)/shard_map/conv_gather/spread_own/pallas_call | solution.py:362
  74.4 0.5 collective-permute-done.5.rest_other_ref
  75.0 1.2 %spread_other.1 = (f32[9,256,256]{2,1,0:T(8,128)}, f32[64,256]{1,0:T(8,128)}) custom-call(bf16[32,72,128]{2,1,0:T(8,128)(2,1)S(1)} %collective-permute-done.4.other_ref, bf16[16,384]{1,0:T(8,128)(2,1)S(1)} %get-tuple-element.31.rest_ref, bf16[16,384]{1,0:T(8,128)(2,1)S(1)} %collective-permute-done.5.rest_other_ref, ...), custom_call_target="tpu_custom_call", output_to_operand_aliasing={{0}: (3, {})} | custom-call | flops 1000000 | bytes 2000000 | tf_op jit(solution)/shard_map/end/spread_other/pallas_call | solution.py:368
  (3 shorter events, 0.0 us)
Async XLA Ops:
  4.2 23.9 %copy-start = (bf16[1024,256]{1,0:T(8,128)(2,1)S(1)}, bf16[1024,256]{1,0:T(8,128)(2,1)}, u32[]{:S(2)}) copy-start(bf16[1024,256]{1,0:T(8,128)(2,1)} %join_ref.1) | copy-start | bytes 1572868
  26.0 3.8 %copy-start.1 = (bf16[2,256]{1,0:T(2,128)(2,1)S(1)}, bf16[2,256]{1,0:T(2,128)(2,1)}, u32[]{:S(2)}) copy-start(bf16[2,256]{1,0:T(2,128)(2,1)} %grad_ref.3) | copy-start | bytes 3076
  26.0 3.8 %collective-permute-start = (bf16[2304,128]{1,0:T(8,128)(2,1)S(1)}, bf16[2304,128]{1,0:T(8,128)(2,1)S(1)}, u32[]{:S(2)}, u32[]{:S(2)}) collective-permute-start(bf16[2304,128]{1,0:T(8,128)(2,1)S(1)} %get-tuple-element.24), channel_id=1, source_target_pairs={{0,16},{16,0},{1,17},{17,1},{2,18},{18,2},{3,19},{19,3},{4,20},{20... | collective-permute-start | bytes 1769480 | tf_op jit(solution)/shard_map/backward/ppermute | solution.py:327
  47.2 5.7 %collective-permute-start.3 = (bf16[80,128]{1,0:T(8,128)(2,1)S(1)}, bf16[80,128]{1,0:T(8,128)(2,1)S(1)}, u32[]{:S(2)}, u32[]{:S(2)}) collective-permute-start(bf16[80,128]{1,0:T(8,128)(2,1)S(1)} %get-tuple-element.27.own_ref), channel_id=1, source_target_pairs={{0,12},{4,8},{8,4},{12,0},{1,13},{5,9},{9,5},{13,1},{2,14},{6,10},... | collective-permute-start | bytes 61448 | tf_op jit(solution)/shard_map/conv_middle/ppermute | solution.py:354
  47.3 6.6 %collective-permute-start.2 = (bf16[80,128]{1,0:T(8,128)(2,1)S(1)}, bf16[80,128]{1,0:T(8,128)(2,1)S(1)}, u32[]{:S(2)}, u32[]{:S(2)}) collective-permute-start(bf16[80,128]{1,0:T(8,128)(2,1)S(1)} %get-tuple-element.27.own_ref), channel_id=1, source_target_pairs={{0,8},{4,12},{8,0},{12,4},{1,9},{5,13},{9,1},{13,5},{2,10},{6,14},... | collective-permute-start | bytes 61448 | tf_op jit(solution)/shard_map/conv_middle/ppermute | solution.py:354
  51.1 3.8 %collective-permute-start.1 = (bf16[80,128]{1,0:T(8,128)(2,1)S(1)}, bf16[80,128]{1,0:T(8,128)(2,1)S(1)}, u32[]{:S(2)}, u32[]{:S(2)}) collective-permute-start(bf16[80,128]{1,0:T(8,128)(2,1)S(1)} %get-tuple-element.27.own_ref), channel_id=1, source_target_pairs={{0,4},{4,0},{8,12},{12,8},{1,5},{5,1},{9,13},{13,9},{2,6},{6,2},{1... | collective-permute-start | bytes 61448 | tf_op jit(solution)/shard_map/conv_middle/ppermute | solution.py:354
  69.1 5.8 %collective-permute-start.4 = (bf16[32,72,128]{2,1,0:T(8,128)(2,1)S(1)}, bf16[32,72,128]{2,1,0:T(8,128)(2,1)S(1)}, u32[]{:S(2)}, u32[]{:S(2)}) collective-permute-start(bf16[32,72,128]{2,1,0:T(8,128)(2,1)S(1)} %all_to_all.17.own_ref), channel_id=1, source_target_pairs={{0,16},{16,0},{1,17},{17,1},{2,18},{18,2},{3,19},{19,3},{4,20},{20... | collective-permute-start | bytes 1769480 | tf_op jit(solution)/shard_map/conv_gather/ppermute | solution.py:361
  73.3 1.6 %collective-permute-start.5 = (bf16[16,384]{1,0:T(8,128)(2,1)S(1)}, bf16[16,384]{1,0:T(8,128)(2,1)S(1)}, u32[]{:S(2)}, u32[]{:S(2)}) collective-permute-start(bf16[16,384]{1,0:T(8,128)(2,1)S(1)} %get-tuple-element.31.rest_ref), channel_id=1, source_target_pairs={{0,16},{16,0},{1,17},{17,1},{2,18},{18,2},{3,19},{19,3},{4,20},{20... | collective-permute-start | bytes 36872 | tf_op jit(solution)/shard_map/end/ppermute | solution.py:367

commit v10 on v9

--- a/solution.py
+++ b/solution.py
@@ -212,7 +212,9 @@
     rest_ref[...] = rows_ref[...].astype(BF)
 
 
-def finish_kernel(own_ref, one_ref, two_ref, three_ref, out_ref, latent_ref):
+def finish_kernel(own_ref, one_ref, two_ref, three_ref, rest_ref, rest_other_ref, out_ref, latent_ref, both_ref):
+    both_ref[0] = rest_ref[...]
+    both_ref[1] = rest_other_ref[...]
     own, one, two, three = (ref[...].astype(F32) for ref in (own_ref, one_ref, two_ref, three_ref))
     total = (own + two) + (one + three)
     latent_ref[...] = total[72:80]
@@ -245,12 +247,12 @@
     small.wait()
 
 
-def spread_other_kernel(other_ref, rest_ref, rest_other_ref, begun_hbm, conv_hbm, join_hbm, slabs, join_ref, sems):
+def spread_other_kernel(other_ref, both_ref, begun_hbm, conv_hbm, join_hbm, slabs, join_ref, sems):
     core = lax.axis_index("c")
     copy = spread_half(other_ref, 1 - core, conv_hbm, slabs, sems.at[0])
     total = jnp.zeros((64, 256), F32)
-    for ref in (rest_ref, rest_other_ref):
-        rows = ref[...]
+    for half in range(2):
+        rows = both_ref[half]
         joined = jnp.where(core == 0, rows[:, 0:64], rows[:, 64:128])
         total = total + lax.dot_general(joined, rows[:, 128:384], (((0,), (0,)), ((), ())), preferred_element_type=F32)
     join_ref[...] = total
@@ -354,9 +356,10 @@
         away = [lax.ppermute(middle, "zh", [(i, i ^ k) for i in range(4)]) for k in (1, 2, 3)]
 
     with jax.named_scope("conv_gather"):
-        summed, latent_sums = call(
-            finish_kernel, "finish", [shape(32, 72, 128, dtype=BF), shape(8, 128)], [VM] * 4
-        )(middle, *away)
+        rest_other = lax.ppermute(rest, "c", SWAP)
+        summed, latent_sums, both = call(
+            finish_kernel, "finish", [shape(32, 72, 128, dtype=BF), shape(8, 128), shape(2, 16, 384, dtype=BF)], [VM] * 6
+        )(middle, *away, rest, rest_other)
         own = lax.all_to_all(summed, BLOCK, 0, 0)
         other = lax.ppermute(own, "c", SWAP)
         begun, latent = spread(spread_own_kernel, "spread_own", (2, 256), [VM, VM], {})(
@@ -364,10 +367,9 @@
         )
 
     with jax.named_scope("end"):
-        rest_other = lax.ppermute(rest, "c", SWAP)
         conv_grad, join_grad = spread(
-            spread_other_kernel, "spread_other", (64, 256), [VM, VM, VM, HBM], {3: 0}
-        )(other, rest, rest_other, begun)
+            spread_other_kernel, "spread_other", (64, 256), [VM, VM, HBM], {2: 0}
+        )(other, both, begun)
     return (latent, conv_grad, join_grad)
 
 

time: 76.4 us -> 77.2 us (1.010)
  starting transfers between devices: 12.1 us -> 14.7 us
  waiting for transfers between devices: 3.27 us -> 2.17 us
  blocking collectives: 52.2 us -> 51.4 us
    ppermute x1, starting transfers between devices: 0.01 us -> 3.21 us  [on_device(): rest_other = lax.ppermute(rest, 'c', SWAP)]
    ppermute x3, waiting for transfers between devices: 1.93 us -> 0.01 us  [on_device(): lax.ppermute(middle, 'zh', [(i, i ^ k) for i in range(4)])]
  transfers between devices with their start and end apart: 6 -> 6, of which waited for: 4 -> 3; matrix products, arithmetic and copies ran while one was open for 0% -> 0% of each run, Pallas kernels for 3% -> 2%
where the time goes in v10:
time: 77.2 us; the launch traced here: 77 us
  blocking collectives  51.4 us (67%)
  starting transfers between devices  14.7 us (19%)
  Pallas kernels  7.95 us (10%)
  waiting for transfers between devices  2.17 us (3%)
    all_to_all x1, blocking collectives, on_device(): cam_shares = lax.all_to_all(shares, ('zh', 'y'), 0, 0)  20.9 us
    all_to_all x1, blocking collectives, on_device(): blocks = lax.all_to_all(packed, BLOCK, 0, 0)  17.1 us
    all_to_all x1, blocking collectives, on_device(): own = lax.all_to_all(summed, BLOCK, 0, 0)  13.5 us
    ppermute x3, starting transfers between devices, on_device(): lax.ppermute(middle, 'zh', [(i, i ^ k) for i in range(4)])  5.74 us
    pallas_call x1, Pallas kernels, on_device(): call(forward_kernel, 'forward', [shape(16, 16, 256, dtype=BF), shape(22,...  3.59 us
    ppermute x1, starting transfers between devices, on_device(): other = lax.ppermute(own, 'c', SWAP)  3.55 us
    ppermute x1, starting transfers between devices, on_device(): rest_other = lax.ppermute(rest, 'c', SWAP)  3.21 us
    ppermute x1, starting transfers between devices, on_device(): got = lax.ppermute(send, 'c', SWAP)  2.19 us
  transfers between devices with their start and end apart: 6, of which 3 were waited for; matrix products, arithmetic and copies ran while one was open for 0% of the time, Pallas kernels for 2%

profile of v10, /device:TPU:1, one launch (start us, length us, event | category | flops | bytes accessed | tf_op | source)
XLA Modules:
  0.0 77.0 jit_solution(3012856128886871586)
XLA Ops:
  0.6 3.6 %forward.1 = (bf16[16,16,256]{2,1,0:T(8,128)(2,1)S(1)}, f32[22,64,256]{2,1,0:T(8,128)S(1)}, bf16[2,768,768]{2,1,0:T(8,128)(2,1)S(1)}) custom-call(s32[2,176]{1,0:T(2,128)} %valid_hbm.1, bf16[2,256]{1,0:T(2,128)(2,1)} %grad_ref.3, bf16[1024,256]{1,0:T(8,128)(2,1)} %join_ref.1, bf16[22,64,256]{2,1,0:T(8,128)(2,1)} %bitcast.1, bf16[9,256,256]{2,1,0:T(8,128)(2,1)} %conv_hbm.1), custom_call_target="tpu_custom_call" | custom-call | flops 1200000000 | bytes 3000000 | tf_op jit(solution)/shard_map/forward/forward/pallas_call | solution.py:302
  4.2 0.0 copy-start
  4.2 20.9 %all_to_all.15.grad_ref.got_ref = bf16[16,16,256]{2,1,0:T(8,128)(2,1)S(1)} all-to-all(bf16[16,16,256]{2,1,0:T(8,128)(2,1)S(1)} %get-tuple-element.21), channel_id=1, replica_groups=mesh['zl'=2,'x'=4,'c'=2,'zh'=4,'y'=4] {'zh','y'}, dimensions={0} | all-to-all | bytes 262144 | tf_op jit(solution)/shard_map/forward/all_to_all | solution.py:318
  25.2 0.8 %backward_send.1 = (bf16[2,768,256]{2,1,0:T(8,128)(2,1)S(1)}, bf16[2304,128]{1,0:T(8,128)(2,1)S(1)}) custom-call(bf16[16,16,256]{2,1,0:T(8,128)(2,1)S(1)} %all_to_all.15.grad_ref.got_ref, f32[22,64,256]{2,1,0:T(8,128)S(1)} %get-tuple-element.22.slope_ref, bf16[2,768,768]{2,1,0:T(8,128)(2,1)S(1)} %get-tuple-element.20.turned_ref), custom_call_target="tpu_custom_call" | custom-call | flops 600000000 | bytes 3000000 | tf_op jit(solution)/shard_map/backward/backward_send/pallas_call | solution.py:321
  26.0 0.0 copy-start.1
  26.0 2.2 %collective-permute-start = (bf16[2304,128]{1,0:T(8,128)(2,1)S(1)}, bf16[2304,128]{1,0:T(8,128)(2,1)S(1)}, u32[]{:S(2)}, u32[]{:S(2)}) collective-permute-start(bf16[2304,128]{1,0:T(8,128)(2,1)S(1)} %get-tuple-element.25), channel_id=1, source_target_pairs={{0,16},{16,0},{1,17},{17,1},{2,18},{18,2},{3,19},{19,3},{4,20},{20... | collective-permute-start | bytes 1769480 | tf_op jit(solution)/shard_map/backward/ppermute | solution.py:329
  28.2 0.8 %backward_mine.1 = (f32[2304,128]{1,0:T(8,128)S(1)}, f32[8,256]{1,0:T(8,128)S(1)}, f32[2,256]{1,0:T(2,128)S(1)}) custom-call(bf16[2,768,768]{2,1,0:T(8,128)(2,1)S(1)} %get-tuple-element.20.turned_ref, bf16[2,768,256]{2,1,0:T(8,128)(2,1)S(1)} %get-tuple-element.23.pre_ref, bf16[16,16,256]{2,1,0:T(8,128)(2,1)S(1)} %all_to_all.15.grad_ref.got_ref, ...), custom_call_target="tpu_custom_call" | custom-call | flops 600000000 | bytes 3000000 | tf_op jit(solution)/shard_map/backward/backward_mine/pallas_call | solution.py:330
  29.0 0.8 %collective-permute-done.got_ref = bf16[2304,128]{1,0:T(8,128)(2,1)S(1)} collective-permute-done((bf16[2304,128]{1,0:T(8,128)(2,1)S(1)}, bf16[2304,128]{1,0:T(8,128)(2,1)S(1)}, u32[]{:S(2)}, u32[]{:S(2)}) %collective-permute-start) | collective-permute-done | bytes 589856 | tf_op jit(solution)/shard_map/backward/ppermute | solution.py:329
  29.8 0.2 pack.1
  30.0 17.1 %all_to_all.16.got_ref = bf16[32,80,128]{2,1,0:T(8,128)(2,1)S(1)} all-to-all(bf16[32,80,128]{2,1,0:T(8,128)(2,1)S(1)} %pack.1), channel_id=1, replica_groups=mesh['zl'=2,'x'=4,'c'=2,'zh'=4,'y'=4] {'zl','x','y'}, dimensions={0} | all-to-all | bytes 1310720 | tf_op jit(solution)/shard_map/conv_scatter/all_to_all | solution.py:346
  47.1 0.1 middle.1
  47.2 0.1 collective-permute-start.3
  47.3 3.7 %collective-permute-start.2 = (bf16[80,128]{1,0:T(8,128)(2,1)S(1)}, bf16[80,128]{1,0:T(8,128)(2,1)S(1)}, u32[]{:S(2)}, u32[]{:S(2)}) collective-permute-start(bf16[80,128]{1,0:T(8,128)(2,1)S(1)} %get-tuple-element.28.own_ref), channel_id=1, source_target_pairs={{0,8},{4,12},{8,0},{12,4},{1,9},{5,13},{9,1},{13,5},{2,10},{6,14},... | collective-permute-start | bytes 61448 | tf_op jit(solution)/shard_map/conv_middle/ppermute | solution.py:356
  51.1 1.9 %collective-permute-start.1 = (bf16[80,128]{1,0:T(8,128)(2,1)S(1)}, bf16[80,128]{1,0:T(8,128)(2,1)S(1)}, u32[]{:S(2)}, u32[]{:S(2)}) collective-permute-start(bf16[80,128]{1,0:T(8,128)(2,1)S(1)} %get-tuple-element.28.own_ref), channel_id=1, source_target_pairs={{0,4},{4,0},{8,12},{12,8},{1,5},{5,1},{9,13},{13,9},{2,6},{6,2},{1... | collective-permute-start | bytes 61448 | tf_op jit(solution)/shard_map/conv_middle/ppermute | solution.py:356
  53.0 3.2 %collective-permute-start.4 = (bf16[16,384]{1,0:T(8,128)(2,1)S(1)}, bf16[16,384]{1,0:T(8,128)(2,1)S(1)}, u32[]{:S(2)}, u32[]{:S(2)}) collective-permute-start(bf16[16,384]{1,0:T(8,128)(2,1)S(1)} %get-tuple-element.29.rest_ref), channel_id=1, source_target_pairs={{0,16},{16,0},{1,17},{17,1},{2,18},{18,2},{3,19},{19,3},{4,20},{20... | collective-permute-start | bytes 36872 | tf_op jit(solution)/shard_map/conv_gather/ppermute | solution.py:359
  56.2 0.8 %collective-permute-done.4.rest_other_ref = bf16[16,384]{1,0:T(8,128)(2,1)S(1)} collective-permute-done((bf16[16,384]{1,0:T(8,128)(2,1)S(1)}, bf16[16,384]{1,0:T(8,128)(2,1)S(1)}, u32[]{:S(2)}, u32[]{:S(2)}) %collective-permute-start.4) | collective-permute-done | bytes 12320 | tf_op jit(solution)/shard_map/conv_gather/ppermute | solution.py:359
  57.0 0.0 collective-permute-done.3.three_ref
  57.0 0.0 collective-permute-done.2.two_ref
  57.0 0.1 finish.1
  57.1 13.5 %all_to_all.17.own_ref = bf16[32,72,128]{2,1,0:T(8,128)(2,1)S(1)} all-to-all(bf16[32,72,128]{2,1,0:T(8,128)(2,1)S(1)} %get-tuple-element.30), channel_id=1, replica_groups=mesh['zl'=2,'x'=4,'c'=2,'zh'=4,'y'=4] {'zl','x','y'}, dimensions={0} | all-to-all | bytes 1179648 | tf_op jit(solution)/shard_map/conv_gather/all_to_all | solution.py:363
  70.5 3.6 %collective-permute-start.5 = (bf16[32,72,128]{2,1,0:T(8,128)(2,1)S(1)}, bf16[32,72,128]{2,1,0:T(8,128)(2,1)S(1)}, u32[]{:S(2)}, u32[]{:S(2)}) collective-permute-start(bf16[32,72,128]{2,1,0:T(8,128)(2,1)S(1)} %all_to_all.17.own_ref), channel_id=1, source_target_pairs={{0,16},{16,0},{1,17},{17,1},{2,18},{18,2},{3,19},{19,3},{4,20},{20... | collective-permute-start | bytes 1769480 | tf_op jit(solution)/shard_map/conv_gather/ppermute | solution.py:364
  74.1 1.1 %spread_own.1 = (f32[9,256,256]{2,1,0:T(8,128)}, f32[2,256]{1,0:T(2,128)}) custom-call(bf16[32,72,128]{2,1,0:T(8,128)(2,1)S(1)} %all_to_all.17.own_ref, f32[8,128]{1,0:T(8,128)S(1)} %get-tuple-element.31.sums_ref), custom_call_target="tpu_custom_call" | custom-call | flops 1000000 | bytes 2000000 | tf_op jit(solution)/shard_map/conv_gather/spread_own/pallas_call | solution.py:365
  75.2 0.5 collective-permute-done.5.other_ref
  75.7 1.2 %spread_other.1 = (f32[9,256,256]{2,1,0:T(8,128)}, f32[64,256]{1,0:T(8,128)}) custom-call(bf16[32,72,128]{2,1,0:T(8,128)(2,1)S(1)} %collective-permute-done.5.other_ref, bf16[2,16,384]{2,1,0:T(8,128)(2,1)S(1)} %get-tuple-element.33.both_ref, f32[9,256,256]{2,1,0:T(8,128)} %get-tuple-element.34.begun_hbm), custom_call_target="tpu_custom_call", output_to_operand_aliasing={{0}: (2, {})} | custom-call | flops 1000000 | bytes 2000000 | tf_op jit(solution)/shard_map/end/spread_other/pallas_call | solution.py:370
  (3 shorter events, 0.0 us)
Async XLA Ops:
  4.2 23.9 %copy-start = (bf16[1024,256]{1,0:T(8,128)(2,1)S(1)}, bf16[1024,256]{1,0:T(8,128)(2,1)}, u32[]{:S(2)}) copy-start(bf16[1024,256]{1,0:T(8,128)(2,1)} %join_ref.1) | copy-start | bytes 1572868
  26.0 3.8 %copy-start.1 = (bf16[2,256]{1,0:T(2,128)(2,1)S(1)}, bf16[2,256]{1,0:T(2,128)(2,1)}, u32[]{:S(2)}) copy-start(bf16[2,256]{1,0:T(2,128)(2,1)} %grad_ref.3) | copy-start | bytes 3076
  26.0 3.8 %collective-permute-start = (bf16[2304,128]{1,0:T(8,128)(2,1)S(1)}, bf16[2304,128]{1,0:T(8,128)(2,1)S(1)}, u32[]{:S(2)}, u32[]{:S(2)}) collective-permute-start(bf16[2304,128]{1,0:T(8,128)(2,1)S(1)} %get-tuple-element.25), channel_id=1, source_target_pairs={{0,16},{16,0},{1,17},{17,1},{2,18},{18,2},{3,19},{19,3},{4,20},{20... | collective-permute-start | bytes 1769480 | tf_op jit(solution)/shard_map/backward/ppermute | solution.py:329
  47.2 9.8 %collective-permute-start.3 = (bf16[80,128]{1,0:T(8,128)(2,1)S(1)}, bf16[80,128]{1,0:T(8,128)(2,1)S(1)}, u32[]{:S(2)}, u32[]{:S(2)}) collective-permute-start(bf16[80,128]{1,0:T(8,128)(2,1)S(1)} %get-tuple-element.28.own_ref), channel_id=1, source_target_pairs={{0,12},{4,8},{8,4},{12,0},{1,13},{5,9},{9,5},{13,1},{2,14},{6,10},... | collective-permute-start | bytes 61448 | tf_op jit(solution)/shard_map/conv_middle/ppermute | solution.py:356
  47.3 9.7 %collective-permute-start.2 = (bf16[80,128]{1,0:T(8,128)(2,1)S(1)}, bf16[80,128]{1,0:T(8,128)(2,1)S(1)}, u32[]{:S(2)}, u32[]{:S(2)}) collective-permute-start(bf16[80,128]{1,0:T(8,128)(2,1)S(1)} %get-tuple-element.28.own_ref), channel_id=1, source_target_pairs={{0,8},{4,12},{8,0},{12,4},{1,9},{5,13},{9,1},{13,5},{2,10},{6,14},... | collective-permute-start | bytes 61448 | tf_op jit(solution)/shard_map/conv_middle/ppermute | solution.py:356
  51.1 6.0 %collective-permute-start.1 = (bf16[80,128]{1,0:T(8,128)(2,1)S(1)}, bf16[80,128]{1,0:T(8,128)(2,1)S(1)}, u32[]{:S(2)}, u32[]{:S(2)}) collective-permute-start(bf16[80,128]{1,0:T(8,128)(2,1)S(1)} %get-tuple-element.28.own_ref), channel_id=1, source_target_pairs={{0,4},{4,0},{8,12},{12,8},{1,5},{5,1},{9,13},{13,9},{2,6},{6,2},{1... | collective-permute-start | bytes 61448 | tf_op jit(solution)/shard_map/conv_middle/ppermute | solution.py:356
  53.0 4.0 %collective-permute-start.4 = (bf16[16,384]{1,0:T(8,128)(2,1)S(1)}, bf16[16,384]{1,0:T(8,128)(2,1)S(1)}, u32[]{:S(2)}, u32[]{:S(2)}) collective-permute-start(bf16[16,384]{1,0:T(8,128)(2,1)S(1)} %get-tuple-element.29.rest_ref), channel_id=1, source_target_pairs={{0,16},{16,0},{1,17},{17,1},{2,18},{18,2},{3,19},{19,3},{4,20},{20... | collective-permute-start | bytes 36872 | tf_op jit(solution)/shard_map/conv_gather/ppermute | solution.py:359
  70.5 5.2 %collective-permute-start.5 = (bf16[32,72,128]{2,1,0:T(8,128)(2,1)S(1)}, bf16[32,72,128]{2,1,0:T(8,128)(2,1)S(1)}, u32[]{:S(2)}, u32[]{:S(2)}) collective-permute-start(bf16[32,72,128]{2,1,0:T(8,128)(2,1)S(1)} %all_to_all.17.own_ref), channel_id=1, source_target_pairs={{0,16},{16,0},{1,17},{17,1},{2,18},{18,2},{3,19},{19,3},{4,20},{20... | collective-permute-start | bytes 1769480 | tf_op jit(solution)/shard_map/conv_gather/ppermute | solution.py:364
